TPU v7x, 1024 devices: a whole 4x8x16 slice. The times are simulated.
1024 devices in a mesh: section: 16 (over z), row: 16 (over y, core), col: 4 (over x).
Axes of the slice: x: 4, y: 8, z: 16, core: 2. Of those that a mesh axis runs over, the one named last changes fastest.
Arguments:
- tokens: bfloat16 [16, 512, 3072], P('section', None, 'col'), may hold values from -6 to 6
- up_weight: bfloat16 [16, 3072, 12288], P('section', 'col', 'row'), may hold values from -0.109375 to 0.109375
- down_weight: bfloat16 [16, 12288, 3072], P('section', 'row', 'col'), may hold values from -0.0546875 to 0.0546875
- out_grad: bfloat16 [16, 512, 3072], P('section', None, 'col'), may hold values from -6 to 6
- saved_hidden: bfloat16 [16, 512, 12288], P('section', 'col', 'row'), may hold values from -6 to 6
Outputs:
- next_tokens: bfloat16 [16, 512, 3072], P('section', None, 'col')
- prev_grads: bfloat16 [16, 512, 3072], P('section', None, 'col')
All inputs are finite; a program needn't handle non-finite values.
Results may differ from a plain program's by a relative error of at most 0.019.
Values may be sent and summed in bfloat16 or wider, within the bound.
No kernel may reach another device: no remote copies, remote signals or barrier semaphores. Data moves between devices by JAX's collectives and lax.ppermute only.
A program may use at most 32 MiB of HBM per device.

v0:
```python
import jax
import jax.numpy as jnp
from jax import lax
from jax.sharding import PartitionSpec as P

inv_root_two = 0.7071067811865476
inv_root_tau = 0.3989422804014327


def passed_along(block, axis, distance):
    devices = range(lax.axis_size(axis))
    route = [((i - distance) % len(devices), i) for i in devices]
    return lax.ppermute(block, axis, route)


def gelu_value(hidden):
    return 0.5 * hidden * (1.0 + lax.erf(hidden * inv_root_two))


def gelu_slope(hidden):
    return (
        0.5 * (1.0 + lax.erf(hidden * inv_root_two))
        + hidden * jnp.exp(-0.5 * hidden * hidden) * inv_root_tau
    )


def hidden_share(operand, weight, contract):
    return lax.psum_scatter(
        lax.dot_general(
            operand, weight, (((1,), (contract,)), ((), ())), preferred_element_type=jnp.float32
        ).astype(jnp.bfloat16),
        "col",
        scatter_dimension=0,
        tiled=True,
    ).astype(jnp.float32)


def feature_terms(hidden_part, weight, contract):
    return lax.dot_general(
        lax.all_gather(hidden_part, "col", axis=0, tiled=True),
        weight,
        (((1,), (contract,)), ((), ())),
        preferred_element_type=jnp.float32,
    )


def finish(partial_value, residual, shift_by):
    summed = lax.psum(partial_value.astype(jnp.bfloat16), "row").astype(jnp.float32)
    result = (residual.astype(jnp.float32) + summed).astype(jnp.bfloat16)
    return passed_along(result, "section", shift_by)


def body(tokens, up_weight, down_weight, out_grad, saved_hidden):
    inputs = tokens[0]
    w_up = up_weight[0]
    w_down = down_weight[0]
    upstream = out_grad[0]
    stored = saved_hidden[0].astype(jnp.float32)
    hidden = hidden_share(inputs, w_up, 0)
    active = gelu_value(hidden).astype(jnp.bfloat16)
    forward_terms = feature_terms(active, w_down, 0)
    next_tokens = finish(forward_terms, inputs, 1)
    slope_in = hidden_share(upstream, w_down, 1)
    hidden_grad = (slope_in * gelu_slope(stored)).astype(jnp.bfloat16)
    backward_terms = feature_terms(hidden_grad, w_up, 1)
    prev_grads = finish(backward_terms, upstream, -1)
    return (next_tokens[None], prev_grads[None])


def solution(mesh):
    return jax.shard_map(
        body,
        mesh=mesh,
        in_specs=(
            P("section", None, "col"),
            P("section", "col", "row"),
            P("section", "row", "col"),
            P("section", None, "col"),
            P("section", "col", "row"),
        ),
        out_specs=(P("section", None, "col"), P("section", None, "col")),
        check_vma=False,
    )
```

profile of v0, /device:TPU:1, one launch (start us, length us, event | category | flops | bytes accessed | tf_op | source)
XLA Modules:
  0.0 275.0 jit_solution(6883387074222219745)
XLA Ops:
  7.2 0.0 reduce-scatter.3.cloned.1.call-start
  7.2 3.3 %convolution_convert_fusion.3 = bf16[512,768]{1,0:T(8,128)(2,1)} fusion(bf16[1,768,768]{2,1,0:T(8,128)(2,1)} %param.6, bf16[1,512,768]{2,1,0:T(8,128)(2,1)} %param.5), kind=kOutput, calls=%fused_computation.5 | convolution fusion | flops 604372992 | bytes 2752512 | tf_op jit(solution)/shard_map/dot_general | solution.py:29
  10.5 0.0 reduce-scatter.3.cloned.1.call-update
  10.6 0.0 reduce-scatter.5.cloned.1.call-start
  10.6 1.7 convolution_convert_fusion.1
  12.3 0.0 reduce-scatter.5.cloned.1.call-update
  12.3 0.0 all-reduce.3.cloned.1.call-start
  12.4 40.3 %reduce-scatter.3.cloned.1.call-done = bf16[128,768]{1,0:T(8,128)(2,1)} async-done(((bf16[512,768]{1,0:T(8,128)(2,1)}), bf16[128,768]{1,0:T(8,128)(2,1)}) %reduce-scatter.3.cloned.1.call-update) | async-done | bytes 196624 | tf_op jit(solution)/shard_map/reduce_scatter | solution.py:28
  52.7 1.0 fusion.7
  53.7 11.8 %all_gather.6 = bf16[512,768]{1,0:T(8,128)(2,1)S(1)} all-gather(bf16[128,768]{1,0:T(8,128)(2,1)S(1)} %fusion.7), channel_id=1, replica_groups=mesh['section'=16,'row'=16,'col'=4] {'col'}, dimensions={0}, use_global_device_ids=true | all-gather | bytes 983040 | tf_op jit(solution)/shard_map/all_gather | solution.py:40
  65.5 1.7 convolution_convert_fusion.2
  67.1 22.7 %reduce-scatter.5.cloned.1.call-done = bf16[128,768]{1,0:T(8,128)(2,1)} async-done(((bf16[512,768]{1,0:T(8,128)(2,1)}), bf16[128,768]{1,0:T(8,128)(2,1)}) %reduce-scatter.5.cloned.1.call-update) | async-done | bytes 196624 | tf_op jit(solution)/shard_map/reduce_scatter | solution.py:28
  89.8 1.1 fusion.17
  90.9 11.8 %all_gather.7 = bf16[512,768]{1,0:T(8,128)(2,1)S(1)} all-gather(bf16[128,768]{1,0:T(8,128)(2,1)S(1)} %fusion.17), channel_id=1, replica_groups=mesh['section'=16,'row'=16,'col'=4] {'col'}, dimensions={0}, use_global_device_ids=true | all-gather | bytes 983040 | tf_op jit(solution)/shard_map/all_gather | solution.py:40
  102.7 1.7 convolution_convert_fusion
  104.4 132.8 %all-reduce.3.cloned.1.call-done = (bf16[512,768]{1,0:T(8,128)(2,1)}, bf16[512,768]{1,0:T(8,128)(2,1)}) async-done(((bf16[512,768]{1,0:T(8,128)(2,1)}, bf16[512,768]{1,0:T(8,128)(2,1)}), (bf16[512,768]{1,0:T(8,128)(2,1)}, bf16[512,768]{1,0:T(8,128)(2,1)})) %all-reduce.3.cloned.1.call-update) | async-done | bytes 1572880 | tf_op jit(solution)/shard_map/psum | solution.py:48
  237.2 1.4 add_convert_fusion
  238.6 6.9 %collective-permute-start.1 = (bf16[512,768]{1,0:T(8,128)(2,1)S(1)}, bf16[512,768]{1,0:T(8,128)(2,1)S(1)}, u32[]{:S(2)}, u32[]{:S(2)}) collective-permute-start(bf16[512,768]{1,0:T(8,128)(2,1)S(1)} %add_convert_fusion), channel_id=1, source_target_pairs={{64,0},{128,64},{192,128},{256,192},{320,256},{384,320},{448,384},... | collective-permute-start | bytes 2359304 | tf_op jit(solution)/shard_map/ppermute | solution.py:13
  245.6 0.2 add_convert_fusion.1
  245.8 1.9 collective-permute-start
  247.7 13.7 %collective-permute-done.1 = bf16[512,768]{1,0:T(8,128)(2,1)S(1)} collective-permute-done((bf16[512,768]{1,0:T(8,128)(2,1)S(1)}, bf16[512,768]{1,0:T(8,128)(2,1)S(1)}, u32[]{:S(2)}, u32[]{:S(2)}) %collective-permute-start.1) | collective-permute-done | bytes 786464 | tf_op jit(solution)/shard_map/ppermute | solution.py:13
  261.4 5.2 %collective-permute-done = bf16[512,768]{1,0:T(8,128)(2,1)S(1)} collective-permute-done((bf16[512,768]{1,0:T(8,128)(2,1)S(1)}, bf16[512,768]{1,0:T(8,128)(2,1)S(1)}, u32[]{:S(2)}, u32[]{:S(2)}) %collective-permute-start) | collective-permute-done | bytes 786464 | tf_op jit(solution)/shard_map/ppermute | solution.py:13
  266.7 0.9 copy.11
  267.6 0.9 copy.12
  (13 shorter events, 0.0 us)
Async XLA Ops:
  7.2 3.4 %copy-start = (bf16[1,768,768]{2,1,0:T(8,128)(2,1)S(1)}, bf16[1,768,768]{2,1,0:T(8,128)(2,1)}, u32[]{:S(2)}) copy-start(bf16[1,768,768]{2,1,0:T(8,128)(2,1)} %param.7) | copy-start | bytes 3538948
  7.2 3.4 %copy-start.1 = (bf16[1,512,768]{2,1,0:T(8,128)(2,1)S(1)}, bf16[1,512,768]{2,1,0:T(8,128)(2,1)}, u32[]{:S(2)}) copy-start(bf16[1,512,768]{2,1,0:T(8,128)(2,1)} %param.8) | copy-start | bytes 2359300
  7.2 45.5 %reduce-scatter.3.cloned.1.call-start = ((), (), s32[]{:S(2)}) async-start(), calls=%async_computation.2 | async-start | bytes 983040 | tf_op jit(solution)/shard_map/reduce_scatter | solution.py:28
  10.6 79.2 %reduce-scatter.5.cloned.1.call-start = ((), (), s32[]{:S(2)}) async-start(), calls=%async_computation.3 | async-start | bytes 983040 | tf_op jit(solution)/shard_map/reduce_scatter | solution.py:28
  12.3 224.8 %all-reduce.3.cloned.1.call-start = ((), (), s32[]{:S(2)}) async-start(), calls=%async_computation.4 | async-start | bytes 3145728 | tf_op jit(solution)/shard_map/psum | solution.py:48
  65.5 24.3 %copy-start.4 = (bf16[1,128,768]{2,1,0:T(8,128)(2,1)S(1)}, bf16[1,128,768]{2,1,0:T(8,128)(2,1)}, u32[]{:S(2)}) copy-start(bf16[1,128,768]{2,1,0:T(8,128)(2,1)} %param.9) | copy-start | bytes 589828
  67.1 35.5 %copy-start.5 = (bf16[1,768,768]{2,1,0:T(8,128)(2,1)S(1)}, bf16[1,768,768]{2,1,0:T(8,128)(2,1)}, u32[]{:S(2)}) copy-start(bf16[1,768,768]{2,1,0:T(8,128)(2,1)} %param.6) | copy-start | bytes 3538948
  237.2 8.4 %copy-start.2 = (bf16[1,512,768]{2,1,0:T(8,128)(2,1)S(1)}, bf16[1,512,768]{2,1,0:T(8,128)(2,1)}, u32[]{:S(2)}) copy-start(bf16[1,512,768]{2,1,0:T(8,128)(2,1)} %param.5) | copy-start | bytes 2359300
  237.2 8.4 %copy-start.3 = (bf16[512,768]{1,0:T(8,128)(2,1)S(1)}, bf16[512,768]{1,0:T(8,128)(2,1)}, u32[]{:S(2)}) copy-start(bf16[512,768]{1,0:T(8,128)(2,1)} %get-tuple-element.2) | copy-start | bytes 2359300
  238.6 22.8 %collective-permute-start.1 = (bf16[512,768]{1,0:T(8,128)(2,1)S(1)}, bf16[512,768]{1,0:T(8,128)(2,1)S(1)}, u32[]{:S(2)}, u32[]{:S(2)}) collective-permute-start(bf16[512,768]{1,0:T(8,128)(2,1)S(1)} %add_convert_fusion), channel_id=1, source_target_pairs={{64,0},{128,64},{192,128},{256,192},{320,256},{384,320},{448,384},... | collective-permute-start | bytes 2359304 | tf_op jit(solution)/shard_map/ppermute | solution.py:13
  245.8 20.9 %collective-permute-start = (bf16[512,768]{1,0:T(8,128)(2,1)S(1)}, bf16[512,768]{1,0:T(8,128)(2,1)S(1)}, u32[]{:S(2)}, u32[]{:S(2)}) collective-permute-start(bf16[512,768]{1,0:T(8,128)(2,1)S(1)} %add_convert_fusion.1), channel_id=1, source_target_pairs={{960,0},{0,64},{64,128},{128,192},{192,256},{256,320},{320,384},{3... | collective-permute-start | bytes 2359304 | tf_op jit(solution)/shard_map/ppermute | solution.py:13
Sparse Core Ops, SparseCore 0:
  12.0 40.6 reduce-scatter.2
  56.7 33.0 reduce-scatter.4
  104.5 132.6 all-reduce.2
where the time goes:
time: 276 us; the launch traced here: 275 us
  waiting for transfers between devices  215 us (78%)
  blocking collectives  23.5 us (9%)
  between operations  13.8 us (5%)
  starting transfers between devices  8.99 us (3%)
  matrix products  8.35 us (3%)
  other arithmetic  3.75 us (1%)
    psum x1, waiting for transfers between devices, finish(): lax.psum(partial_value.astype(jnp.bfloat16), 'row').astype(jnp.float32)  133 us
    reduce_scatter x2, waiting for transfers between devices, hidden_share(): lax.psum_scatter(lax.dot_general(operand, weight, (((1,), (contract,)), (...  62.9 us
    all_gather x2, blocking collectives, feature_terms(): lax.all_gather(hidden_part, 'col', axis=0, tiled=True)  23.5 us
    ppermute x2, waiting for transfers between devices, passed_along(): return lax.ppermute(block, axis, route)  19 us
    ppermute x2, starting transfers between devices, passed_along(): return lax.ppermute(block, axis, route)  8.87 us
  transfers between devices with their start and end apart: 5, of which 5 were waited for; matrix products, arithmetic and copies ran while one was open for 2% of the time, Pallas kernels for 0%

commit v1 on v0

v1 whole, which is shorter than its diff:
```python
import jax
import jax.numpy as jnp
from jax import lax
from jax.sharding import Mesh, PartitionSpec as P

inv_root_two = 0.7071067811865476
inv_root_tau = 0.3989422804014327


def passed_along(block, axis, distance):
    devices = range(lax.axis_size(axis))
    route = [((i - distance) % len(devices), i) for i in devices]
    return lax.ppermute(block, axis, route)


def gelu_value(hidden):
    return 0.5 * hidden * (1.0 + lax.erf(hidden * inv_root_two))


def gelu_slope(hidden):
    return (
        0.5 * (1.0 + lax.erf(hidden * inv_root_two))
        + hidden * jnp.exp(-0.5 * hidden * hidden) * inv_root_tau
    )


def product(operand, weight, contract):
    return lax.dot_general(
        operand, weight, (((1,), (contract,)), ((), ())), preferred_element_type=jnp.float32
    )


def hidden_share(operand, weight, contract):
    n = lax.axis_size("col")
    partial = product(operand, weight, contract).astype(jnp.bfloat16)
    parts = lax.all_to_all(partial.reshape(n, -1, partial.shape[1]), "col", 0, 0, tiled=True)
    return parts.astype(jnp.float32).sum(0)


def feature_sum(hidden_part, weight, contract, residual, shift_by):
    rows, ny = lax.axis_size("y") * lax.axis_size("core"), lax.axis_size("y")
    gathered = lax.all_gather(hidden_part, "col", axis=0, tiled=True)
    tokens, width = gathered.shape
    piece = tokens // rows
    by_core = gathered.reshape(ny, 2, piece, width)
    core = lax.axis_index("core")
    theirs = lax.dynamic_slice_in_dim(by_core, 1 - core, 1, 1).reshape(tokens // 2, width)
    ours = lax.dynamic_slice_in_dim(by_core, core, 1, 1).reshape(tokens // 2, width)
    sent = product(theirs, weight, contract).astype(jnp.bfloat16)
    arrived = passed_along(sent, "core", 1)
    chip_sum = (product(ours, weight, contract) + arrived.astype(jnp.float32)).astype(jnp.bfloat16)
    parts = lax.all_to_all(chip_sum.reshape(ny, piece, -1), "y", 0, 0, tiled=True)
    summed = parts.astype(jnp.float32).sum(0)
    mine = lax.axis_index("y") * 2 + core
    own_residual = lax.dynamic_slice_in_dim(residual, mine * piece, piece, 0)
    result = (own_residual.astype(jnp.float32) + summed).astype(jnp.bfloat16)
    moved = passed_along(result, "section", shift_by)
    return lax.all_gather(moved, ("y", "core"), axis=0, tiled=True)


def body(tokens, up_weight, down_weight, out_grad, saved_hidden):
    inputs = tokens[0]
    w_up = up_weight[0]
    w_down = down_weight[0]
    upstream = out_grad[0]
    stored = saved_hidden[0].astype(jnp.float32)
    hidden = hidden_share(inputs, w_up, 0)
    active = gelu_value(hidden).astype(jnp.bfloat16)
    next_tokens = feature_sum(active, w_down, 0, inputs, 1)
    slope_in = hidden_share(upstream, w_down, 1)
    hidden_grad = (slope_in * gelu_slope(stored)).astype(jnp.bfloat16)
    prev_grads = feature_sum(hidden_grad, w_up, 1, upstream, -1)
    return (next_tokens[None], prev_grads[None])


def solution(mesh):
    sections, rows, cols = mesh.devices.shape
    fine = Mesh(mesh.devices.reshape(sections, rows // 2, 2, cols), ("section", "y", "core", "col"))
    features = P("section", None, "col")
    return jax.shard_map(
        body,
        mesh=fine,
        in_specs=(
            features,
            P("section", "col", ("y", "core")),
            P("section", ("y", "core"), "col"),
            features,
            P("section", "col", ("y", "core")),
        ),
        out_specs=(features, features),
        check_vma=False,
    )
```

time: 276 us -> 157 us (0.57)
  waiting for transfers between devices: 215 us -> 21.3 us
  blocking collectives: 23.5 us -> 68.4 us
  starting transfers between devices: 8.99 us -> 49.5 us
  between operations: 13.8 us -> 0.8 us
    psum x1 -> x0, waiting for transfers between devices: 133 us -> none  [finish(): lax.psum(partial_value.astype(jnp.bfloat16), 'row').astype(jnp.float32)]
    reduce_scatter x2 -> x0, waiting for transfers between devices: 62.9 us -> none  [hidden_share(): lax.psum_scatter(lax.dot_general(operand, weight, (((1,), (contract,)), (...]
    all_gather x2 -> x4, blocking collectives: 23.5 us -> 68.4 us  [the longest x2 34.9 us: feature_sum(): return lax.all_gather(moved, ('y', 'core'), axis=0, tiled=True)]
    ppermute x2 -> x4, starting transfers between devices: 8.87 us -> 33.5 us  [passed_along(): return lax.ppermute(block, axis, route)]
    all_to_all x0 -> x4, waiting for transfers between devices: none -> 18.6 us  [the longest x2 13.1 us: feature_sum(): lax.all_to_all(chip_sum.reshape(ny, piece, -1), 'y', 0, 0, tiled=True)]
    ppermute x2 -> x4, waiting for transfers between devices: 19 us -> 2.66 us  [passed_along(): return lax.ppermute(block, axis, route)]
    all_to_all x0 -> x4, starting transfers between devices: none -> 16.1 us  [the longest x2 9.16 us: hidden_share(): lax.all_to_all(partial.reshape(n, -1, partial.shape[1]), 'col', 0, 0, til...]
    dot_general x4 -> x6, matrix products: 8.35 us -> 9.08 us  [product(): lax.dot_general(operand, weight, (((1,), (contract,)), ((), ())), preferr...]
  transfers between devices with their start and end apart: 5 -> 8, of which waited for: 5 -> 5; matrix products, arithmetic and copies ran while one was open for 2% -> 4% of each run, Pallas kernels for 0% -> 0%
where the time goes in v1:
time: 157 us; the launch traced here: 156 us
  blocking collectives  68.4 us (44%)
  starting transfers between devices  49.5 us (32%)
  waiting for transfers between devices  21.3 us (14%)
  matrix products  9.08 us (6%)
  local copies, waits for them, and re-layouts  3.91 us (2%)
  other arithmetic  3.39 us (2%)
    all_gather x2, blocking collectives, feature_sum(): return lax.all_gather(moved, ('y', 'core'), axis=0, tiled=True)  34.9 us
    all_gather x2, blocking collectives, feature_sum(): gathered = lax.all_gather(hidden_part, 'col', axis=0, tiled=True)  33.5 us
    ppermute x4, starting transfers between devices, passed_along(): return lax.ppermute(block, axis, route)  33.5 us
    all_to_all x2, waiting for transfers between devices, feature_sum(): lax.all_to_all(chip_sum.reshape(ny, piece, -1), 'y', 0, 0, tiled=True)  13.1 us
    all_to_all x2, starting transfers between devices, hidden_share(): lax.all_to_all(partial.reshape(n, -1, partial.shape[1]), 'col', 0, 0, til...  9.16 us
    dot_general x6, matrix products, product(): lax.dot_general(operand, weight, (((1,), (contract,)), ((), ())), preferr...  9.08 us
    all_to_all x2, starting transfers between devices, feature_sum(): lax.all_to_all(chip_sum.reshape(ny, piece, -1), 'y', 0, 0, tiled=True)  6.91 us
    all_to_all x2, waiting for transfers between devices, hidden_share(): lax.all_to_all(partial.reshape(n, -1, partial.shape[1]), 'col', 0, 0, til...  5.52 us
  transfers between devices with their start and end apart: 8, of which 5 were waited for; matrix products, arithmetic and copies ran while one was open for 4% of the time, Pallas kernels for 0%

profile of v1, /device:TPU:1, one launch (start us, length us, event | category | flops | bytes accessed | tf_op | source)
XLA Modules:
  0.0 156.4 jit_solution(10858193827425696521)
XLA Ops:
  0.6 1.3 copy-done
  1.9 2.8 %convolution_convert_fusion.1 = bf16[512,768]{1,0:T(8,128)(2,1)} fusion(bf16[1,768,768]{2,1,0:T(8,128)(2,1)S(1)} %copy-done, bf16[1,512,768]{2,1,0:T(8,128)(2,1)} %param.5), kind=kOutput, calls=%fused_computation.3 | convolution fusion | flops 604372992 | bytes 2752512 | tf_op jit(solution)/shard_map/dot_general | solution.py:28
  4.7 5.0 %all-to-all-start = ((bf16[4,128,768]{2,1,0:T(8,128)(2,1)}), bf16[4,128,768]{2,1,0:T(8,128)(2,1)S(1)}, u32[]{:S(2)}, u32[]{:S(2)}) async-start(bf16[4,128,768]{2,1,0:T(8,128)(2,1)} %bitcast.57), calls=%async_computation | async-start | bytes 1572864 | tf_op jit(solution)/shard_map/all_to_all | solution.py:36
  9.7 2.8 %convolution_convert_fusion = bf16[512,768]{1,0:T(8,128)(2,1)} fusion(bf16[1,768,768]{2,1,0:T(8,128)(2,1)S(1)} %copy-done.1, bf16[1,512,768]{2,1,0:T(8,128)(2,1)} %param.8), kind=kOutput, calls=%fused_computation.2 | convolution fusion | flops 604372992 | bytes 2752512 | tf_op jit(solution)/shard_map/dot_general | solution.py:28
  12.5 5.5 %all-to-all-done = bf16[4,128,768]{2,1,0:T(8,128)(2,1)S(1)} async-done(((bf16[4,128,768]{2,1,0:T(8,128)(2,1)}), bf16[4,128,768]{2,1,0:T(8,128)(2,1)S(1)}, u32[]{:S(2)}, u32[]{:S(2)}) %all-to-all-start) | async-done | bytes 786464 | tf_op jit(solution)/shard_map/all_to_all | solution.py:36
  18.0 4.2 %all-to-all-start.2 = ((bf16[4,128,768]{2,1,0:T(8,128)(2,1)}), bf16[4,128,768]{2,1,0:T(8,128)(2,1)}, u32[]{:S(2)}, u32[]{:S(2)}) async-start(bf16[4,128,768]{2,1,0:T(8,128)(2,1)} %bitcast.58), calls=%async_computation.2 | async-start | bytes 1572864 | tf_op jit(solution)/shard_map/all_to_all | solution.py:36
  22.4 18.4 %all_gather.12 = bf16[512,768]{1,0:T(8,128)(2,1)S(1)} all-gather(bf16[128,768]{1,0:T(8,128)(2,1)S(1)} %multiply_convert_fusion), channel_id=1, replica_groups=mesh['section'=16,'y'=8,'core'=2,'col'=4] {'col'}, dimensions={0}, use_global_device_ids=true | all-gather | bytes 983040 | tf_op jit(solution)/shard_map/all_gather | solution.py:42
  40.9 1.3 convert_reduce_fusion
  42.4 15.0 %all_gather.14 = bf16[512,768]{1,0:T(8,128)(2,1)S(1)} all-gather(bf16[128,768]{1,0:T(8,128)(2,1)S(1)} %fusion.17), channel_id=1, replica_groups=mesh['section'=16,'y'=8,'core'=2,'col'=4] {'col'}, dimensions={0}, use_global_device_ids=true | all-gather | bytes 983040 | tf_op jit(solution)/shard_map/all_gather | solution.py:42
  58.8 18.5 %collective-permute-start.2 = (bf16[256,768]{1,0:T(8,128)(2,1)S(1)}, bf16[256,768]{1,0:T(8,128)(2,1)S(1)}, u32[]{:S(2)}, u32[]{:S(2)}) collective-permute-start(bf16[256,768]{1,0:T(8,128)(2,1)S(1)} %convolution_convert_fusion.2), channel_id=1, source_target_pairs={{4,0},{0,4},{5,1},{1,5},{6,2},{2,6},{7,3},{3,7},{12,8},{8,12},{13,... | collective-permute-start | bytes 1179656 | tf_op jit(solution)/shard_map/ppermute | solution.py:13
  77.2 1.3 collective-permute-done.2
  78.6 1.3 add_convert_fusion
  79.8 3.5 %all-to-all-start.3 = ((bf16[8,32,768]{2,1,0:T(8,128)(2,1)}), bf16[8,32,768]{2,1,0:T(8,128)(2,1)S(1)}, u32[]{:S(2)}, u32[]{:S(2)}) async-start(bf16[8,32,768]{2,1,0:T(8,128)(2,1)} %bitcast.18), calls=%async_computation.3 | async-start | bytes 786432 | tf_op jit(solution)/shard_map/all_to_all | solution.py:52
  83.8 2.3 %collective-permute-start = (bf16[256,768]{1,0:T(8,128)(2,1)S(1)}, bf16[256,768]{1,0:T(8,128)(2,1)S(1)}, u32[]{:S(2)}, u32[]{:S(2)}) collective-permute-start(bf16[256,768]{1,0:T(8,128)(2,1)S(1)} %convolution_convert_fusion.3), channel_id=1, source_target_pairs={{4,0},{0,4},{5,1},{1,5},{6,2},{2,6},{7,3},{3,7},{12,8},{8,12},{13,... | collective-permute-start | bytes 1179656 | tf_op jit(solution)/shard_map/ppermute | solution.py:13
  86.1 1.3 collective-permute-done
  87.4 1.2 add_convert_fusion.1
  88.6 9.7 %all-to-all-done.3 = bf16[8,32,768]{2,1,0:T(8,128)(2,1)S(1)} async-done(((bf16[8,32,768]{2,1,0:T(8,128)(2,1)}), bf16[8,32,768]{2,1,0:T(8,128)(2,1)S(1)}, u32[]{:S(2)}, u32[]{:S(2)}) %all-to-all-start.3) | async-done | bytes 393248 | tf_op jit(solution)/shard_map/all_to_all | solution.py:52
  98.4 3.5 %all-to-all-start.1 = ((bf16[8,32,768]{2,1,0:T(8,128)(2,1)}), bf16[8,32,768]{2,1,0:T(8,128)(2,1)S(1)}, u32[]{:S(2)}, u32[]{:S(2)}) async-start(bf16[8,32,768]{2,1,0:T(8,128)(2,1)} %bitcast.8), calls=%async_computation.1 | async-start | bytes 786432 | tf_op jit(solution)/shard_map/all_to_all | solution.py:52
  102.7 10.8 %collective-permute-start.3 = (bf16[32,768]{1,0:T(8,128)(2,1)S(1)}, bf16[32,768]{1,0:T(8,128)(2,1)S(1)}, u32[]{:S(2)}, u32[]{:S(2)}) collective-permute-start(bf16[32,768]{1,0:T(8,128)(2,1)S(1)} %fusion.18), channel_id=1, source_target_pairs={{64,0},{128,64},{192,128},{256,192},{320,256},{384,320},{448,384},... | collective-permute-start | bytes 147464 | tf_op jit(solution)/shard_map/ppermute | solution.py:13
  113.5 3.4 %all-to-all-done.1 = bf16[8,32,768]{2,1,0:T(8,128)(2,1)S(1)} async-done(((bf16[8,32,768]{2,1,0:T(8,128)(2,1)}), bf16[8,32,768]{2,1,0:T(8,128)(2,1)S(1)}, u32[]{:S(2)}, u32[]{:S(2)}) %all-to-all-start.1) | async-done | bytes 393248 | tf_op jit(solution)/shard_map/all_to_all | solution.py:52
  117.8 1.9 %collective-permute-start.1 = (bf16[32,768]{1,0:T(8,128)(2,1)S(1)}, bf16[32,768]{1,0:T(8,128)(2,1)S(1)}, u32[]{:S(2)}, u32[]{:S(2)}) collective-permute-start(bf16[32,768]{1,0:T(8,128)(2,1)S(1)} %fusion.19), channel_id=1, source_target_pairs={{960,0},{0,64},{64,128},{128,192},{192,256},{256,320},{320,384},{3... | collective-permute-start | bytes 147464 | tf_op jit(solution)/shard_map/ppermute | solution.py:13
  119.7 17.2 %all_gather.15 = bf16[512,768]{1,0:T(8,128)(2,1)S(1)} all-gather(bf16[32,768]{1,0:T(8,128)(2,1)S(1)} %collective-permute-done.3), channel_id=1, replica_groups=mesh['section'=16,'y'=8,'core'=2,'col'=4] {'y','core'}, dimensions={0}, use_global_device_ids=true | all-gather | bytes 835584 | tf_op jit(solution)/shard_map/all_gather | solution.py:58
  136.9 17.7 %all_gather.13 = bf16[512,768]{1,0:T(8,128)(2,1)S(1)} all-gather(bf16[32,768]{1,0:T(8,128)(2,1)S(1)} %collective-permute-done.1), channel_id=1, replica_groups=mesh['section'=16,'y'=8,'core'=2,'col'=4] {'y','core'}, dimensions={0}, use_global_device_ids=true | all-gather | bytes 835584 | tf_op jit(solution)/shard_map/all_gather | solution.py:58
  154.6 0.9 copy.9
  (21 shorter events, 4.9 us)
Async XLA Ops:
  0.6 1.3 copy-start
  4.7 5.0 %copy-start.1 = (bf16[1,768,768]{2,1,0:T(8,128)(2,1)S(1)}, bf16[1,768,768]{2,1,0:T(8,128)(2,1)}, u32[]{:S(2)}) copy-start(bf16[1,768,768]{2,1,0:T(8,128)(2,1)} %param.7) | copy-start | bytes 3538948
  4.7 13.3 %all-to-all-start = ((bf16[4,128,768]{2,1,0:T(8,128)(2,1)}), bf16[4,128,768]{2,1,0:T(8,128)(2,1)S(1)}, u32[]{:S(2)}, u32[]{:S(2)}) async-start(bf16[4,128,768]{2,1,0:T(8,128)(2,1)} %bitcast.57), calls=%async_computation | async-start | bytes 1572864 | tf_op jit(solution)/shard_map/all_to_all | solution.py:36
  18.0 22.9 %all-to-all-start.2 = ((bf16[4,128,768]{2,1,0:T(8,128)(2,1)}), bf16[4,128,768]{2,1,0:T(8,128)(2,1)}, u32[]{:S(2)}, u32[]{:S(2)}) async-start(bf16[4,128,768]{2,1,0:T(8,128)(2,1)} %bitcast.58), calls=%async_computation.2 | async-start | bytes 1572864 | tf_op jit(solution)/shard_map/all_to_all | solution.py:36
  22.4 19.8 %copy-start.3 = (bf16[1,128,768]{2,1,0:T(8,128)(2,1)S(1)}, bf16[1,128,768]{2,1,0:T(8,128)(2,1)}, u32[]{:S(2)}) copy-start(bf16[1,128,768]{2,1,0:T(8,128)(2,1)} %param.9) | copy-start | bytes 589828
  58.8 19.8 %collective-permute-start.2 = (bf16[256,768]{1,0:T(8,128)(2,1)S(1)}, bf16[256,768]{1,0:T(8,128)(2,1)S(1)}, u32[]{:S(2)}, u32[]{:S(2)}) collective-permute-start(bf16[256,768]{1,0:T(8,128)(2,1)S(1)} %convolution_convert_fusion.2), channel_id=1, source_target_pairs={{4,0},{0,4},{5,1},{1,5},{6,2},{2,6},{7,3},{3,7},{12,8},{8,12},{13,... | collective-permute-start | bytes 1179656 | tf_op jit(solution)/shard_map/ppermute | solution.py:13
  78.6 4.7 %copy-start.2 = (bf16[8,1,32,768]{3,2,1,0:T(8,128)(2,1)S(1)}, bf16[8,1,32,768]{3,2,1,0:T(8,128)(2,1)}, u32[]{:S(2)}) copy-start(bf16[8,1,32,768]{3,2,1,0:T(8,128)(2,1)} %get-tuple-element.7) | copy-start | bytes 1179652
  79.8 18.5 %all-to-all-start.3 = ((bf16[8,32,768]{2,1,0:T(8,128)(2,1)}), bf16[8,32,768]{2,1,0:T(8,128)(2,1)S(1)}, u32[]{:S(2)}, u32[]{:S(2)}) async-start(bf16[8,32,768]{2,1,0:T(8,128)(2,1)} %bitcast.18), calls=%async_computation.3 | async-start | bytes 786432 | tf_op jit(solution)/shard_map/all_to_all | solution.py:52
  83.8 3.6 %collective-permute-start = (bf16[256,768]{1,0:T(8,128)(2,1)S(1)}, bf16[256,768]{1,0:T(8,128)(2,1)S(1)}, u32[]{:S(2)}, u32[]{:S(2)}) collective-permute-start(bf16[256,768]{1,0:T(8,128)(2,1)S(1)} %convolution_convert_fusion.3), channel_id=1, source_target_pairs={{4,0},{0,4},{5,1},{1,5},{6,2},{2,6},{7,3},{3,7},{12,8},{8,12},{13,... | collective-permute-start | bytes 1179656 | tf_op jit(solution)/shard_map/ppermute | solution.py:13
  98.4 18.5 %all-to-all-start.1 = ((bf16[8,32,768]{2,1,0:T(8,128)(2,1)}), bf16[8,32,768]{2,1,0:T(8,128)(2,1)S(1)}, u32[]{:S(2)}, u32[]{:S(2)}) async-start(bf16[8,32,768]{2,1,0:T(8,128)(2,1)} %bitcast.8), calls=%async_computation.1 | async-start | bytes 786432 | tf_op jit(solution)/shard_map/all_to_all | solution.py:52
  102.7 17.0 %collective-permute-start.3 = (bf16[32,768]{1,0:T(8,128)(2,1)S(1)}, bf16[32,768]{1,0:T(8,128)(2,1)S(1)}, u32[]{:S(2)}, u32[]{:S(2)}) collective-permute-start(bf16[32,768]{1,0:T(8,128)(2,1)S(1)} %fusion.18), channel_id=1, source_target_pairs={{64,0},{128,64},{192,128},{256,192},{320,256},{384,320},{448,384},... | collective-permute-start | bytes 147464 | tf_op jit(solution)/shard_map/ppermute | solution.py:13
  117.8 19.1 %collective-permute-start.1 = (bf16[32,768]{1,0:T(8,128)(2,1)S(1)}, bf16[32,768]{1,0:T(8,128)(2,1)S(1)}, u32[]{:S(2)}, u32[]{:S(2)}) collective-permute-start(bf16[32,768]{1,0:T(8,128)(2,1)S(1)} %fusion.19), channel_id=1, source_target_pairs={{960,0},{0,64},{64,128},{128,192},{192,256},{256,320},{320,384},{3... | collective-permute-start | bytes 147464 | tf_op jit(solution)/shard_map/ppermute | solution.py:13

commit v2 on v1

--- a/solution.py
+++ b/solution.py
@@ -37,25 +37,30 @@
     return parts.astype(jnp.float32).sum(0)
 
 
+def given_to_all(block, axis):
+    copies = jnp.broadcast_to(block[None], (lax.axis_size(axis),) + block.shape)
+    blocks = lax.all_to_all(copies, axis, 0, 0, tiled=True)
+    return blocks.reshape(-1, block.shape[1])
+
+
 def feature_sum(hidden_part, weight, contract, residual, shift_by):
-    rows, ny = lax.axis_size("y") * lax.axis_size("core"), lax.axis_size("y")
-    gathered = lax.all_gather(hidden_part, "col", axis=0, tiled=True)
-    tokens, width = gathered.shape
-    piece = tokens // rows
-    by_core = gathered.reshape(ny, 2, piece, width)
+    ny = lax.axis_size("y")
+    gathered = given_to_all(hidden_part, "col")
+    half = gathered.shape[0] // 2
+    piece = half // ny
     core = lax.axis_index("core")
-    theirs = lax.dynamic_slice_in_dim(by_core, 1 - core, 1, 1).reshape(tokens // 2, width)
-    ours = lax.dynamic_slice_in_dim(by_core, core, 1, 1).reshape(tokens // 2, width)
+    theirs = lax.dynamic_slice_in_dim(gathered, (1 - core) * half, half, 0)
+    ours = lax.dynamic_slice_in_dim(gathered, core * half, half, 0)
     sent = product(theirs, weight, contract).astype(jnp.bfloat16)
     arrived = passed_along(sent, "core", 1)
     chip_sum = (product(ours, weight, contract) + arrived.astype(jnp.float32)).astype(jnp.bfloat16)
     parts = lax.all_to_all(chip_sum.reshape(ny, piece, -1), "y", 0, 0, tiled=True)
     summed = parts.astype(jnp.float32).sum(0)
-    mine = lax.axis_index("y") * 2 + core
+    mine = core * ny + lax.axis_index("y")
     own_residual = lax.dynamic_slice_in_dim(residual, mine * piece, piece, 0)
     result = (own_residual.astype(jnp.float32) + summed).astype(jnp.bfloat16)
     moved = passed_along(result, "section", shift_by)
-    return lax.all_gather(moved, ("y", "core"), axis=0, tiled=True)
+    return lax.all_gather(given_to_all(moved, "y"), "core", axis=0, tiled=True)
 
 
 def body(tokens, up_weight, down_weight, out_grad, saved_hidden):

time: 157 us -> 162 us (1.032)
  blocking collectives: 68.4 us -> 12.4 us
  waiting for transfers between devices: 21.3 us -> 72.2 us
  starting transfers between devices: 49.5 us -> 57.3 us
  matrix products: 9.08 us -> 11.2 us
    all_gather x4 -> x2, blocking collectives: 68.4 us -> 12.4 us  [feature_sum(): return lax.all_gather(given_to_all(moved, 'y'), 'core', axis=0, tiled=True)]
    all_to_all x0 -> x4, waiting for transfers between devices: none -> 32.7 us  [given_to_all(): blocks = lax.all_to_all(copies, axis, 0, 0, tiled=True)]
    all_to_all x0 -> x4, starting transfers between devices: none -> 14.6 us  [given_to_all(): blocks = lax.all_to_all(copies, axis, 0, 0, tiled=True)]
    all_to_all x2, waiting for transfers between devices: 5.52 us -> 17.8 us  [hidden_share(): lax.all_to_all(partial.reshape(n, -1, partial.shape[1]), 'col', 0, 0, til...]
    all_to_all x2, waiting for transfers between devices: 13.1 us -> 19.3 us  [feature_sum(): lax.all_to_all(chip_sum.reshape(ny, piece, -1), 'y', 0, 0, tiled=True)]
    ppermute x4, starting transfers between devices: 33.5 us -> 27.3 us  [passed_along(): return lax.ppermute(block, axis, route)]
    broadcast_in_dim x0 -> x4, local copies, waits for them, and re-layouts: none -> 3.41 us  [given_to_all(): copies = jnp.broadcast_to(block[None], (lax.axis_size(axis),) + block.shape)]
    dot_general x6, matrix products: 9.08 us -> 11.2 us  [product(): lax.dot_general(operand, weight, (((1,), (contract,)), ((), ())), preferr...]
  transfers between devices with their start and end apart: 8 -> 12, of which waited for: 5 -> 10; matrix products, arithmetic and copies ran while one was open for 4% -> 6% of each run, Pallas kernels for 0% -> 0%
where the time goes in v2:
time: 162 us; the launch traced here: 161 us
  waiting for transfers between devices  72.2 us (45%)
  starting transfers between devices  57.3 us (35%)
  blocking collectives  12.4 us (8%)
  matrix products  11.2 us (7%)
  local copies, waits for them, and re-layouts  5.2 us (3%)
  other arithmetic  2.22 us (1%)
    all_to_all x4, waiting for transfers between devices, given_to_all(): blocks = lax.all_to_all(copies, axis, 0, 0, tiled=True)  32.7 us
    ppermute x4, starting transfers between devices, passed_along(): return lax.ppermute(block, axis, route)  27.3 us
    all_to_all x2, waiting for transfers between devices, feature_sum(): lax.all_to_all(chip_sum.reshape(ny, piece, -1), 'y', 0, 0, tiled=True)  19.3 us
    all_to_all x2, waiting for transfers between devices, hidden_share(): lax.all_to_all(partial.reshape(n, -1, partial.shape[1]), 'col', 0, 0, til...  17.8 us
    all_to_all x4, starting transfers between devices, given_to_all(): blocks = lax.all_to_all(copies, axis, 0, 0, tiled=True)  14.6 us
    all_gather x2, blocking collectives, feature_sum(): return lax.all_gather(given_to_all(moved, 'y'), 'core', axis=0, tiled=True)  12.4 us
    dot_general x6, matrix products, product(): lax.dot_general(operand, weight, (((1,), (contract,)), ((), ())), preferr...  11.2 us
    all_to_all x2, starting transfers between devices, hidden_share(): lax.all_to_all(partial.reshape(n, -1, partial.shape[1]), 'col', 0, 0, til...  8.47 us
  transfers between devices with their start and end apart: 12, of which 10 were waited for; matrix products, arithmetic and copies ran while one was open for 6% of the time, Pallas kernels for 0%

profile of v2, /device:TPU:1, one launch (start us, length us, event | category | flops | bytes accessed | tf_op | source)
XLA Modules:
  0.0 161.4 jit_solution(16123894348709480065)
XLA Ops:
  0.6 3.3 %convolution_convert_fusion.1 = bf16[512,768]{1,0:T(8,128)(2,1)} fusion(bf16[1,768,768]{2,1,0:T(8,128)(2,1)} %param.6, bf16[1,512,768]{2,1,0:T(8,128)(2,1)} %param.5), kind=kOutput, calls=%fused_computation.3 | convolution fusion | flops 604372992 | bytes 2752512 | tf_op jit(solution)/shard_map/dot_general | solution.py:28
  3.9 5.0 %all-to-all-start = ((bf16[4,128,768]{2,1,0:T(8,128)(2,1)}), bf16[4,128,768]{2,1,0:T(8,128)(2,1)S(1)}, u32[]{:S(2)}, u32[]{:S(2)}) async-start(bf16[4,128,768]{2,1,0:T(8,128)(2,1)} %bitcast.3), calls=%async_computation | async-start | bytes 1572864 | tf_op jit(solution)/shard_map/all_to_all | solution.py:36
  10.6 6.6 %all-to-all-done = bf16[4,128,768]{2,1,0:T(8,128)(2,1)S(1)} async-done(((bf16[4,128,768]{2,1,0:T(8,128)(2,1)}), bf16[4,128,768]{2,1,0:T(8,128)(2,1)S(1)}, u32[]{:S(2)}, u32[]{:S(2)}) %all-to-all-start) | async-done | bytes 786464 | tf_op jit(solution)/shard_map/all_to_all | solution.py:36
  17.2 3.5 %all-to-all-start.4 = ((bf16[4,128,768]{2,1,0:T(8,128)(2,1)}), bf16[4,128,768]{2,1,0:T(8,128)(2,1)S(1)}, u32[]{:S(2)}, u32[]{:S(2)}) async-start(bf16[4,128,768]{2,1,0:T(8,128)(2,1)} %bitcast.11), calls=%async_computation.4 | async-start | bytes 1572864 | tf_op jit(solution)/shard_map/all_to_all | solution.py:36
  20.9 11.1 %all-to-all-done.4 = bf16[4,128,768]{2,1,0:T(8,128)(2,1)S(1)} async-done(((bf16[4,128,768]{2,1,0:T(8,128)(2,1)}), bf16[4,128,768]{2,1,0:T(8,128)(2,1)S(1)}, u32[]{:S(2)}, u32[]{:S(2)}) %all-to-all-start.4) | async-done | bytes 786464 | tf_op jit(solution)/shard_map/all_to_all | solution.py:36
  33.0 3.5 %all-to-all-start.1 = ((bf16[4,128,768]{2,1,0:T(8,128)(2,1)}), bf16[4,128,768]{2,1,0:T(8,128)(2,1)S(1)}, u32[]{:S(2)}, u32[]{:S(2)}) async-start(bf16[4,128,768]{2,1,0:T(8,128)(2,1)} %broadcast_in_dim.14), calls=%async_computation.1 | async-start | bytes 1572864 | tf_op jit(solution)/shard_map/all_to_all | solution.py:42
  36.6 11.2 %all-to-all-done.1 = bf16[4,128,768]{2,1,0:T(8,128)(2,1)S(1)} async-done(((bf16[4,128,768]{2,1,0:T(8,128)(2,1)}), bf16[4,128,768]{2,1,0:T(8,128)(2,1)S(1)}, u32[]{:S(2)}, u32[]{:S(2)}) %all-to-all-start.1) | async-done | bytes 786464 | tf_op jit(solution)/shard_map/all_to_all | solution.py:42
  49.0 17.7 %collective-permute-start = (bf16[256,768]{1,0:T(8,128)(2,1)}, bf16[256,768]{1,0:T(8,128)(2,1)S(1)}, u32[]{:S(2)}, u32[]{:S(2)}) collective-permute-start(bf16[256,768]{1,0:T(8,128)(2,1)} %convolution_convert_fusion.3), channel_id=1, source_target_pairs={{4,0},{0,4},{5,1},{1,5},{6,2},{2,6},{7,3},{3,7},{12,8},{8,12},{13,... | collective-permute-start | bytes 1179656 | tf_op jit(solution)/shard_map/ppermute | solution.py:13
  67.8 4.2 %all-to-all-start.5 = ((bf16[4,128,768]{2,1,0:T(8,128)(2,1)}), bf16[4,128,768]{2,1,0:T(8,128)(2,1)}, u32[]{:S(2)}, u32[]{:S(2)}) async-start(bf16[4,128,768]{2,1,0:T(8,128)(2,1)} %broadcast_in_dim.36), calls=%async_computation.5 | async-start | bytes 1572864 | tf_op jit(solution)/shard_map/all_to_all | solution.py:42
  73.3 11.2 %all-to-all-done.5 = bf16[4,128,768]{2,1,0:T(8,128)(2,1)} async-done(((bf16[4,128,768]{2,1,0:T(8,128)(2,1)}), bf16[4,128,768]{2,1,0:T(8,128)(2,1)}, u32[]{:S(2)}, u32[]{:S(2)}) %all-to-all-start.5) | async-done | bytes 786464 | tf_op jit(solution)/shard_map/all_to_all | solution.py:42
  84.5 3.5 %all-to-all-start.2 = ((bf16[8,32,768]{2,1,0:T(8,128)(2,1)}), bf16[8,32,768]{2,1,0:T(8,128)(2,1)S(1)}, u32[]{:S(2)}, u32[]{:S(2)}) async-start(bf16[8,32,768]{2,1,0:T(8,128)(2,1)} %bitcast.6), calls=%async_computation.2 | async-start | bytes 786432 | tf_op jit(solution)/shard_map/all_to_all | solution.py:57
  89.5 2.7 %collective-permute-start.2 = (bf16[256,768]{1,0:T(8,128)(2,1)S(1)}, bf16[256,768]{1,0:T(8,128)(2,1)S(1)}, u32[]{:S(2)}, u32[]{:S(2)}) collective-permute-start(bf16[256,768]{1,0:T(8,128)(2,1)S(1)} %convolution_convert_fusion.2), channel_id=1, source_target_pairs={{4,0},{0,4},{5,1},{1,5},{6,2},{2,6},{7,3},{3,7},{12,8},{8,12},{13,... | collective-permute-start | bytes 1179656 | tf_op jit(solution)/shard_map/ppermute | solution.py:13
  93.6 2.2 %add_convert_fusion = bf16[256,768]{1,0:T(8,128)(2,1)} fusion(bf16[256,768]{1,0:T(8,128)(2,1)S(1)} %collective-permute-done.2, bf16[1,768,768]{2,1,0:T(8,128)(2,1)S(1)} %copy-done.1, bf16[512,768]{1,0:T(8,128)(2,1)} %bitcast.14, s32[]{:T(128)S(6)} %select_n.13), kind=kOutput, calls=%fused_computation.17 | convolution fusion | flops 302579712 | bytes 2359300 | tf_op jit(solution)/shard_map/dot_general | solution.py:28
  95.8 7.1 %all-to-all-done.2 = bf16[8,32,768]{2,1,0:T(8,128)(2,1)S(1)} async-done(((bf16[8,32,768]{2,1,0:T(8,128)(2,1)}), bf16[8,32,768]{2,1,0:T(8,128)(2,1)S(1)}, u32[]{:S(2)}, u32[]{:S(2)}) %all-to-all-start.2) | async-done | bytes 393248 | tf_op jit(solution)/shard_map/all_to_all | solution.py:57
  102.9 3.5 %all-to-all-start.6 = ((bf16[8,32,768]{2,1,0:T(8,128)(2,1)}), bf16[8,32,768]{2,1,0:T(8,128)(2,1)S(1)}, u32[]{:S(2)}, u32[]{:S(2)}) async-start(bf16[8,32,768]{2,1,0:T(8,128)(2,1)} %bitcast.15), calls=%async_computation.6 | async-start | bytes 786432 | tf_op jit(solution)/shard_map/all_to_all | solution.py:57
  107.2 1.9 %collective-permute-start.1 = (bf16[32,768]{1,0:T(8,128)(2,1)S(1)}, bf16[32,768]{1,0:T(8,128)(2,1)S(1)}, u32[]{:S(2)}, u32[]{:S(2)}) collective-permute-start(bf16[32,768]{1,0:T(8,128)(2,1)S(1)} %fusion.32), channel_id=1, source_target_pairs={{960,0},{0,64},{64,128},{128,192},{192,256},{256,320},{320,384},{3... | collective-permute-start | bytes 147464 | tf_op jit(solution)/shard_map/ppermute | solution.py:13
  109.2 12.2 %all-to-all-done.6 = bf16[8,32,768]{2,1,0:T(8,128)(2,1)S(1)} async-done(((bf16[8,32,768]{2,1,0:T(8,128)(2,1)}), bf16[8,32,768]{2,1,0:T(8,128)(2,1)S(1)}, u32[]{:S(2)}, u32[]{:S(2)}) %all-to-all-start.6) | async-done | bytes 393248 | tf_op jit(solution)/shard_map/all_to_all | solution.py:57
  122.2 3.5 %all-to-all-start.3 = ((bf16[8,32,768]{2,1,0:T(8,128)(2,1)}), bf16[8,32,768]{2,1,0:T(8,128)(2,1)S(1)}, u32[]{:S(2)}, u32[]{:S(2)}) async-start(bf16[8,32,768]{2,1,0:T(8,128)(2,1)} %broadcast_in_dim.15), calls=%async_computation.3 | async-start | bytes 786432 | tf_op jit(solution)/shard_map/all_to_all | solution.py:42
  126.5 5.0 %collective-permute-start.3 = (bf16[32,768]{1,0:T(8,128)(2,1)S(1)}, bf16[32,768]{1,0:T(8,128)(2,1)S(1)}, u32[]{:S(2)}, u32[]{:S(2)}) collective-permute-start(bf16[32,768]{1,0:T(8,128)(2,1)S(1)} %fusion.31), channel_id=1, source_target_pairs={{64,0},{128,64},{192,128},{256,192},{320,256},{384,320},{448,384},... | collective-permute-start | bytes 147464 | tf_op jit(solution)/shard_map/ppermute | solution.py:13
  132.7 5.1 %all-to-all-done.3 = bf16[8,32,768]{2,1,0:T(8,128)(2,1)S(1)} async-done(((bf16[8,32,768]{2,1,0:T(8,128)(2,1)}), bf16[8,32,768]{2,1,0:T(8,128)(2,1)S(1)}, u32[]{:S(2)}, u32[]{:S(2)}) %all-to-all-start.3) | async-done | bytes 393248 | tf_op jit(solution)/shard_map/all_to_all | solution.py:42
  138.6 3.5 %all-to-all-start.7 = ((bf16[8,32,768]{2,1,0:T(8,128)(2,1)}), bf16[8,32,768]{2,1,0:T(8,128)(2,1)S(1)}, u32[]{:S(2)}, u32[]{:S(2)}) async-start(bf16[8,32,768]{2,1,0:T(8,128)(2,1)} %broadcast_in_dim.37), calls=%async_computation.7 | async-start | bytes 786432 | tf_op jit(solution)/shard_map/all_to_all | solution.py:42
  142.1 5.3 %all_gather.6 = bf16[512,768]{1,0:T(8,128)(2,1)S(1)} all-gather(bf16[256,768]{1,0:T(8,128)(2,1)S(1)} %bitcast.52), channel_id=1, replica_groups=mesh['section'=16,'y'=8,'core'=2,'col'=4] {'core'}, dimensions={0}, use_global_device_ids=true | all-gather | bytes 1179648 | tf_op jit(solution)/shard_map/all_gather | solution.py:63
  147.4 5.1 %all-to-all-done.7 = bf16[8,32,768]{2,1,0:T(8,128)(2,1)S(1)} async-done(((bf16[8,32,768]{2,1,0:T(8,128)(2,1)}), bf16[8,32,768]{2,1,0:T(8,128)(2,1)S(1)}, u32[]{:S(2)}, u32[]{:S(2)}) %all-to-all-start.7) | async-done | bytes 393248 | tf_op jit(solution)/shard_map/all_to_all | solution.py:42
  152.5 7.1 %all_gather.7 = bf16[512,768]{1,0:T(8,128)(2,1)S(1)} all-gather(bf16[256,768]{1,0:T(8,128)(2,1)S(1)} %bitcast.53), channel_id=1, replica_groups=mesh['section'=16,'y'=8,'core'=2,'col'=4] {'core'}, dimensions={0}, use_global_device_ids=true | all-gather | bytes 1179648 | tf_op jit(solution)/shard_map/all_gather | solution.py:63
  (30 shorter events, 15.6 us)
Async XLA Ops:
  0.6 8.3 %copy-start = (bf16[1,768,768]{2,1,0:T(8,128)(2,1)S(1)}, bf16[1,768,768]{2,1,0:T(8,128)(2,1)}, u32[]{:S(2)}) copy-start(bf16[1,768,768]{2,1,0:T(8,128)(2,1)} %param.7) | copy-start | bytes 3538948
  3.9 5.0 %copy-start.3 = (bf16[1,512,768]{2,1,0:T(8,128)(2,1)S(1)}, bf16[1,512,768]{2,1,0:T(8,128)(2,1)}, u32[]{:S(2)}) copy-start(bf16[1,512,768]{2,1,0:T(8,128)(2,1)} %param.8) | copy-start | bytes 2359300
  3.9 13.3 %all-to-all-start = ((bf16[4,128,768]{2,1,0:T(8,128)(2,1)}), bf16[4,128,768]{2,1,0:T(8,128)(2,1)S(1)}, u32[]{:S(2)}, u32[]{:S(2)}) async-start(bf16[4,128,768]{2,1,0:T(8,128)(2,1)} %bitcast.3), calls=%async_computation | async-start | bytes 1572864 | tf_op jit(solution)/shard_map/all_to_all | solution.py:36
  17.2 14.8 %all-to-all-start.4 = ((bf16[4,128,768]{2,1,0:T(8,128)(2,1)}), bf16[4,128,768]{2,1,0:T(8,128)(2,1)S(1)}, u32[]{:S(2)}, u32[]{:S(2)}) async-start(bf16[4,128,768]{2,1,0:T(8,128)(2,1)} %bitcast.11), calls=%async_computation.4 | async-start | bytes 1572864 | tf_op jit(solution)/shard_map/all_to_all | solution.py:36
  33.0 14.8 %all-to-all-start.1 = ((bf16[4,128,768]{2,1,0:T(8,128)(2,1)}), bf16[4,128,768]{2,1,0:T(8,128)(2,1)S(1)}, u32[]{:S(2)}, u32[]{:S(2)}) async-start(bf16[4,128,768]{2,1,0:T(8,128)(2,1)} %broadcast_in_dim.14), calls=%async_computation.1 | async-start | bytes 1572864 | tf_op jit(solution)/shard_map/all_to_all | solution.py:42
  36.6 30.1 %copy-start.2 = (bf16[1,128,768]{2,1,0:T(8,128)(2,1)S(1)}, bf16[1,128,768]{2,1,0:T(8,128)(2,1)}, u32[]{:S(2)}) copy-start(bf16[1,128,768]{2,1,0:T(8,128)(2,1)} %param.9) | copy-start | bytes 589828
  49.0 23.0 %collective-permute-start = (bf16[256,768]{1,0:T(8,128)(2,1)}, bf16[256,768]{1,0:T(8,128)(2,1)S(1)}, u32[]{:S(2)}, u32[]{:S(2)}) collective-permute-start(bf16[256,768]{1,0:T(8,128)(2,1)} %convolution_convert_fusion.3), channel_id=1, source_target_pairs={{4,0},{0,4},{5,1},{1,5},{6,2},{2,6},{7,3},{3,7},{12,8},{8,12},{13,... | collective-permute-start | bytes 1179656 | tf_op jit(solution)/shard_map/ppermute | solution.py:13
  67.8 16.7 %all-to-all-start.5 = ((bf16[4,128,768]{2,1,0:T(8,128)(2,1)}), bf16[4,128,768]{2,1,0:T(8,128)(2,1)}, u32[]{:S(2)}, u32[]{:S(2)}) async-start(bf16[4,128,768]{2,1,0:T(8,128)(2,1)} %broadcast_in_dim.36), calls=%async_computation.5 | async-start | bytes 1572864 | tf_op jit(solution)/shard_map/all_to_all | solution.py:42
  72.0 16.0 %copy-start.1 = (bf16[1,768,768]{2,1,0:T(8,128)(2,1)S(1)}, bf16[1,768,768]{2,1,0:T(8,128)(2,1)}, u32[]{:S(2)}) copy-start(bf16[1,768,768]{2,1,0:T(8,128)(2,1)} %param.6) | copy-start | bytes 3538948
  84.5 18.4 %all-to-all-start.2 = ((bf16[8,32,768]{2,1,0:T(8,128)(2,1)}), bf16[8,32,768]{2,1,0:T(8,128)(2,1)S(1)}, u32[]{:S(2)}, u32[]{:S(2)}) async-start(bf16[8,32,768]{2,1,0:T(8,128)(2,1)} %bitcast.6), calls=%async_computation.2 | async-start | bytes 786432 | tf_op jit(solution)/shard_map/all_to_all | solution.py:57
  89.5 4.0 %collective-permute-start.2 = (bf16[256,768]{1,0:T(8,128)(2,1)S(1)}, bf16[256,768]{1,0:T(8,128)(2,1)S(1)}, u32[]{:S(2)}, u32[]{:S(2)}) collective-permute-start(bf16[256,768]{1,0:T(8,128)(2,1)S(1)} %convolution_convert_fusion.2), channel_id=1, source_target_pairs={{4,0},{0,4},{5,1},{1,5},{6,2},{2,6},{7,3},{3,7},{12,8},{8,12},{13,... | collective-permute-start | bytes 1179656 | tf_op jit(solution)/shard_map/ppermute | solution.py:13
  102.9 18.5 %all-to-all-start.6 = ((bf16[8,32,768]{2,1,0:T(8,128)(2,1)}), bf16[8,32,768]{2,1,0:T(8,128)(2,1)S(1)}, u32[]{:S(2)}, u32[]{:S(2)}) async-start(bf16[8,32,768]{2,1,0:T(8,128)(2,1)} %bitcast.15), calls=%async_computation.6 | async-start | bytes 786432 | tf_op jit(solution)/shard_map/all_to_all | solution.py:57
  107.2 14.2 %collective-permute-start.1 = (bf16[32,768]{1,0:T(8,128)(2,1)S(1)}, bf16[32,768]{1,0:T(8,128)(2,1)S(1)}, u32[]{:S(2)}, u32[]{:S(2)}) collective-permute-start(bf16[32,768]{1,0:T(8,128)(2,1)S(1)} %fusion.32), channel_id=1, source_target_pairs={{960,0},{0,64},{64,128},{128,192},{192,256},{256,320},{320,384},{3... | collective-permute-start | bytes 147464 | tf_op jit(solution)/shard_map/ppermute | solution.py:13
  122.2 15.7 %all-to-all-start.3 = ((bf16[8,32,768]{2,1,0:T(8,128)(2,1)}), bf16[8,32,768]{2,1,0:T(8,128)(2,1)S(1)}, u32[]{:S(2)}, u32[]{:S(2)}) async-start(bf16[8,32,768]{2,1,0:T(8,128)(2,1)} %broadcast_in_dim.15), calls=%async_computation.3 | async-start | bytes 786432 | tf_op jit(solution)/shard_map/all_to_all | solution.py:42
  126.5 6.2 %collective-permute-start.3 = (bf16[32,768]{1,0:T(8,128)(2,1)S(1)}, bf16[32,768]{1,0:T(8,128)(2,1)S(1)}, u32[]{:S(2)}, u32[]{:S(2)}) collective-permute-start(bf16[32,768]{1,0:T(8,128)(2,1)S(1)} %fusion.31), channel_id=1, source_target_pairs={{64,0},{128,64},{192,128},{256,192},{320,256},{384,320},{448,384},... | collective-permute-start | bytes 147464 | tf_op jit(solution)/shard_map/ppermute | solution.py:13
  138.6 13.9 %all-to-all-start.7 = ((bf16[8,32,768]{2,1,0:T(8,128)(2,1)}), bf16[8,32,768]{2,1,0:T(8,128)(2,1)S(1)}, u32[]{:S(2)}, u32[]{:S(2)}) async-start(bf16[8,32,768]{2,1,0:T(8,128)(2,1)} %broadcast_in_dim.37), calls=%async_computation.7 | async-start | bytes 786432 | tf_op jit(solution)/shard_map/all_to_all | solution.py:42

commit v3 on v1

v3 whole, which is shorter than its diff:
```python
import jax
import jax.numpy as jnp
from jax import lax
from jax.sharding import Mesh, PartitionSpec as P

inv_root_two = 0.7071067811865476
inv_root_tau = 0.3989422804014327


def gelu_value(hidden):
    return 0.5 * hidden * (1.0 + lax.erf(hidden * inv_root_two))


def gelu_slope(hidden):
    return (
        0.5 * (1.0 + lax.erf(hidden * inv_root_two))
        + hidden * jnp.exp(-0.5 * hidden * hidden) * inv_root_tau
    )


def product(operand, weight, contract):
    return lax.dot_general(
        operand, weight, (((1,), (contract,)), ((), ())), preferred_element_type=jnp.float32
    )


def swapped(block):
    return lax.ppermute(block, "core", [(0, 1), (1, 0)])


def body(tokens, up_weight, down_weight, out_grad, saved_hidden):
    inputs, w_up, w_down, upstream = tokens[0], up_weight[0], down_weight[0], out_grad[0]
    stored = saved_hidden[0].astype(jnp.float32)
    ncol, ny, nz = lax.axis_size("col"), lax.axis_size("y"), lax.axis_size("section")
    core = lax.axis_index("core")
    forward = core == 0
    count = inputs.shape[0]
    arrived = swapped(jnp.where(forward, w_up, w_down))

    def by_col(partial):
        return partial.astype(jnp.bfloat16).reshape(ncol, count // ncol, -1)

    partials = jnp.stack(
        [by_col(product(inputs, w_up, 0)), by_col(product(upstream, w_down, 1))], axis=1
    )
    sums = lax.all_to_all(partials, "col", 0, 0, tiled=True).astype(jnp.float32).sum(0)
    active = gelu_value(sums[0]).astype(jnp.bfloat16)
    hidden_grad = (sums[1] * gelu_slope(stored)).astype(jnp.bfloat16)
    copies = jnp.concatenate(
        [jnp.broadcast_to(part[None], (ncol,) + part.shape) for part in (active, hidden_grad)]
    )
    gathered = lax.all_to_all(copies, ("core", "col"), 0, 0, tiled=True)
    first = gathered[:ncol].reshape(count, -1)
    second = gathered[ncol:].reshape(count, -1)
    chip_sum = lax.cond(
        forward,
        lambda: product(first, w_down, 0) + product(second, arrived, 0),
        lambda: product(first, arrived, 1) + product(second, w_up, 1),
    ).astype(jnp.bfloat16)
    piece = count // ny
    summed = lax.all_to_all(chip_sum.reshape(ny, piece, -1), "y", 0, 0, tiled=True)
    summed = summed.astype(jnp.float32).sum(0)
    start = lax.axis_index("y") * piece
    residual = jnp.where(
        forward,
        lax.dynamic_slice_in_dim(inputs, start, piece, 0),
        lax.dynamic_slice_in_dim(upstream, start, piece, 0),
    )
    result = (residual.astype(jnp.float32) + summed).astype(jnp.bfloat16)
    route = [(2 * s, 2 * ((s + 1) % nz)) for s in range(nz)]
    route += [(2 * s + 1, 2 * ((s - 1) % nz) + 1) for s in range(nz)]
    moved = lax.ppermute(result, ("section", "core"), route)
    pieces = jnp.broadcast_to(moved[None], (ny,) + moved.shape)
    mine = lax.all_to_all(pieces, "y", 0, 0, tiled=True).reshape(count, -1)
    other = swapped(mine)
    next_tokens = jnp.where(forward, mine, other)
    prev_grads = jnp.where(forward, other, mine)
    return (next_tokens[None], prev_grads[None])


def solution(mesh):
    sections, rows, cols = mesh.devices.shape
    fine = Mesh(mesh.devices.reshape(sections, rows // 2, 2, cols), ("section", "y", "core", "col"))
    features = P("section", None, "col")
    return jax.shard_map(
        body,
        mesh=fine,
        in_specs=(
            features,
            P("section", "col", ("y", "core")),
            P("section", ("y", "core"), "col"),
            features,
            P("section", "col", ("y", "core")),
        ),
        out_specs=(features, features),
        check_vma=False,
    )
```

time: 157 us -> 146 us (0.930)
  blocking collectives: 68.4 us -> 40.1 us
  waiting for transfers between devices: 21.3 us -> 43.3 us
  starting transfers between devices: 49.5 us -> 44.8 us
  other arithmetic: 3.39 us -> 7.73 us
  matrix products: 9.08 us -> 6.12 us
  local copies, waits for them, and re-layouts: 3.91 us -> 2.11 us
    all_gather x4 -> x0, blocking collectives: 68.4 us -> none  [the longest x2 34.9 us: feature_sum(): return lax.all_gather(moved, ('y', 'core'), axis=0, tiled=True)]
    all_to_all x0 -> x2, blocking collectives: none -> 40.1 us  [the longest x1 22.9 us: body(): mine = lax.all_to_all(pieces, 'y', 0, 0, tiled=True).reshape(count, -1)]
    all_to_all x4 -> x2, waiting for transfers between devices: 18.6 us -> 39.7 us  [the longest x1 23.6 us: body(): lax.all_to_all(chip_sum.reshape(ny, piece, -1), 'y', 0, 0, tiled=True)]
    ppermute x4 -> x3, starting transfers between devices: 33.5 us -> 24.7 us  [the longest x1 17.2 us: body(): moved = lax.ppermute(result, ('section', 'core'), route)]
    all_to_all x4 -> x2, starting transfers between devices: 16.1 us -> 20.2 us  [the longest x1 16.6 us: body(): gathered = lax.all_to_all(copies, ('core', 'col'), 0, 0, tiled=True)]
    dot_general x6 -> x4, matrix products: 9.08 us -> 6.12 us  [product(): lax.dot_general(operand, weight, (((1,), (contract,)), ((), ())), preferr...]
    select_n x0 -> x1, other arithmetic: none -> 2.42 us  [body(): arrived = swapped(jnp.where(forward, w_up, w_down))]
    ppermute x4 -> x3, waiting for transfers between devices: 2.66 us -> 3.51 us  [the longest x2 1.89 us: swapped(): return lax.ppermute(block, 'core', [(0, 1), (1, 0)])]
  transfers between devices with their start and end apart: 8 -> 5, of which waited for: 5 -> 4; matrix products, arithmetic and copies ran while one was open for 4% -> 2% of each run, Pallas kernels for 0% -> 0%
where the time goes in v3:
time: 146 us; the launch traced here: 145 us
  starting transfers between devices  44.8 us (31%)
  waiting for transfers between devices  43.3 us (30%)
  blocking collectives  40.1 us (27%)
  other arithmetic  7.73 us (5%)
  matrix products  6.12 us (4%)
  local copies, waits for them, and re-layouts  2.11 us (1%)
    all_to_all x1, waiting for transfers between devices, body(): lax.all_to_all(chip_sum.reshape(ny, piece, -1), 'y', 0, 0, tiled=True)  23.6 us
    all_to_all x1, blocking collectives, body(): mine = lax.all_to_all(pieces, 'y', 0, 0, tiled=True).reshape(count, -1)  22.9 us
    ppermute x1, starting transfers between devices, body(): moved = lax.ppermute(result, ('section', 'core'), route)  17.2 us
    all_to_all x1, blocking collectives, body(): lax.all_to_all(partials, 'col', 0, 0, tiled=True).astype(jnp.float32).sum(0)  17.2 us
    all_to_all x1, starting transfers between devices, body(): gathered = lax.all_to_all(copies, ('core', 'col'), 0, 0, tiled=True)  16.6 us
    all_to_all x1, waiting for transfers between devices, body(): gathered = lax.all_to_all(copies, ('core', 'col'), 0, 0, tiled=True)  16.2 us
    ppermute x2, starting transfers between devices, swapped(): return lax.ppermute(block, 'core', [(0, 1), (1, 0)])  7.44 us
    dot_general x4, matrix products, product(): lax.dot_general(operand, weight, (((1,), (contract,)), ((), ())), preferr...  6.12 us
  transfers between devices with their start and end apart: 5, of which 4 were waited for; matrix products, arithmetic and copies ran while one was open for 2% of the time, Pallas kernels for 0%

profile of v3, /device:TPU:1, one launch (start us, length us, event | category | flops | bytes accessed | tf_op | source)
XLA Modules:
  0.0 145.0 jit_solution(5516682692007553801)
XLA Ops:
  0.7 2.4 %convolution_convert_fusion.1 = bf16[512,768]{1,0:T(8,128)(2,1)S(1)} fusion(bf16[1,512,768]{2,1,0:T(8,128)(2,1)} %param.7, bf16[1,768,768]{2,1,0:T(8,128)(2,1)} %param.8), kind=kOutput, calls=%fused_computation.6 | convolution fusion | flops 604372992 | bytes 2752512 | tf_op jit(solution)/shard_map/dot_general | solution.py:22
  3.1 0.8 convolution_convert_fusion
  4.1 17.2 %all_to_all.20 = bf16[4,2,128,768]{3,2,1,0:T(8,128)(2,1)S(1)} all-to-all(bf16[4,2,128,768]{3,2,1,0:T(8,128)(2,1)S(1)} %pad_maximum_fusion), channel_id=1, replica_groups=mesh['section'=16,'y'=8,'core'=2,'col'=4] {'col'}, dimensions={0} | all-to-all | bytes 3145728 | tf_op jit(solution)/shard_map/all_to_all | solution.py:46
  21.5 0.7 copy-done.2
  22.2 0.2 fusion.11
  22.6 1.3 pad_maximum_fusion.1
  23.9 16.6 %all-to-all-start.1 = ((bf16[8,128,768]{2,1,0:T(8,128)(2,1)}), bf16[8,128,768]{2,1,0:T(8,128)(2,1)S(1)}, u32[]{:S(2)}, u32[]{:S(2)}) async-start(bf16[8,128,768]{2,1,0:T(8,128)(2,1)} %pad_maximum_fusion.1), calls=%async_computation.1 | async-start | bytes 3145728 | tf_op jit(solution)/shard_map/all_to_all | solution.py:52
  40.5 2.4 %broadcast_select_fusion = bf16[768,768]{1,0:T(8,128)(2,1)} fusion(pred[]{:T(512)S(6)} %eq.3, bf16[1,768,768]{2,1,0:T(8,128)(2,1)S(1)} %copy-done, bf16[1,768,768]{2,1,0:T(8,128)(2,1)} %param.8), kind=kLoop, calls=%fused_computation.7 | loop fusion | flops 589824 | bytes 3538945 | tf_op jit(solution)/shard_map/jit(_where)/select_n | solution.py:38
  42.9 2.0 %collective-permute-start = (bf16[768,768]{1,0:T(8,128)(2,1)}, bf16[768,768]{1,0:T(8,128)(2,1)}, u32[]{:S(2)}, u32[]{:S(2)}) collective-permute-start(bf16[768,768]{1,0:T(8,128)(2,1)} %broadcast_select_fusion), channel_id=1, source_target_pairs={{0,4},{4,0},{1,5},{5,1},{2,6},{6,2},{3,7},{7,3},{8,12},{12,8},{9,1... | collective-permute-start | bytes 3538952 | tf_op jit(solution)/shard_map/ppermute | solution.py:28
  44.9 16.2 %all-to-all-done.1 = bf16[8,128,768]{2,1,0:T(8,128)(2,1)S(1)} async-done(((bf16[8,128,768]{2,1,0:T(8,128)(2,1)}), bf16[8,128,768]{2,1,0:T(8,128)(2,1)S(1)}, u32[]{:S(2)}, u32[]{:S(2)}) %all-to-all-start.1) | async-done | bytes 1572896 | tf_op jit(solution)/shard_map/all_to_all | solution.py:52
  61.2 1.1 copy-done.1
  62.4 2.9 %conditional.1 = (f32[512,768]{1,0:T(8,128)S(1)}, f32[512,768]{1,0:T(8,128)S(1)}) conditional(s32[]{:T(128)} %convert_element_type.41, (bf16[512,768]{1,0:T(8,128)(2,1)S(1)}, bf16[768,768]{1,0:T(8,128)(2,1)}, bf16[512,768]{1,0:T(8,128)(2,1)S(1)}, bf16[768,768]{1,0:T(8,128)(2,1)S(1)}) %tuple.31, (bf16[512,768]{1,0:T(8,128)(2,1)S(1)}, ...), branch_computations={%region_1.2_spmd, %region_2.3_spmd} | conditional | flops 1207959552 | bytes 7077904 | solution.py:55
  62.4 2.1 %fusion.16 = f32[512,768]{1,0:T(8,128)S(1)} fusion(bf16[512,768]{1,0:T(8,128)(2,1)S(1)} %get-tuple-element.19, bf16[768,768]{1,0:T(8,128)(2,1)} %get-tuple-element.20), kind=kOutput, calls=%fused_computation.32 | convolution fusion | flops 603979776 | bytes 3538944 | tf_op jit(solution)/shard_map/cond/branch_0_fun/dot_general | solution.py:22
  64.4 0.8 fusion.17
  65.3 1.0 add_convert_fusion
  66.3 3.5 %all-to-all-start.2 = ((bf16[8,64,768]{2,1,0:T(8,128)(2,1)}), bf16[8,64,768]{2,1,0:T(8,128)(2,1)S(1)}, u32[]{:S(2)}, u32[]{:S(2)}) async-start(bf16[8,64,768]{2,1,0:T(8,128)(2,1)} %bitcast.13), calls=%async_computation.2 | async-start | bytes 1572864 | tf_op jit(solution)/shard_map/all_to_all | solution.py:61
  69.8 23.6 %all-to-all-done.2 = bf16[8,64,768]{2,1,0:T(8,128)(2,1)S(1)} async-done(((bf16[8,64,768]{2,1,0:T(8,128)(2,1)}), bf16[8,64,768]{2,1,0:T(8,128)(2,1)S(1)}, u32[]{:S(2)}, u32[]{:S(2)}) %all-to-all-start.2) | async-done | bytes 786464 | tf_op jit(solution)/shard_map/all_to_all | solution.py:61
  93.5 1.0 fusion.10
  94.5 17.2 %collective-permute-start.1 = (bf16[64,768]{1,0:T(8,128)(2,1)S(1)}, bf16[64,768]{1,0:T(8,128)(2,1)S(1)}, u32[]{:S(2)}, u32[]{:S(2)}) collective-permute-start(bf16[64,768]{1,0:T(8,128)(2,1)S(1)} %fusion.10), channel_id=1, source_target_pairs={{0,64},{64,128},{128,192},{192,256},{256,320},{320,384},{384,448},... | collective-permute-start | bytes 294920 | tf_op jit(solution)/shard_map/ppermute | solution.py:72
  111.7 1.6 %collective-permute-done.1 = bf16[64,768]{1,0:T(8,128)(2,1)S(1)} collective-permute-done((bf16[64,768]{1,0:T(8,128)(2,1)S(1)}, bf16[64,768]{1,0:T(8,128)(2,1)S(1)}, u32[]{:S(2)}, u32[]{:S(2)}) %collective-permute-start.1) | collective-permute-done | bytes 98336 | tf_op jit(solution)/shard_map/ppermute | solution.py:72
  113.4 22.9 %all_to_all.21 = bf16[8,64,768]{2,1,0:T(8,128)(2,1)S(1)} all-to-all(bf16[8,64,768]{2,1,0:T(8,128)(2,1)S(1)} %broadcast_in_dim.32), channel_id=1, replica_groups=mesh['section'=16,'y'=8,'core'=2,'col'=4] {'y'}, dimensions={0} | all-to-all | bytes 1572864 | tf_op jit(solution)/shard_map/all_to_all | solution.py:74
  136.3 5.4 %collective-permute-start.2 = (bf16[512,768]{1,0:T(8,128)(2,1)S(1)}, bf16[512,768]{1,0:T(8,128)(2,1)S(1)}, u32[]{:S(2)}, u32[]{:S(2)}) collective-permute-start(bf16[512,768]{1,0:T(8,128)(2,1)S(1)} %bitcast.45), channel_id=1, source_target_pairs={{0,4},{4,0},{1,5},{5,1},{2,6},{6,2},{3,7},{7,3},{8,12},{12,8},{9,1... | collective-permute-start | bytes 2359304 | tf_op jit(solution)/shard_map/ppermute | solution.py:28
  141.8 1.9 %collective-permute-done.2 = bf16[512,768]{1,0:T(8,128)(2,1)S(1)} collective-permute-done((bf16[512,768]{1,0:T(8,128)(2,1)S(1)}, bf16[512,768]{1,0:T(8,128)(2,1)S(1)}, u32[]{:S(2)}, u32[]{:S(2)}) %collective-permute-start.2) | collective-permute-done | bytes 786464 | tf_op jit(solution)/shard_map/ppermute | solution.py:28
  143.7 1.3 select_bitcast_fusion
  (14 shorter events, 0.8 us)
Async XLA Ops:
  0.6 2.5 %copy-start = (bf16[1,768,768]{2,1,0:T(8,128)(2,1)S(1)}, bf16[1,768,768]{2,1,0:T(8,128)(2,1)}, u32[]{:S(2)}) copy-start(bf16[1,768,768]{2,1,0:T(8,128)(2,1)} %param.9) | copy-start | bytes 3538948
  0.6 2.5 %copy-start.3 = (bf16[1,512,768]{2,1,0:T(8,128)(2,1)S(1)}, bf16[1,512,768]{2,1,0:T(8,128)(2,1)}, u32[]{:S(2)}) copy-start(bf16[1,512,768]{2,1,0:T(8,128)(2,1)} %param.10) | copy-start | bytes 2359300
  21.3 0.9 copy-start.2
  23.9 37.2 %all-to-all-start.1 = ((bf16[8,128,768]{2,1,0:T(8,128)(2,1)}), bf16[8,128,768]{2,1,0:T(8,128)(2,1)S(1)}, u32[]{:S(2)}, u32[]{:S(2)}) async-start(bf16[8,128,768]{2,1,0:T(8,128)(2,1)} %pad_maximum_fusion.1), calls=%async_computation.1 | async-start | bytes 3145728 | tf_op jit(solution)/shard_map/all_to_all | solution.py:52
  42.9 18.3 %collective-permute-start = (bf16[768,768]{1,0:T(8,128)(2,1)}, bf16[768,768]{1,0:T(8,128)(2,1)}, u32[]{:S(2)}, u32[]{:S(2)}) collective-permute-start(bf16[768,768]{1,0:T(8,128)(2,1)} %broadcast_select_fusion), channel_id=1, source_target_pairs={{0,4},{4,0},{1,5},{5,1},{2,6},{6,2},{3,7},{7,3},{8,12},{12,8},{9,1... | collective-permute-start | bytes 3538952 | tf_op jit(solution)/shard_map/ppermute | solution.py:28
  61.1 1.3 copy-start.1
  66.3 27.1 %all-to-all-start.2 = ((bf16[8,64,768]{2,1,0:T(8,128)(2,1)}), bf16[8,64,768]{2,1,0:T(8,128)(2,1)S(1)}, u32[]{:S(2)}, u32[]{:S(2)}) async-start(bf16[8,64,768]{2,1,0:T(8,128)(2,1)} %bitcast.13), calls=%async_computation.2 | async-start | bytes 1572864 | tf_op jit(solution)/shard_map/all_to_all | solution.py:61
  94.5 18.9 %collective-permute-start.1 = (bf16[64,768]{1,0:T(8,128)(2,1)S(1)}, bf16[64,768]{1,0:T(8,128)(2,1)S(1)}, u32[]{:S(2)}, u32[]{:S(2)}) collective-permute-start(bf16[64,768]{1,0:T(8,128)(2,1)S(1)} %fusion.10), channel_id=1, source_target_pairs={{0,64},{64,128},{128,192},{192,256},{256,320},{320,384},{384,448},... | collective-permute-start | bytes 294920 | tf_op jit(solution)/shard_map/ppermute | solution.py:72
  136.3 7.3 %collective-permute-start.2 = (bf16[512,768]{1,0:T(8,128)(2,1)S(1)}, bf16[512,768]{1,0:T(8,128)(2,1)S(1)}, u32[]{:S(2)}, u32[]{:S(2)}) collective-permute-start(bf16[512,768]{1,0:T(8,128)(2,1)S(1)} %bitcast.45), channel_id=1, source_target_pairs={{0,4},{4,0},{1,5},{5,1},{2,6},{6,2},{3,7},{7,3},{8,12},{12,8},{9,1... | collective-permute-start | bytes 2359304 | tf_op jit(solution)/shard_map/ppermute | solution.py:28

commit v4 on v3

--- a/solution.py
+++ b/solution.py
@@ -1,6 +1,8 @@
 import jax
 import jax.numpy as jnp
 from jax import lax
+from jax.experimental import pallas as pl
+from jax.experimental.pallas import tpu as pltpu
 from jax.sharding import Mesh, PartitionSpec as P
 
 inv_root_two = 0.7071067811865476
@@ -28,14 +30,76 @@
     return lax.ppermute(block, "core", [(0, 1), (1, 0)])
 
 
+def hidden_kernel(parts_ref, stored_ref, copies_ref):
+    ncol = parts_ref.shape[0]
+    sums = parts_ref[0].astype(jnp.float32)
+    for i in range(1, ncol):
+        sums += parts_ref[i].astype(jnp.float32)
+    active = gelu_value(sums[0]).astype(jnp.bfloat16)
+    hidden_grad = (sums[1] * gelu_slope(stored_ref[...].astype(jnp.float32))).astype(jnp.bfloat16)
+    for i in range(ncol):
+        copies_ref[0, i] = active
+        copies_ref[1, i] = hidden_grad
+
+
+def hidden_copies(parts, stored, steps=2):
+    ncol, _, rows, width = parts.shape
+    tile = rows // steps
+    return pl.pallas_call(
+        hidden_kernel,
+        grid=(steps,),
+        in_specs=[
+            pl.BlockSpec((ncol, 2, tile, width), lambda i: (0, 0, i, 0)),
+            pl.BlockSpec((tile, width), lambda i: (i, 0)),
+        ],
+        out_specs=pl.BlockSpec((2, ncol, tile, width), lambda i: (0, 0, i, 0)),
+        out_shape=jax.ShapeDtypeStruct((2, ncol, rows, width), jnp.bfloat16),
+        compiler_params=pltpu.CompilerParams(vmem_limit_bytes=32 << 20),
+    )(parts, stored)
+
+
+def feature_kernel(core_ref, hidden_ref, own_ref, arrived_ref, out_ref):
+    def both(first_weight, second_weight, contract):
+        total = product(hidden_ref[0], first_weight[...], contract)
+        total += product(hidden_ref[1], second_weight[...], contract)
+        out_ref[...] = total.astype(jnp.bfloat16)
+
+    @pl.when(core_ref[0] == 0)
+    def _():
+        both(own_ref, arrived_ref, 0)
+
+    @pl.when(core_ref[0] != 0)
+    def _():
+        both(arrived_ref, own_ref, 1)
+
+
+def feature_terms(core, hidden, own, arrived, steps=2):
+    _, rows, width = hidden.shape
+    tile = rows // steps
+    whole = pl.BlockSpec(own.shape, lambda i, core: (0, 0))
+    return pl.pallas_call(
+        feature_kernel,
+        grid_spec=pltpu.PrefetchScalarGridSpec(
+            num_scalar_prefetch=1,
+            grid=(steps,),
+            in_specs=[
+                pl.BlockSpec((2, tile, width), lambda i, core: (0, i, 0)),
+                whole,
+                whole,
+            ],
+            out_specs=pl.BlockSpec((tile, width), lambda i, core: (i, 0)),
+        ),
+        out_shape=jax.ShapeDtypeStruct((rows, own.shape[0]), jnp.bfloat16),
+        compiler_params=pltpu.CompilerParams(vmem_limit_bytes=32 << 20),
+    )(core.reshape(1), hidden, own, arrived)
+
+
 def body(tokens, up_weight, down_weight, out_grad, saved_hidden):
     inputs, w_up, w_down, upstream = tokens[0], up_weight[0], down_weight[0], out_grad[0]
-    stored = saved_hidden[0].astype(jnp.float32)
     ncol, ny, nz = lax.axis_size("col"), lax.axis_size("y"), lax.axis_size("section")
     core = lax.axis_index("core")
     forward = core == 0
     count = inputs.shape[0]
-    arrived = swapped(jnp.where(forward, w_up, w_down))
 
     def by_col(partial):
         return partial.astype(jnp.bfloat16).reshape(ncol, count // ncol, -1)
@@ -43,29 +107,24 @@
     partials = jnp.stack(
         [by_col(product(inputs, w_up, 0)), by_col(product(upstream, w_down, 1))], axis=1
     )
-    sums = lax.all_to_all(partials, "col", 0, 0, tiled=True).astype(jnp.float32).sum(0)
-    active = gelu_value(sums[0]).astype(jnp.bfloat16)
-    hidden_grad = (sums[1] * gelu_slope(stored)).astype(jnp.bfloat16)
-    copies = jnp.concatenate(
-        [jnp.broadcast_to(part[None], (ncol,) + part.shape) for part in (active, hidden_grad)]
-    )
+    piece = count // ny
+    start = lax.axis_index("y") * piece
+    partials, core, forward, start = lax.optimization_barrier((partials, core, forward, start))
+    parts = lax.all_to_all(partials, "col", 0, 0, tiled=True)
+    own = jnp.where(forward, w_down, w_up)
+    arrived = swapped(jnp.where(forward, w_up, w_down))
+    copies = hidden_copies(parts, saved_hidden[0])
+    copies = copies.reshape((2 * ncol,) + copies.shape[2:])
     gathered = lax.all_to_all(copies, ("core", "col"), 0, 0, tiled=True)
-    first = gathered[:ncol].reshape(count, -1)
-    second = gathered[ncol:].reshape(count, -1)
-    chip_sum = lax.cond(
-        forward,
-        lambda: product(first, w_down, 0) + product(second, arrived, 0),
-        lambda: product(first, arrived, 1) + product(second, w_up, 1),
-    ).astype(jnp.bfloat16)
-    piece = count // ny
-    summed = lax.all_to_all(chip_sum.reshape(ny, piece, -1), "y", 0, 0, tiled=True)
-    summed = summed.astype(jnp.float32).sum(0)
-    start = lax.axis_index("y") * piece
+    chip_sum = feature_terms(core, gathered.reshape(2, count, -1), own, arrived)
     residual = jnp.where(
         forward,
         lax.dynamic_slice_in_dim(inputs, start, piece, 0),
         lax.dynamic_slice_in_dim(upstream, start, piece, 0),
     )
+    chip_sum, residual = lax.optimization_barrier((chip_sum, residual))
+    summed = lax.all_to_all(chip_sum.reshape(ny, piece, -1), "y", 0, 0, tiled=True)
+    summed = summed.astype(jnp.float32).sum(0)
     result = (residual.astype(jnp.float32) + summed).astype(jnp.bfloat16)
     route = [(2 * s, 2 * ((s + 1) % nz)) for s in range(nz)]
     route += [(2 * s + 1, 2 * ((s - 1) % nz) + 1) for s in range(nz)]

time: 146 us -> 141 us (0.966)
  blocking collectives: 40.1 us -> 65.4 us
  waiting for transfers between devices: 43.3 us -> 18.3 us
  Pallas kernels: 0 us -> 4.49 us
  matrix products: 6.12 us -> 3.23 us
  starting transfers between devices: 44.8 us -> 42.4 us
  other arithmetic: 7.73 us -> 5.37 us
  local copies, waits for them, and re-layouts: 2.11 us -> 0.07 us
    all_to_all x1 -> x2, blocking collectives: 17.2 us -> 42.9 us  [the longest x1 25.6 us: body(): lax.all_to_all(chip_sum.reshape(ny, piece, -1), 'y', 0, 0, tiled=True)]
    all_to_all x1 -> x0, waiting for transfers between devices: 23.6 us -> none  [body(): lax.all_to_all(chip_sum.reshape(ny, piece, -1), 'y', 0, 0, tiled=True)]
    pallas_call x0 -> x2, Pallas kernels: none -> 4.49 us  [the longest x1 2.99 us: feature_terms(): pl.pallas_call(feature_kernel, grid_spec=pltpu.PrefetchScalarGridSpec(num...]
    all_to_all x1 -> x0, starting transfers between devices: 3.55 us -> none  [body(): lax.all_to_all(chip_sum.reshape(ny, piece, -1), 'y', 0, 0, tiled=True)]
    all_to_all x1, waiting for transfers between devices: 16.2 us -> 12.7 us  [body(): gathered = lax.all_to_all(copies, ('core', 'col'), 0, 0, tiled=True)]
    dot_general x4 -> x2, matrix products: 6.12 us -> 3.23 us  [product(): lax.dot_general(operand, weight, (((1,), (contract,)), ((), ())), preferr...]
    ppermute x2, waiting for transfers between devices: 1.89 us -> 3.95 us  [swapped(): return lax.ppermute(block, 'core', [(0, 1), (1, 0)])]
    unnamed x8 -> x6, local copies, waits for them, and re-layouts: 1.84 us -> 0.02 us
  transfers between devices with their start and end apart: 5 -> 4, of which waited for: 4 -> 4; matrix products, arithmetic and copies ran while one was open for 2% -> 3% of each run, Pallas kernels for 0% -> 0%
where the time goes in v4:
time: 141 us; the launch traced here: 140 us
  blocking collectives  65.4 us (46%)
  starting transfers between devices  42.4 us (30%)
  waiting for transfers between devices  18.3 us (13%)
  other arithmetic  5.37 us (4%)
  Pallas kernels  4.49 us (3%)
  matrix products  3.23 us (2%)
    all_to_all x1, blocking collectives, body(): lax.all_to_all(chip_sum.reshape(ny, piece, -1), 'y', 0, 0, tiled=True)  25.6 us
    all_to_all x1, blocking collectives, body(): mine = lax.all_to_all(pieces, 'y', 0, 0, tiled=True).reshape(count, -1)  22.5 us
    ppermute x1, starting transfers between devices, body(): moved = lax.ppermute(result, ('section', 'core'), route)  17.9 us
    all_to_all x1, blocking collectives, body(): parts = lax.all_to_all(partials, 'col', 0, 0, tiled=True)  17.3 us
    all_to_all x1, starting transfers between devices, body(): gathered = lax.all_to_all(copies, ('core', 'col'), 0, 0, tiled=True)  16.6 us
    all_to_all x1, waiting for transfers between devices, body(): gathered = lax.all_to_all(copies, ('core', 'col'), 0, 0, tiled=True)  12.7 us
    ppermute x2, starting transfers between devices, swapped(): return lax.ppermute(block, 'core', [(0, 1), (1, 0)])  7.86 us
    ppermute x2, waiting for transfers between devices, swapped(): return lax.ppermute(block, 'core', [(0, 1), (1, 0)])  3.95 us
  transfers between devices with their start and end apart: 4, of which 4 were waited for; matrix products, arithmetic and copies ran while one was open for 3% of the time, Pallas kernels for 0%

profile of v4, /device:TPU:1, one launch (start us, length us, event | category | flops | bytes accessed | tf_op | source)
XLA Modules:
  0.0 140.1 jit_solution(7732605619492181972)
XLA Ops:
  0.6 0.0 copy-start.1
  0.6 0.0 copy-start.2
  0.7 2.5 %convolution_convert_fusion = bf16[512,768]{1,0:T(8,128)(2,1)S(1)} fusion(bf16[1,768,768]{2,1,0:T(8,128)(2,1)} %param.7, bf16[1,512,768]{2,1,0:T(8,128)(2,1)} %param.8), kind=kOutput, calls=%fused_computation.2 | convolution fusion | flops 604372992 | bytes 2752512 | tf_op jit(solution)/shard_map/dot_general | solution.py:24
  3.1 0.8 convolution_convert_fusion.1
  3.9 0.1 pad_maximum_fusion
  4.1 0.0 copy-start
  4.1 17.3 %all_to_all.20.parts_ref = bf16[4,2,128,768]{3,2,1,0:T(8,128)(2,1)S(1)} all-to-all(bf16[4,2,128,768]{3,2,1,0:T(8,128)(2,1)S(1)} %pad_maximum_fusion), channel_id=1, replica_groups=mesh['section'=16,'y'=8,'core'=2,'col'=4] {'col'}, dimensions={0} | all-to-all | bytes 3145728 | tf_op jit(solution)/shard_map/all_to_all | solution.py:113
  21.4 1.5 %shard_map.68 = bf16[2,4,128,768]{3,2,1,0:T(8,128)(2,1)} custom-call(bf16[4,2,128,768]{3,2,1,0:T(8,128)(2,1)S(1)} %all_to_all.20.parts_ref, bf16[128,768]{1,0:T(8,128)(2,1)S(1)} %bitcast.34), custom_call_target="tpu_custom_call" | custom-call | tf_op jit(solution)/shard_map/pallas_call | solution.py:48
  22.9 16.6 %all-to-all-start.1 = ((bf16[8,128,768]{2,1,0:T(8,128)(2,1)}), bf16[8,128,768]{2,1,0:T(8,128)(2,1)S(1)}, u32[]{:S(2)}, u32[]{:S(2)}) async-start(bf16[8,128,768]{2,1,0:T(8,128)(2,1)} %bitcast.8), calls=%async_computation.1 | async-start | bytes 3145728 | tf_op jit(solution)/shard_map/all_to_all | solution.py:118
  39.5 2.8 %bitcast_select_fusion = (bf16[768,768]{1,0:T(8,128)(2,1)}, bf16[768,768]{1,0:T(8,128)(2,1)S(1)}) fusion(bf16[1,768,768]{2,1,0:T(8,128)(2,1)} %param.7, bf16[1,768,768]{2,1,0:T(8,128)(2,1)} %param.6, pred[]{:T(512)S(6)} %eq.3), kind=kLoop, calls=%fused_computation.4 | loop fusion | flops 1179648 | bytes 4718593 | tf_op jit(solution)/shard_map/jit(_where)/select_n | solution.py:115
  42.3 2.0 %collective-permute-start = (bf16[768,768]{1,0:T(8,128)(2,1)}, bf16[768,768]{1,0:T(8,128)(2,1)}, u32[]{:S(2)}, u32[]{:S(2)}) collective-permute-start(bf16[768,768]{1,0:T(8,128)(2,1)} %get-tuple-element.14), channel_id=1, source_target_pairs={{0,4},{4,0},{1,5},{5,1},{2,6},{6,2},{3,7},{7,3},{8,12},{12,8},{9,1... | collective-permute-start | bytes 3538952 | tf_op jit(solution)/shard_map/ppermute | solution.py:30
  44.3 1.0 select_bitcast_fusion.2
  45.3 2.1 %collective-permute-done.arrived_ref = bf16[768,768]{1,0:T(8,128)(2,1)} collective-permute-done((bf16[768,768]{1,0:T(8,128)(2,1)}, bf16[768,768]{1,0:T(8,128)(2,1)}, u32[]{:S(2)}, u32[]{:S(2)}) %collective-permute-start) | collective-permute-done | bytes 1179680 | tf_op jit(solution)/shard_map/ppermute | solution.py:30
  47.4 12.7 %all-to-all-done.1 = bf16[8,128,768]{2,1,0:T(8,128)(2,1)S(1)} async-done(((bf16[8,128,768]{2,1,0:T(8,128)(2,1)}), bf16[8,128,768]{2,1,0:T(8,128)(2,1)S(1)}, u32[]{:S(2)}, u32[]{:S(2)}) %all-to-all-start.1) | async-done | bytes 1572896 | tf_op jit(solution)/shard_map/all_to_all | solution.py:118
  60.1 3.0 %shard_map.69 = bf16[512,768]{1,0:T(8,128)(2,1)S(1)} custom-call(s32[1]{0:T(128)} %bitcast.6.core_ref, bf16[2,512,768]{2,1,0:T(8,128)(2,1)S(1)} %bitcast.32, bf16[768,768]{1,0:T(8,128)(2,1)S(1)} %get-tuple-element.15.own_ref, bf16[768,768]{1,0:T(8,128)(2,1)} %collective-permute-done.arrived_ref), custom_call_target="tpu_custom_call" | custom-call | tf_op jit(solution)/shard_map/pallas_call | solution.py:80
  63.1 25.6 %all_to_all.21 = bf16[8,64,768]{2,1,0:T(8,128)(2,1)S(1)} all-to-all(bf16[8,64,768]{2,1,0:T(8,128)(2,1)S(1)} %bitcast.33), channel_id=1, replica_groups=mesh['section'=16,'y'=8,'core'=2,'col'=4] {'y'}, dimensions={0} | all-to-all | bytes 1572864 | tf_op jit(solution)/shard_map/all_to_all | solution.py:126
  88.7 0.1 convert_reduce_fusion
  88.9 17.9 %collective-permute-start.1 = (bf16[64,768]{1,0:T(8,128)(2,1)S(1)}, bf16[64,768]{1,0:T(8,128)(2,1)S(1)}, u32[]{:S(2)}, u32[]{:S(2)}) collective-permute-start(bf16[64,768]{1,0:T(8,128)(2,1)S(1)} %add_convert_fusion), channel_id=1, source_target_pairs={{0,64},{64,128},{128,192},{192,256},{256,320},{320,384},{384,448},... | collective-permute-start | bytes 294920 | tf_op jit(solution)/shard_map/ppermute | solution.py:131
  106.8 1.6 %collective-permute-done.1 = bf16[64,768]{1,0:T(8,128)(2,1)S(1)} collective-permute-done((bf16[64,768]{1,0:T(8,128)(2,1)S(1)}, bf16[64,768]{1,0:T(8,128)(2,1)S(1)}, u32[]{:S(2)}, u32[]{:S(2)}) %collective-permute-start.1) | collective-permute-done | bytes 98336 | tf_op jit(solution)/shard_map/ppermute | solution.py:131
  108.4 0.1 broadcast_in_dim.12
  108.5 22.5 %all_to_all.22 = bf16[8,64,768]{2,1,0:T(8,128)(2,1)S(1)} all-to-all(bf16[8,64,768]{2,1,0:T(8,128)(2,1)S(1)} %broadcast_in_dim.12), channel_id=1, replica_groups=mesh['section'=16,'y'=8,'core'=2,'col'=4] {'y'}, dimensions={0} | all-to-all | bytes 1572864 | tf_op jit(solution)/shard_map/all_to_all | solution.py:133
  131.0 5.9 %collective-permute-start.2 = (bf16[512,768]{1,0:T(8,128)(2,1)S(1)}, bf16[512,768]{1,0:T(8,128)(2,1)S(1)}, u32[]{:S(2)}, u32[]{:S(2)}) collective-permute-start(bf16[512,768]{1,0:T(8,128)(2,1)S(1)} %bitcast.35), channel_id=1, source_target_pairs={{0,4},{4,0},{1,5},{5,1},{2,6},{6,2},{3,7},{7,3},{8,12},{12,8},{9,1... | collective-permute-start | bytes 2359304 | tf_op jit(solution)/shard_map/ppermute | solution.py:30
  136.9 1.9 %collective-permute-done.2 = bf16[512,768]{1,0:T(8,128)(2,1)S(1)} collective-permute-done((bf16[512,768]{1,0:T(8,128)(2,1)S(1)}, bf16[512,768]{1,0:T(8,128)(2,1)S(1)}, u32[]{:S(2)}, u32[]{:S(2)}) %collective-permute-start.2) | collective-permute-done | bytes 786464 | tf_op jit(solution)/shard_map/ppermute | solution.py:30
  138.8 1.3 select_bitcast_fusion
  (4 shorter events, 0.0 us)
Async XLA Ops:
  0.6 2.5 %copy-start.1 = (bf16[1,768,768]{2,1,0:T(8,128)(2,1)S(1)}, bf16[1,768,768]{2,1,0:T(8,128)(2,1)}, u32[]{:S(2)}) copy-start(bf16[1,768,768]{2,1,0:T(8,128)(2,1)} %param.6) | copy-start | bytes 3538948
  0.6 2.5 %copy-start.2 = (bf16[1,512,768]{2,1,0:T(8,128)(2,1)S(1)}, bf16[1,512,768]{2,1,0:T(8,128)(2,1)}, u32[]{:S(2)}) copy-start(bf16[1,512,768]{2,1,0:T(8,128)(2,1)} %param.5) | copy-start | bytes 2359300
  4.1 17.3 %copy-start = (bf16[1,128,768]{2,1,0:T(8,128)(2,1)S(1)}, bf16[1,128,768]{2,1,0:T(8,128)(2,1)}, u32[]{:S(2)}) copy-start(bf16[1,128,768]{2,1,0:T(8,128)(2,1)} %param.9) | copy-start | bytes 589828
  22.9 37.2 %all-to-all-start.1 = ((bf16[8,128,768]{2,1,0:T(8,128)(2,1)}), bf16[8,128,768]{2,1,0:T(8,128)(2,1)S(1)}, u32[]{:S(2)}, u32[]{:S(2)}) async-start(bf16[8,128,768]{2,1,0:T(8,128)(2,1)} %bitcast.8), calls=%async_computation.1 | async-start | bytes 3145728 | tf_op jit(solution)/shard_map/all_to_all | solution.py:118
  42.3 5.1 %collective-permute-start = (bf16[768,768]{1,0:T(8,128)(2,1)}, bf16[768,768]{1,0:T(8,128)(2,1)}, u32[]{:S(2)}, u32[]{:S(2)}) collective-permute-start(bf16[768,768]{1,0:T(8,128)(2,1)} %get-tuple-element.14), channel_id=1, source_target_pairs={{0,4},{4,0},{1,5},{5,1},{2,6},{6,2},{3,7},{7,3},{8,12},{12,8},{9,1... | collective-permute-start | bytes 3538952 | tf_op jit(solution)/shard_map/ppermute | solution.py:30
  88.9 19.6 %collective-permute-start.1 = (bf16[64,768]{1,0:T(8,128)(2,1)S(1)}, bf16[64,768]{1,0:T(8,128)(2,1)S(1)}, u32[]{:S(2)}, u32[]{:S(2)}) collective-permute-start(bf16[64,768]{1,0:T(8,128)(2,1)S(1)} %add_convert_fusion), channel_id=1, source_target_pairs={{0,64},{64,128},{128,192},{192,256},{256,320},{320,384},{384,448},... | collective-permute-start | bytes 294920 | tf_op jit(solution)/shard_map/ppermute | solution.py:131
  131.0 7.8 %collective-permute-start.2 = (bf16[512,768]{1,0:T(8,128)(2,1)S(1)}, bf16[512,768]{1,0:T(8,128)(2,1)S(1)}, u32[]{:S(2)}, u32[]{:S(2)}) collective-permute-start(bf16[512,768]{1,0:T(8,128)(2,1)S(1)} %bitcast.35), channel_id=1, source_target_pairs={{0,4},{4,0},{1,5},{5,1},{2,6},{6,2},{3,7},{7,3},{8,12},{12,8},{9,1... | collective-permute-start | bytes 2359304 | tf_op jit(solution)/shard_map/ppermute | solution.py:30

commit v5 on v4

--- a/solution.py
+++ b/solution.py
@@ -30,32 +30,58 @@
     return lax.ppermute(block, "core", [(0, 1), (1, 0)])
 
 
-def hidden_kernel(parts_ref, stored_ref, copies_ref):
-    ncol = parts_ref.shape[0]
-    sums = parts_ref[0].astype(jnp.float32)
-    for i in range(1, ncol):
-        sums += parts_ref[i].astype(jnp.float32)
+def partial_kernel(chunks_ref, inputs_ref, upstream_ref, up_ref, down_ref, *out_refs):
+    terms = [
+        product(inputs_ref[...], up_ref[...], 0).astype(jnp.bfloat16),
+        product(upstream_ref[...], down_ref[...], 1).astype(jnp.bfloat16),
+    ]
+    for step, out_ref in enumerate(out_refs):
+
+        @pl.when(pl.program_id(0) == step)
+        def _():
+            out_ref[0], out_ref[1] = terms
+
+
+def partial_sums(chunks, count, inputs, upstream, w_up, w_down, rows):
+    width = w_up.shape[1]
+    chunk = pl.BlockSpec((rows, inputs.shape[1]), lambda i, chunks: (chunks[i], 0))
+    whole = pl.BlockSpec(w_up.shape, lambda i, chunks: (0, 0))
+    kept = pl.BlockSpec((2, rows, width), lambda i, chunks: (0, 0, 0))
+    return pl.pallas_call(
+        partial_kernel,
+        grid_spec=pltpu.PrefetchScalarGridSpec(
+            num_scalar_prefetch=1,
+            grid=(count,),
+            in_specs=[chunk, chunk, whole, whole],
+            out_specs=[kept] * count,
+        ),
+        out_shape=[jax.ShapeDtypeStruct((2, rows, width), jnp.bfloat16)] * count,
+        compiler_params=pltpu.CompilerParams(vmem_limit_bytes=58 << 20),
+    )(chunks, inputs, upstream, w_up, w_down)
+
+
+def hidden_kernel(*refs):
+    *part_refs, stored_ref, copies_ref = refs
+    sums = sum(part_ref[...].astype(jnp.float32) for part_ref in part_refs)
     active = gelu_value(sums[0]).astype(jnp.bfloat16)
     hidden_grad = (sums[1] * gelu_slope(stored_ref[...].astype(jnp.float32))).astype(jnp.bfloat16)
-    for i in range(ncol):
+    for i in range(copies_ref.shape[1]):
         copies_ref[0, i] = active
         copies_ref[1, i] = hidden_grad
 
 
 def hidden_copies(parts, stored, steps=2):
-    ncol, _, rows, width = parts.shape
+    _, rows, width = parts[0].shape
     tile = rows // steps
     return pl.pallas_call(
         hidden_kernel,
         grid=(steps,),
-        in_specs=[
-            pl.BlockSpec((ncol, 2, tile, width), lambda i: (0, 0, i, 0)),
-            pl.BlockSpec((tile, width), lambda i: (i, 0)),
-        ],
-        out_specs=pl.BlockSpec((2, ncol, tile, width), lambda i: (0, 0, i, 0)),
-        out_shape=jax.ShapeDtypeStruct((2, ncol, rows, width), jnp.bfloat16),
+        in_specs=[pl.BlockSpec((2, tile, width), lambda i: (0, i, 0))] * len(parts)
+        + [pl.BlockSpec((tile, width), lambda i: (i, 0))],
+        out_specs=pl.BlockSpec((2, len(parts), tile, width), lambda i: (0, 0, i, 0)),
+        out_shape=jax.ShapeDtypeStruct((2, len(parts), rows, width), jnp.bfloat16),
         compiler_params=pltpu.CompilerParams(vmem_limit_bytes=32 << 20),
-    )(parts, stored)
+    )(*parts, stored)
 
 
 def feature_kernel(core_ref, hidden_ref, own_ref, arrived_ref, out_ref):
@@ -100,28 +126,29 @@
     core = lax.axis_index("core")
     forward = core == 0
     count = inputs.shape[0]
-
-    def by_col(partial):
-        return partial.astype(jnp.bfloat16).reshape(ncol, count // ncol, -1)
-
-    partials = jnp.stack(
-        [by_col(product(inputs, w_up, 0)), by_col(product(upstream, w_down, 1))], axis=1
-    )
     piece = count // ny
     start = lax.axis_index("y") * piece
-    partials, core, forward, start = lax.optimization_barrier((partials, core, forward, start))
-    parts = lax.all_to_all(partials, "col", 0, 0, tiled=True)
+    col = lax.axis_index("col")
+    operands = (inputs, upstream, w_up, w_down, count // ncol)
+    reach = sorted(range(1, ncol), key=lambda d: -min(d, ncol - d))
+    chunks = jnp.stack([(col + d) % ncol for d in reach] + [col])
+    terms = partial_sums(chunks, ncol, *operands)
+    parts = [terms[-1]] + [
+        lax.ppermute(term, "col", [(i, (i + d) % ncol) for i in range(ncol)])
+        for d, term in zip(reach, terms)
+    ]
+    copies = hidden_copies(parts, saved_hidden[0])
+    copies = copies.reshape((2 * ncol,) + copies.shape[2:])
+    copies, w_up, w_down = lax.optimization_barrier((copies, w_up, w_down))
     own = jnp.where(forward, w_down, w_up)
     arrived = swapped(jnp.where(forward, w_up, w_down))
-    copies = hidden_copies(parts, saved_hidden[0])
-    copies = copies.reshape((2 * ncol,) + copies.shape[2:])
-    gathered = lax.all_to_all(copies, ("core", "col"), 0, 0, tiled=True)
-    chip_sum = feature_terms(core, gathered.reshape(2, count, -1), own, arrived)
     residual = jnp.where(
         forward,
         lax.dynamic_slice_in_dim(inputs, start, piece, 0),
         lax.dynamic_slice_in_dim(upstream, start, piece, 0),
     )
+    gathered = lax.all_to_all(copies, ("core", "col"), 0, 0, tiled=True)
+    chip_sum = feature_terms(core, gathered.reshape(2, count, -1), own, arrived)
     chip_sum, residual = lax.optimization_barrier((chip_sum, residual))
     summed = lax.all_to_all(chip_sum.reshape(ny, piece, -1), "y", 0, 0, tiled=True)
     summed = summed.astype(jnp.float32).sum(0)

time: 141 us -> 145 us (1.028)
  blocking collectives: 65.4 us -> 48.5 us
  starting transfers between devices: 42.4 us -> 50.4 us
  waiting for transfers between devices: 18.3 us -> 26 us
  Pallas kernels: 4.49 us -> 11.5 us
  matrix products: 3.23 us -> 0 us
    all_to_all x1 -> x0, blocking collectives: 17.3 us -> none  [body(): parts = lax.all_to_all(partials, 'col', 0, 0, tiled=True)]
    ppermute x0 -> x3, starting transfers between devices: none -> 12 us  [body(): lax.ppermute(term, 'col', [(i, (i + d) % ncol) for i in range(ncol)])]
    ppermute x0 -> x3, waiting for transfers between devices: none -> 7.57 us  [body(): lax.ppermute(term, 'col', [(i, (i + d) % ncol) for i in range(ncol)])]
    pallas_call x1 -> x2, Pallas kernels: 1.5 us -> 8.52 us  [the longest x1 7.01 us: partial_sums(): pl.pallas_call(partial_kernel, grid_spec=pltpu.PrefetchScalarGridSpec(num...]
    dot_general x2 -> x0, matrix products: 3.23 us -> none  [product(): lax.dot_general(operand, weight, (((1,), (contract,)), ((), ())), preferr...]
    all_to_all x1, starting transfers between devices: 16.6 us -> 14 us  [body(): gathered = lax.all_to_all(copies, ('core', 'col'), 0, 0, tiled=True)]
  transfers between devices with their start and end apart: 4 -> 7, of which waited for: 4 -> 6; matrix products, arithmetic and copies ran while one was open for 3% -> 3% of each run, Pallas kernels for 0% -> 0%
where the time goes in v5:
time: 145 us; the launch traced here: 144 us
  starting transfers between devices  50.4 us (35%)
  blocking collectives  48.5 us (33%)
  waiting for transfers between devices  26 us (18%)
  Pallas kernels  11.5 us (8%)
  other arithmetic  5.8 us (4%)
    all_to_all x1, blocking collectives, body(): lax.all_to_all(chip_sum.reshape(ny, piece, -1), 'y', 0, 0, tiled=True)  26 us
    all_to_all x1, blocking collectives, body(): mine = lax.all_to_all(pieces, 'y', 0, 0, tiled=True).reshape(count, -1)  22.5 us
    ppermute x1, starting transfers between devices, body(): moved = lax.ppermute(result, ('section', 'core'), route)  16.6 us
    all_to_all x1, starting transfers between devices, body(): gathered = lax.all_to_all(copies, ('core', 'col'), 0, 0, tiled=True)  14 us
    all_to_all x1, waiting for transfers between devices, body(): gathered = lax.all_to_all(copies, ('core', 'col'), 0, 0, tiled=True)  12.7 us
    ppermute x3, starting transfers between devices, body(): lax.ppermute(term, 'col', [(i, (i + d) % ncol) for i in range(ncol)])  12 us
    ppermute x2, starting transfers between devices, swapped(): return lax.ppermute(block, 'core', [(0, 1), (1, 0)])  7.78 us
    ppermute x3, waiting for transfers between devices, body(): lax.ppermute(term, 'col', [(i, (i + d) % ncol) for i in range(ncol)])  7.57 us
  transfers between devices with their start and end apart: 7, of which 6 were waited for; matrix products, arithmetic and copies ran while one was open for 3% of the time, Pallas kernels for 0%

profile of v5, /device:TPU:1, one launch (start us, length us, event | category | flops | bytes accessed | tf_op | source)
XLA Modules:
  0.0 144.0 jit_solution(2067968324284160938)
XLA Ops:
  0.7 0.6 pad_add_fusion.chunks_ref
  1.3 7.0 %shard_map.68 = (bf16[2,128,768]{2,1,0:T(8,128)(2,1)}, bf16[2,128,768]{2,1,0:T(8,128)(2,1)}, bf16[2,128,768]{2,1,0:T(8,128)(2,1)}, bf16[2,128,768]{2,1,0:T(8,128)(2,1)}) custom-call(s32[4]{0:T(128)} %pad_add_fusion.chunks_ref, bf16[512,768]{1,0:T(8,128)(2,1)} %bitcast.30, bf16[512,768]{1,0:T(8,128)(2,1)} %bitcast.31, bf16[768,768]{1,0:T(8,128)(2,1)} %bitcast.25, ...), custom_call_target="tpu_custom_call" | custom-call | tf_op jit(solution)/shard_map/pallas_call | solution.py:50
  8.3 5.5 %collective-permute-start = (bf16[2,128,768]{2,1,0:T(8,128)(2,1)}, bf16[2,128,768]{2,1,0:T(8,128)(2,1)S(1)}, u32[]{:S(2)}, u32[]{:S(2)}) collective-permute-start(bf16[2,128,768]{2,1,0:T(8,128)(2,1)} %get-tuple-element.12), channel_id=1, source_target_pairs={{0,2},{1,3},{2,0},{3,1},{4,6},{5,7},{6,4},{7,5},{8,10},{9,11},{10,... | collective-permute-start | bytes 1179656 | tf_op jit(solution)/shard_map/ppermute | solution.py:137
  13.8 2.2 %collective-permute-start.1 = (bf16[2,128,768]{2,1,0:T(8,128)(2,1)}, bf16[2,128,768]{2,1,0:T(8,128)(2,1)S(1)}, u32[]{:S(2)}, u32[]{:S(2)}) collective-permute-start(bf16[2,128,768]{2,1,0:T(8,128)(2,1)} %get-tuple-element.13), channel_id=1, source_target_pairs={{0,1},{1,2},{2,3},{3,0},{4,5},{5,6},{6,7},{7,4},{8,9},{9,10},{10,1... | collective-permute-start | bytes 1179656 | tf_op jit(solution)/shard_map/ppermute | solution.py:137
  16.0 4.3 %collective-permute-start.2 = (bf16[2,128,768]{2,1,0:T(8,128)(2,1)}, bf16[2,128,768]{2,1,0:T(8,128)(2,1)S(1)}, u32[]{:S(2)}, u32[]{:S(2)}) collective-permute-start(bf16[2,128,768]{2,1,0:T(8,128)(2,1)} %get-tuple-element.14), channel_id=1, source_target_pairs={{0,3},{1,0},{2,1},{3,2},{4,7},{5,4},{6,5},{7,6},{8,11},{9,8},{10,9... | collective-permute-start | bytes 1179656 | tf_op jit(solution)/shard_map/ppermute | solution.py:137
  20.3 3.4 %collective-permute-done.1.refs_2_ = bf16[2,128,768]{2,1,0:T(8,128)(2,1)S(1)} collective-permute-done((bf16[2,128,768]{2,1,0:T(8,128)(2,1)}, bf16[2,128,768]{2,1,0:T(8,128)(2,1)S(1)}, u32[]{:S(2)}, u32[]{:S(2)}) %collective-permute-start.1) | collective-permute-done | bytes 393248 | tf_op jit(solution)/shard_map/ppermute | solution.py:137
  23.7 4.1 %collective-permute-done.2.refs_3_ = bf16[2,128,768]{2,1,0:T(8,128)(2,1)S(1)} collective-permute-done((bf16[2,128,768]{2,1,0:T(8,128)(2,1)}, bf16[2,128,768]{2,1,0:T(8,128)(2,1)S(1)}, u32[]{:S(2)}, u32[]{:S(2)}) %collective-permute-start.2) | collective-permute-done | bytes 393248 | tf_op jit(solution)/shard_map/ppermute | solution.py:137
  27.9 1.0 copy-done
  28.9 1.5 %shard_map.69 = bf16[2,4,128,768]{3,2,1,0:T(8,128)(2,1)} custom-call(bf16[2,128,768]{2,1,0:T(8,128)(2,1)S(1)} %copy-done, bf16[2,128,768]{2,1,0:T(8,128)(2,1)S(1)} %collective-permute-done.refs_1_, bf16[2,128,768]{2,1,0:T(8,128)(2,1)S(1)} %collective-permute-done.1.refs_2_, bf16[2,128,768]{2,1,0:T(8,128)(2,1)S(1)} %collective-permute-done.2.refs_3_, ...), custom_call_target="tpu_custom_call" | custom-call | tf_op jit(solution)/shard_map/pallas_call | solution.py:76
  30.4 14.0 %all-to-all-start = ((bf16[8,128,768]{2,1,0:T(8,128)(2,1)}), bf16[8,128,768]{2,1,0:T(8,128)(2,1)S(1)}, u32[]{:S(2)}, u32[]{:S(2)}) async-start(bf16[8,128,768]{2,1,0:T(8,128)(2,1)} %bitcast.10), calls=%async_computation | async-start | bytes 3145728 | tf_op jit(solution)/shard_map/all_to_all | solution.py:150
  44.4 2.8 %broadcast_select_fusion = (bf16[768,768]{1,0:T(8,128)(2,1)}, bf16[768,768]{1,0:T(8,128)(2,1)S(1)}) fusion(bf16[768,768]{1,0:T(8,128)(2,1)} %bitcast.26, bf16[768,768]{1,0:T(8,128)(2,1)} %bitcast.28, pred[]{:T(512)S(6)} %eq.7), kind=kLoop, calls=%fused_computation.1 | loop fusion | flops 1179648 | bytes 4718593 | tf_op jit(solution)/shard_map/jit(_where)/select_n | solution.py:144
  47.2 1.9 %collective-permute-start.3 = (bf16[768,768]{1,0:T(8,128)(2,1)}, bf16[768,768]{1,0:T(8,128)(2,1)}, u32[]{:S(2)}, u32[]{:S(2)}) collective-permute-start(bf16[768,768]{1,0:T(8,128)(2,1)} %get-tuple-element.20), channel_id=1, source_target_pairs={{0,4},{4,0},{1,5},{5,1},{2,6},{6,2},{3,7},{7,3},{8,12},{12,8},{9,1... | collective-permute-start | bytes 3538952 | tf_op jit(solution)/shard_map/ppermute | solution.py:30
  49.1 1.0 select_bitcast_fusion.2
  50.1 2.2 %collective-permute-done.3.arrived_ref = bf16[768,768]{1,0:T(8,128)(2,1)} collective-permute-done((bf16[768,768]{1,0:T(8,128)(2,1)}, bf16[768,768]{1,0:T(8,128)(2,1)}, u32[]{:S(2)}, u32[]{:S(2)}) %collective-permute-start.3) | collective-permute-done | bytes 1179680 | tf_op jit(solution)/shard_map/ppermute | solution.py:30
  52.3 12.7 %all-to-all-done = bf16[8,128,768]{2,1,0:T(8,128)(2,1)S(1)} async-done(((bf16[8,128,768]{2,1,0:T(8,128)(2,1)}), bf16[8,128,768]{2,1,0:T(8,128)(2,1)S(1)}, u32[]{:S(2)}, u32[]{:S(2)}) %all-to-all-start) | async-done | bytes 1572896 | tf_op jit(solution)/shard_map/all_to_all | solution.py:150
  65.0 3.0 %shard_map.70 = bf16[512,768]{1,0:T(8,128)(2,1)S(1)} custom-call(s32[1]{0:T(128)} %bitcast.core_ref, bf16[2,512,768]{2,1,0:T(8,128)(2,1)S(1)} %bitcast.22, bf16[768,768]{1,0:T(8,128)(2,1)S(1)} %get-tuple-element.21.own_ref, bf16[768,768]{1,0:T(8,128)(2,1)} %collective-permute-done.3.arrived_ref), custom_call_target="tpu_custom_call" | custom-call | tf_op jit(solution)/shard_map/pallas_call | solution.py:106
  68.0 26.0 %all_to_all.15 = bf16[8,64,768]{2,1,0:T(8,128)(2,1)S(1)} all-to-all(bf16[8,64,768]{2,1,0:T(8,128)(2,1)S(1)} %bitcast.23), channel_id=1, replica_groups=mesh['section'=16,'y'=8,'core'=2,'col'=4] {'y'}, dimensions={0} | all-to-all | bytes 1572864 | tf_op jit(solution)/shard_map/all_to_all | solution.py:153
  94.0 0.1 convert_reduce_fusion
  94.1 16.6 %collective-permute-start.4 = (bf16[64,768]{1,0:T(8,128)(2,1)S(1)}, bf16[64,768]{1,0:T(8,128)(2,1)S(1)}, u32[]{:S(2)}, u32[]{:S(2)}) collective-permute-start(bf16[64,768]{1,0:T(8,128)(2,1)S(1)} %add_convert_fusion), channel_id=1, source_target_pairs={{0,64},{64,128},{128,192},{192,256},{256,320},{320,384},{384,448},... | collective-permute-start | bytes 294920 | tf_op jit(solution)/shard_map/ppermute | solution.py:158
  110.8 1.6 %collective-permute-done.4 = bf16[64,768]{1,0:T(8,128)(2,1)S(1)} collective-permute-done((bf16[64,768]{1,0:T(8,128)(2,1)S(1)}, bf16[64,768]{1,0:T(8,128)(2,1)S(1)}, u32[]{:S(2)}, u32[]{:S(2)}) %collective-permute-start.4) | collective-permute-done | bytes 98336 | tf_op jit(solution)/shard_map/ppermute | solution.py:158
  112.4 22.5 %all_to_all.16 = bf16[8,64,768]{2,1,0:T(8,128)(2,1)S(1)} all-to-all(bf16[8,64,768]{2,1,0:T(8,128)(2,1)S(1)} %broadcast_in_dim.12), channel_id=1, replica_groups=mesh['section'=16,'y'=8,'core'=2,'col'=4] {'y'}, dimensions={0} | all-to-all | bytes 1572864 | tf_op jit(solution)/shard_map/all_to_all | solution.py:160
  134.9 5.9 %collective-permute-start.5 = (bf16[512,768]{1,0:T(8,128)(2,1)S(1)}, bf16[512,768]{1,0:T(8,128)(2,1)S(1)}, u32[]{:S(2)}, u32[]{:S(2)}) collective-permute-start(bf16[512,768]{1,0:T(8,128)(2,1)S(1)} %bitcast.29), channel_id=1, source_target_pairs={{0,4},{4,0},{1,5},{5,1},{2,6},{6,2},{3,7},{7,3},{8,12},{12,8},{9,1... | collective-permute-start | bytes 2359304 | tf_op jit(solution)/shard_map/ppermute | solution.py:30
  140.8 1.9 %collective-permute-done.5 = bf16[512,768]{1,0:T(8,128)(2,1)S(1)} collective-permute-done((bf16[512,768]{1,0:T(8,128)(2,1)S(1)}, bf16[512,768]{1,0:T(8,128)(2,1)S(1)}, u32[]{:S(2)}, u32[]{:S(2)}) %collective-permute-start.5) | collective-permute-done | bytes 786464 | tf_op jit(solution)/shard_map/ppermute | solution.py:30
  142.7 1.3 select_bitcast_fusion
  (6 shorter events, 0.1 us)
Async XLA Ops:
  1.3 26.6 %copy-start.1 = (bf16[1,128,768]{2,1,0:T(8,128)(2,1)S(1)}, bf16[1,128,768]{2,1,0:T(8,128)(2,1)}, u32[]{:S(2)}) copy-start(bf16[1,128,768]{2,1,0:T(8,128)(2,1)} %param.9) | copy-start | bytes 589828
  8.3 12.0 %collective-permute-start = (bf16[2,128,768]{2,1,0:T(8,128)(2,1)}, bf16[2,128,768]{2,1,0:T(8,128)(2,1)S(1)}, u32[]{:S(2)}, u32[]{:S(2)}) collective-permute-start(bf16[2,128,768]{2,1,0:T(8,128)(2,1)} %get-tuple-element.12), channel_id=1, source_target_pairs={{0,2},{1,3},{2,0},{3,1},{4,6},{5,7},{6,4},{7,5},{8,10},{9,11},{10,... | collective-permute-start | bytes 1179656 | tf_op jit(solution)/shard_map/ppermute | solution.py:137
  13.8 9.9 %collective-permute-start.1 = (bf16[2,128,768]{2,1,0:T(8,128)(2,1)}, bf16[2,128,768]{2,1,0:T(8,128)(2,1)S(1)}, u32[]{:S(2)}, u32[]{:S(2)}) collective-permute-start(bf16[2,128,768]{2,1,0:T(8,128)(2,1)} %get-tuple-element.13), channel_id=1, source_target_pairs={{0,1},{1,2},{2,3},{3,0},{4,5},{5,6},{6,7},{7,4},{8,9},{9,10},{10,1... | collective-permute-start | bytes 1179656 | tf_op jit(solution)/shard_map/ppermute | solution.py:137
  16.0 11.9 %collective-permute-start.2 = (bf16[2,128,768]{2,1,0:T(8,128)(2,1)}, bf16[2,128,768]{2,1,0:T(8,128)(2,1)S(1)}, u32[]{:S(2)}, u32[]{:S(2)}) collective-permute-start(bf16[2,128,768]{2,1,0:T(8,128)(2,1)} %get-tuple-element.14), channel_id=1, source_target_pairs={{0,3},{1,0},{2,1},{3,2},{4,7},{5,4},{6,5},{7,6},{8,11},{9,8},{10,9... | collective-permute-start | bytes 1179656 | tf_op jit(solution)/shard_map/ppermute | solution.py:137
  27.9 1.0 copy-start
  30.4 34.6 %all-to-all-start = ((bf16[8,128,768]{2,1,0:T(8,128)(2,1)}), bf16[8,128,768]{2,1,0:T(8,128)(2,1)S(1)}, u32[]{:S(2)}, u32[]{:S(2)}) async-start(bf16[8,128,768]{2,1,0:T(8,128)(2,1)} %bitcast.10), calls=%async_computation | async-start | bytes 3145728 | tf_op jit(solution)/shard_map/all_to_all | solution.py:150
  47.2 5.1 %collective-permute-start.3 = (bf16[768,768]{1,0:T(8,128)(2,1)}, bf16[768,768]{1,0:T(8,128)(2,1)}, u32[]{:S(2)}, u32[]{:S(2)}) collective-permute-start(bf16[768,768]{1,0:T(8,128)(2,1)} %get-tuple-element.20), channel_id=1, source_target_pairs={{0,4},{4,0},{1,5},{5,1},{2,6},{6,2},{3,7},{7,3},{8,12},{12,8},{9,1... | collective-permute-start | bytes 3538952 | tf_op jit(solution)/shard_map/ppermute | solution.py:30
  94.1 18.2 %collective-permute-start.4 = (bf16[64,768]{1,0:T(8,128)(2,1)S(1)}, bf16[64,768]{1,0:T(8,128)(2,1)S(1)}, u32[]{:S(2)}, u32[]{:S(2)}) collective-permute-start(bf16[64,768]{1,0:T(8,128)(2,1)S(1)} %add_convert_fusion), channel_id=1, source_target_pairs={{0,64},{64,128},{128,192},{192,256},{256,320},{320,384},{384,448},... | collective-permute-start | bytes 294920 | tf_op jit(solution)/shard_map/ppermute | solution.py:158
  134.9 7.8 %collective-permute-start.5 = (bf16[512,768]{1,0:T(8,128)(2,1)S(1)}, bf16[512,768]{1,0:T(8,128)(2,1)S(1)}, u32[]{:S(2)}, u32[]{:S(2)}) collective-permute-start(bf16[512,768]{1,0:T(8,128)(2,1)S(1)} %bitcast.29), channel_id=1, source_target_pairs={{0,4},{4,0},{1,5},{5,1},{2,6},{6,2},{3,7},{7,3},{8,12},{12,8},{9,1... | collective-permute-start | bytes 2359304 | tf_op jit(solution)/shard_map/ppermute | solution.py:30

commit v6 on v5

--- a/solution.py
+++ b/solution.py
@@ -30,32 +30,32 @@
     return lax.ppermute(block, "core", [(0, 1), (1, 0)])
 
 
-def partial_kernel(chunks_ref, inputs_ref, upstream_ref, up_ref, down_ref, *out_refs):
-    terms = [
-        product(inputs_ref[...], up_ref[...], 0).astype(jnp.bfloat16),
-        product(upstream_ref[...], down_ref[...], 1).astype(jnp.bfloat16),
-    ]
-    for step, out_ref in enumerate(out_refs):
-
-        @pl.when(pl.program_id(0) == step)
-        def _():
-            out_ref[0], out_ref[1] = terms
+def partial_kernel(chunks_ref, inputs_ref, upstream_ref, up_ref, down_ref, *refs):
+    *out_refs, sums_ref = refs
+    rows = out_refs[0].shape[1]
+    sums_ref[0] = product(inputs_ref[...], up_ref[...], 0).astype(jnp.bfloat16)
+    sums_ref[1] = product(upstream_ref[...], down_ref[...], 1).astype(jnp.bfloat16)
+    for i, out_ref in enumerate(out_refs):
+        start = pl.multiple_of(chunks_ref[i] * rows, rows)
+        out_ref[...] = sums_ref[:, pl.ds(start, rows), :]
 
 
-def partial_sums(chunks, count, inputs, upstream, w_up, w_down, rows):
-    width = w_up.shape[1]
-    chunk = pl.BlockSpec((rows, inputs.shape[1]), lambda i, chunks: (chunks[i], 0))
-    whole = pl.BlockSpec(w_up.shape, lambda i, chunks: (0, 0))
-    kept = pl.BlockSpec((2, rows, width), lambda i, chunks: (0, 0, 0))
+def partial_sums(chunks, inputs, upstream, w_up, w_down):
+    count, width = chunks.shape[0], w_up.shape[1]
+    part = (2, inputs.shape[0] // count, width)
     return pl.pallas_call(
         partial_kernel,
         grid_spec=pltpu.PrefetchScalarGridSpec(
             num_scalar_prefetch=1,
-            grid=(count,),
-            in_specs=[chunk, chunk, whole, whole],
-            out_specs=[kept] * count,
+            grid=(1,),
+            in_specs=[
+                pl.BlockSpec(operand.shape, lambda i, chunks: (0, 0))
+                for operand in (inputs, upstream, w_up, w_down)
+            ],
+            out_specs=[pl.BlockSpec(part, lambda i, chunks: (0, 0, 0))] * count,
+            scratch_shapes=[pltpu.VMEM((2, inputs.shape[0], width), jnp.bfloat16)],
         ),
-        out_shape=[jax.ShapeDtypeStruct((2, rows, width), jnp.bfloat16)] * count,
+        out_shape=[jax.ShapeDtypeStruct(part, jnp.bfloat16)] * count,
         compiler_params=pltpu.CompilerParams(vmem_limit_bytes=58 << 20),
     )(chunks, inputs, upstream, w_up, w_down)
 
@@ -80,7 +80,7 @@
         + [pl.BlockSpec((tile, width), lambda i: (i, 0))],
         out_specs=pl.BlockSpec((2, len(parts), tile, width), lambda i: (0, 0, i, 0)),
         out_shape=jax.ShapeDtypeStruct((2, len(parts), rows, width), jnp.bfloat16),
-        compiler_params=pltpu.CompilerParams(vmem_limit_bytes=32 << 20),
+        compiler_params=pltpu.CompilerParams(vmem_limit_bytes=63 << 20),
     )(*parts, stored)
 
 
@@ -99,7 +99,7 @@
         both(arrived_ref, own_ref, 1)
 
 
-def feature_terms(core, hidden, own, arrived, steps=2):
+def feature_terms(core, hidden, own, arrived, steps=1):
     _, rows, width = hidden.shape
     tile = rows // steps
     whole = pl.BlockSpec(own.shape, lambda i, core: (0, 0))
@@ -129,10 +129,9 @@
     piece = count // ny
     start = lax.axis_index("y") * piece
     col = lax.axis_index("col")
-    operands = (inputs, upstream, w_up, w_down, count // ncol)
     reach = sorted(range(1, ncol), key=lambda d: -min(d, ncol - d))
     chunks = jnp.stack([(col + d) % ncol for d in reach] + [col])
-    terms = partial_sums(chunks, ncol, *operands)
+    terms = partial_sums(chunks, inputs, upstream, w_up, w_down)
     parts = [terms[-1]] + [
         lax.ppermute(term, "col", [(i, (i + d) % ncol) for i in range(ncol)])
         for d, term in zip(reach, terms)

time: 145 us -> 143 us (0.986)
    pallas_call x1, Pallas kernels: 7.01 us -> 5.31 us  [partial_sums(): pl.pallas_call(partial_kernel, grid_spec=pltpu.PrefetchScalarGridSpec(num...]
where the time goes in v6:
time: 143 us; the launch traced here: 142 us
  starting transfers between devices  50.8 us (36%)
  blocking collectives  48.3 us (34%)
  waiting for transfers between devices  26 us (18%)
  Pallas kernels  10.6 us (7%)
  other arithmetic  5.8 us (4%)
    all_to_all x1, blocking collectives, body(): lax.all_to_all(chip_sum.reshape(ny, piece, -1), 'y', 0, 0, tiled=True)  26 us
    all_to_all x1, blocking collectives, body(): mine = lax.all_to_all(pieces, 'y', 0, 0, tiled=True).reshape(count, -1)  22.3 us
    ppermute x1, starting transfers between devices, body(): moved = lax.ppermute(result, ('section', 'core'), route)  16.5 us
    all_to_all x1, starting transfers between devices, body(): gathered = lax.all_to_all(copies, ('core', 'col'), 0, 0, tiled=True)  14.3 us
    all_to_all x1, waiting for transfers between devices, body(): gathered = lax.all_to_all(copies, ('core', 'col'), 0, 0, tiled=True)  12.7 us
    ppermute x3, starting transfers between devices, body(): lax.ppermute(term, 'col', [(i, (i + d) % ncol) for i in range(ncol)])  12 us
    ppermute x2, starting transfers between devices, swapped(): return lax.ppermute(block, 'core', [(0, 1), (1, 0)])  8.02 us
    ppermute x3, waiting for transfers between devices, body(): lax.ppermute(term, 'col', [(i, (i + d) % ncol) for i in range(ncol)])  7.65 us
  transfers between devices with their start and end apart: 7, of which 6 were waited for; matrix products, arithmetic and copies ran while one was open for 3% of the time, Pallas kernels for 0%

profile of v6, /device:TPU:1, one launch (start us, length us, event | category | flops | bytes accessed | tf_op | source)
XLA Modules:
  0.0 142.4 jit_solution(12821149551069387969)
XLA Ops:
  0.7 0.6 pad_add_fusion.chunks_ref
  1.3 5.3 %shard_map.68 = (bf16[2,128,768]{2,1,0:T(8,128)(2,1)}, bf16[2,128,768]{2,1,0:T(8,128)(2,1)}, bf16[2,128,768]{2,1,0:T(8,128)(2,1)}, bf16[2,128,768]{2,1,0:T(8,128)(2,1)}) custom-call(s32[4]{0:T(128)} %pad_add_fusion.chunks_ref, bf16[512,768]{1,0:T(8,128)(2,1)} %bitcast.30, bf16[512,768]{1,0:T(8,128)(2,1)} %bitcast.31, bf16[768,768]{1,0:T(8,128)(2,1)} %bitcast.25, ...), custom_call_target="tpu_custom_call" | custom-call | tf_op jit(solution)/shard_map/pallas_call | solution.py:46
  6.6 5.5 %collective-permute-start = (bf16[2,128,768]{2,1,0:T(8,128)(2,1)}, bf16[2,128,768]{2,1,0:T(8,128)(2,1)S(1)}, u32[]{:S(2)}, u32[]{:S(2)}) collective-permute-start(bf16[2,128,768]{2,1,0:T(8,128)(2,1)} %get-tuple-element.12), channel_id=1, source_target_pairs={{0,2},{1,3},{2,0},{3,1},{4,6},{5,7},{6,4},{7,5},{8,10},{9,11},{10,... | collective-permute-start | bytes 1179656 | tf_op jit(solution)/shard_map/ppermute | solution.py:136
  12.1 2.2 %collective-permute-start.1 = (bf16[2,128,768]{2,1,0:T(8,128)(2,1)}, bf16[2,128,768]{2,1,0:T(8,128)(2,1)S(1)}, u32[]{:S(2)}, u32[]{:S(2)}) collective-permute-start(bf16[2,128,768]{2,1,0:T(8,128)(2,1)} %get-tuple-element.13), channel_id=1, source_target_pairs={{0,1},{1,2},{2,3},{3,0},{4,5},{5,6},{6,7},{7,4},{8,9},{9,10},{10,1... | collective-permute-start | bytes 1179656 | tf_op jit(solution)/shard_map/ppermute | solution.py:136
  14.3 4.3 %collective-permute-start.2 = (bf16[2,128,768]{2,1,0:T(8,128)(2,1)}, bf16[2,128,768]{2,1,0:T(8,128)(2,1)}, u32[]{:S(2)}, u32[]{:S(2)}) collective-permute-start(bf16[2,128,768]{2,1,0:T(8,128)(2,1)} %get-tuple-element.14), channel_id=1, source_target_pairs={{0,3},{1,0},{2,1},{3,2},{4,7},{5,4},{6,5},{7,6},{8,11},{9,8},{10,9... | collective-permute-start | bytes 1179656 | tf_op jit(solution)/shard_map/ppermute | solution.py:136
  18.6 3.4 %collective-permute-done.1.refs_2_ = bf16[2,128,768]{2,1,0:T(8,128)(2,1)S(1)} collective-permute-done((bf16[2,128,768]{2,1,0:T(8,128)(2,1)}, bf16[2,128,768]{2,1,0:T(8,128)(2,1)S(1)}, u32[]{:S(2)}, u32[]{:S(2)}) %collective-permute-start.1) | collective-permute-done | bytes 393248 | tf_op jit(solution)/shard_map/ppermute | solution.py:136
  22.0 4.2 %collective-permute-done.2.refs_3_ = bf16[2,128,768]{2,1,0:T(8,128)(2,1)} collective-permute-done((bf16[2,128,768]{2,1,0:T(8,128)(2,1)}, bf16[2,128,768]{2,1,0:T(8,128)(2,1)}, u32[]{:S(2)}, u32[]{:S(2)}) %collective-permute-start.2) | collective-permute-done | bytes 393248 | tf_op jit(solution)/shard_map/ppermute | solution.py:136
  26.3 2.6 %shard_map.69 = bf16[2,4,128,768]{3,2,1,0:T(8,128)(2,1)} custom-call(bf16[2,128,768]{2,1,0:T(8,128)(2,1)} %get-tuple-element.11.refs_0_, bf16[2,128,768]{2,1,0:T(8,128)(2,1)} %copy-done, bf16[2,128,768]{2,1,0:T(8,128)(2,1)} %copy-done.1, bf16[2,128,768]{2,1,0:T(8,128)(2,1)} %collective-permute-done.2.refs_3_, bf16[128,768]{1,0:T(8,128)(2,1)} %bitcast.32), custom_call_target="tpu_custom_call" | custom-call | tf_op jit(solution)/shard_map/pallas_call | solution.py:76
  28.9 14.3 %all-to-all-start = ((bf16[8,128,768]{2,1,0:T(8,128)(2,1)}), bf16[8,128,768]{2,1,0:T(8,128)(2,1)S(1)}, u32[]{:S(2)}, u32[]{:S(2)}) async-start(bf16[8,128,768]{2,1,0:T(8,128)(2,1)} %bitcast.24), calls=%async_computation | async-start | bytes 3145728 | tf_op jit(solution)/shard_map/all_to_all | solution.py:149
  43.2 2.8 %broadcast_select_fusion = (bf16[768,768]{1,0:T(8,128)(2,1)}, bf16[768,768]{1,0:T(8,128)(2,1)S(1)}) fusion(bf16[768,768]{1,0:T(8,128)(2,1)} %bitcast.26, bf16[768,768]{1,0:T(8,128)(2,1)} %bitcast.28, pred[]{:T(512)S(6)} %eq.7), kind=kLoop, calls=%fused_computation.1 | loop fusion | flops 1179648 | bytes 4718593 | tf_op jit(solution)/shard_map/jit(_where)/select_n | solution.py:143
  46.0 2.0 %collective-permute-start.3 = (bf16[768,768]{1,0:T(8,128)(2,1)}, bf16[768,768]{1,0:T(8,128)(2,1)}, u32[]{:S(2)}, u32[]{:S(2)}) collective-permute-start(bf16[768,768]{1,0:T(8,128)(2,1)} %get-tuple-element.20), channel_id=1, source_target_pairs={{0,4},{4,0},{1,5},{5,1},{2,6},{6,2},{3,7},{7,3},{8,12},{12,8},{9,1... | collective-permute-start | bytes 3538952 | tf_op jit(solution)/shard_map/ppermute | solution.py:30
  48.0 1.0 select_bitcast_fusion.2
  49.0 2.1 %collective-permute-done.3.arrived_ref = bf16[768,768]{1,0:T(8,128)(2,1)} collective-permute-done((bf16[768,768]{1,0:T(8,128)(2,1)}, bf16[768,768]{1,0:T(8,128)(2,1)}, u32[]{:S(2)}, u32[]{:S(2)}) %collective-permute-start.3) | collective-permute-done | bytes 1179680 | tf_op jit(solution)/shard_map/ppermute | solution.py:30
  51.1 12.7 %all-to-all-done = bf16[8,128,768]{2,1,0:T(8,128)(2,1)S(1)} async-done(((bf16[8,128,768]{2,1,0:T(8,128)(2,1)}), bf16[8,128,768]{2,1,0:T(8,128)(2,1)S(1)}, u32[]{:S(2)}, u32[]{:S(2)}) %all-to-all-start) | async-done | bytes 1572896 | tf_op jit(solution)/shard_map/all_to_all | solution.py:149
  63.8 2.7 %shard_map.70 = bf16[512,768]{1,0:T(8,128)(2,1)S(1)} custom-call(s32[1]{0:T(128)} %bitcast.core_ref, bf16[2,512,768]{2,1,0:T(8,128)(2,1)S(1)} %bitcast.22, bf16[768,768]{1,0:T(8,128)(2,1)S(1)} %get-tuple-element.21.own_ref, bf16[768,768]{1,0:T(8,128)(2,1)} %collective-permute-done.3.arrived_ref), custom_call_target="tpu_custom_call" | custom-call | tf_op jit(solution)/shard_map/pallas_call | solution.py:106
  66.5 26.0 %all_to_all.15 = bf16[8,64,768]{2,1,0:T(8,128)(2,1)S(1)} all-to-all(bf16[8,64,768]{2,1,0:T(8,128)(2,1)S(1)} %bitcast.23), channel_id=1, replica_groups=mesh['section'=16,'y'=8,'core'=2,'col'=4] {'y'}, dimensions={0} | all-to-all | bytes 1572864 | tf_op jit(solution)/shard_map/all_to_all | solution.py:152
  92.5 0.1 convert_reduce_fusion
  92.6 16.5 %collective-permute-start.4 = (bf16[64,768]{1,0:T(8,128)(2,1)S(1)}, bf16[64,768]{1,0:T(8,128)(2,1)S(1)}, u32[]{:S(2)}, u32[]{:S(2)}) collective-permute-start(bf16[64,768]{1,0:T(8,128)(2,1)S(1)} %add_convert_fusion), channel_id=1, source_target_pairs={{0,64},{64,128},{128,192},{192,256},{256,320},{320,384},{384,448},... | collective-permute-start | bytes 294920 | tf_op jit(solution)/shard_map/ppermute | solution.py:157
  109.2 1.6 %collective-permute-done.4 = bf16[64,768]{1,0:T(8,128)(2,1)S(1)} collective-permute-done((bf16[64,768]{1,0:T(8,128)(2,1)S(1)}, bf16[64,768]{1,0:T(8,128)(2,1)S(1)}, u32[]{:S(2)}, u32[]{:S(2)}) %collective-permute-start.4) | collective-permute-done | bytes 98336 | tf_op jit(solution)/shard_map/ppermute | solution.py:157
  110.8 0.1 broadcast_in_dim.12
  110.8 22.3 %all_to_all.16 = bf16[8,64,768]{2,1,0:T(8,128)(2,1)S(1)} all-to-all(bf16[8,64,768]{2,1,0:T(8,128)(2,1)S(1)} %broadcast_in_dim.12), channel_id=1, replica_groups=mesh['section'=16,'y'=8,'core'=2,'col'=4] {'y'}, dimensions={0} | all-to-all | bytes 1572864 | tf_op jit(solution)/shard_map/all_to_all | solution.py:159
  133.2 6.0 %collective-permute-start.5 = (bf16[512,768]{1,0:T(8,128)(2,1)S(1)}, bf16[512,768]{1,0:T(8,128)(2,1)S(1)}, u32[]{:S(2)}, u32[]{:S(2)}) collective-permute-start(bf16[512,768]{1,0:T(8,128)(2,1)S(1)} %bitcast.29), channel_id=1, source_target_pairs={{0,4},{4,0},{1,5},{5,1},{2,6},{6,2},{3,7},{7,3},{8,12},{12,8},{9,1... | collective-permute-start | bytes 2359304 | tf_op jit(solution)/shard_map/ppermute | solution.py:30
  139.2 1.9 %collective-permute-done.5 = bf16[512,768]{1,0:T(8,128)(2,1)S(1)} collective-permute-done((bf16[512,768]{1,0:T(8,128)(2,1)S(1)}, bf16[512,768]{1,0:T(8,128)(2,1)S(1)}, u32[]{:S(2)}, u32[]{:S(2)}) %collective-permute-start.5) | collective-permute-done | bytes 786464 | tf_op jit(solution)/shard_map/ppermute | solution.py:30
  141.1 1.3 select_bitcast_fusion
  (6 shorter events, 0.0 us)
Async XLA Ops:
  6.6 12.0 %collective-permute-start = (bf16[2,128,768]{2,1,0:T(8,128)(2,1)}, bf16[2,128,768]{2,1,0:T(8,128)(2,1)S(1)}, u32[]{:S(2)}, u32[]{:S(2)}) collective-permute-start(bf16[2,128,768]{2,1,0:T(8,128)(2,1)} %get-tuple-element.12), channel_id=1, source_target_pairs={{0,2},{1,3},{2,0},{3,1},{4,6},{5,7},{6,4},{7,5},{8,10},{9,11},{10,... | collective-permute-start | bytes 1179656 | tf_op jit(solution)/shard_map/ppermute | solution.py:136
  12.1 9.9 %collective-permute-start.1 = (bf16[2,128,768]{2,1,0:T(8,128)(2,1)}, bf16[2,128,768]{2,1,0:T(8,128)(2,1)S(1)}, u32[]{:S(2)}, u32[]{:S(2)}) collective-permute-start(bf16[2,128,768]{2,1,0:T(8,128)(2,1)} %get-tuple-element.13), channel_id=1, source_target_pairs={{0,1},{1,2},{2,3},{3,0},{4,5},{5,6},{6,7},{7,4},{8,9},{9,10},{10,1... | collective-permute-start | bytes 1179656 | tf_op jit(solution)/shard_map/ppermute | solution.py:136
  14.3 12.0 %collective-permute-start.2 = (bf16[2,128,768]{2,1,0:T(8,128)(2,1)}, bf16[2,128,768]{2,1,0:T(8,128)(2,1)}, u32[]{:S(2)}, u32[]{:S(2)}) collective-permute-start(bf16[2,128,768]{2,1,0:T(8,128)(2,1)} %get-tuple-element.14), channel_id=1, source_target_pairs={{0,3},{1,0},{2,1},{3,2},{4,7},{5,4},{6,5},{7,6},{8,11},{9,8},{10,9... | collective-permute-start | bytes 1179656 | tf_op jit(solution)/shard_map/ppermute | solution.py:136
  18.6 7.7 %copy-start = (bf16[2,128,768]{2,1,0:T(8,128)(2,1)}, bf16[2,128,768]{2,1,0:T(8,128)(2,1)S(1)}, u32[]{:S(2)}) copy-start(bf16[2,128,768]{2,1,0:T(8,128)(2,1)S(1)} %collective-permute-done.refs_1_) | copy-start | bytes 1179652
  22.0 4.3 %copy-start.1 = (bf16[2,128,768]{2,1,0:T(8,128)(2,1)}, bf16[2,128,768]{2,1,0:T(8,128)(2,1)S(1)}, u32[]{:S(2)}) copy-start(bf16[2,128,768]{2,1,0:T(8,128)(2,1)S(1)} %collective-permute-done.1.refs_2_) | copy-start | bytes 1179652
  28.9 34.9 %all-to-all-start = ((bf16[8,128,768]{2,1,0:T(8,128)(2,1)}), bf16[8,128,768]{2,1,0:T(8,128)(2,1)S(1)}, u32[]{:S(2)}, u32[]{:S(2)}) async-start(bf16[8,128,768]{2,1,0:T(8,128)(2,1)} %bitcast.24), calls=%async_computation | async-start | bytes 3145728 | tf_op jit(solution)/shard_map/all_to_all | solution.py:149
  46.0 5.1 %collective-permute-start.3 = (bf16[768,768]{1,0:T(8,128)(2,1)}, bf16[768,768]{1,0:T(8,128)(2,1)}, u32[]{:S(2)}, u32[]{:S(2)}) collective-permute-start(bf16[768,768]{1,0:T(8,128)(2,1)} %get-tuple-element.20), channel_id=1, source_target_pairs={{0,4},{4,0},{1,5},{5,1},{2,6},{6,2},{3,7},{7,3},{8,12},{12,8},{9,1... | collective-permute-start | bytes 3538952 | tf_op jit(solution)/shard_map/ppermute | solution.py:30
  92.6 18.1 %collective-permute-start.4 = (bf16[64,768]{1,0:T(8,128)(2,1)S(1)}, bf16[64,768]{1,0:T(8,128)(2,1)S(1)}, u32[]{:S(2)}, u32[]{:S(2)}) collective-permute-start(bf16[64,768]{1,0:T(8,128)(2,1)S(1)} %add_convert_fusion), channel_id=1, source_target_pairs={{0,64},{64,128},{128,192},{192,256},{256,320},{320,384},{384,448},... | collective-permute-start | bytes 294920 | tf_op jit(solution)/shard_map/ppermute | solution.py:157
  133.2 7.9 %collective-permute-start.5 = (bf16[512,768]{1,0:T(8,128)(2,1)S(1)}, bf16[512,768]{1,0:T(8,128)(2,1)S(1)}, u32[]{:S(2)}, u32[]{:S(2)}) collective-permute-start(bf16[512,768]{1,0:T(8,128)(2,1)S(1)} %bitcast.29), channel_id=1, source_target_pairs={{0,4},{4,0},{1,5},{5,1},{2,6},{6,2},{3,7},{7,3},{8,12},{12,8},{9,1... | collective-permute-start | bytes 2359304 | tf_op jit(solution)/shard_map/ppermute | solution.py:30

commit v7 on v4

--- a/solution.py
+++ b/solution.py
@@ -38,8 +38,8 @@
     active = gelu_value(sums[0]).astype(jnp.bfloat16)
     hidden_grad = (sums[1] * gelu_slope(stored_ref[...].astype(jnp.float32))).astype(jnp.bfloat16)
     for i in range(ncol):
-        copies_ref[0, i] = active
-        copies_ref[1, i] = hidden_grad
+        copies_ref[0, i] = hidden_grad
+        copies_ref[1, i] = active
 
 
 def hidden_copies(parts, stored, steps=2):
@@ -66,14 +66,14 @@
 
     @pl.when(core_ref[0] == 0)
     def _():
-        both(own_ref, arrived_ref, 0)
+        both(own_ref, arrived_ref, 1)
 
     @pl.when(core_ref[0] != 0)
     def _():
-        both(arrived_ref, own_ref, 1)
+        both(arrived_ref, own_ref, 0)
 
 
-def feature_terms(core, hidden, own, arrived, steps=2):
+def feature_terms(core, hidden, own, arrived, steps=1):
     _, rows, width = hidden.shape
     tile = rows // steps
     whole = pl.BlockSpec(own.shape, lambda i, core: (0, 0))
@@ -98,7 +98,7 @@
     inputs, w_up, w_down, upstream = tokens[0], up_weight[0], down_weight[0], out_grad[0]
     ncol, ny, nz = lax.axis_size("col"), lax.axis_size("y"), lax.axis_size("section")
     core = lax.axis_index("core")
-    forward = core == 0
+    forward = core == 1
     count = inputs.shape[0]
 
     def by_col(partial):
@@ -126,14 +126,14 @@
     summed = lax.all_to_all(chip_sum.reshape(ny, piece, -1), "y", 0, 0, tiled=True)
     summed = summed.astype(jnp.float32).sum(0)
     result = (residual.astype(jnp.float32) + summed).astype(jnp.bfloat16)
-    route = [(2 * s, 2 * ((s + 1) % nz)) for s in range(nz)]
-    route += [(2 * s + 1, 2 * ((s - 1) % nz) + 1) for s in range(nz)]
+    route = [(2 * s + 1, 2 * ((s + 1) % nz)) for s in range(nz)]
+    route += [(2 * s, 2 * ((s - 1) % nz) + 1) for s in range(nz)]
     moved = lax.ppermute(result, ("section", "core"), route)
     pieces = jnp.broadcast_to(moved[None], (ny,) + moved.shape)
     mine = lax.all_to_all(pieces, "y", 0, 0, tiled=True).reshape(count, -1)
     other = swapped(mine)
-    next_tokens = jnp.where(forward, mine, other)
-    prev_grads = jnp.where(forward, other, mine)
+    next_tokens = jnp.where(forward, other, mine)
+    prev_grads = jnp.where(forward, mine, other)
     return (next_tokens[None], prev_grads[None])
 
 

time: 141 us -> 132 us (0.936)
  blocking collectives: 65.4 us -> 59.5 us
  starting transfers between devices: 42.4 us -> 40 us
    ppermute x1, starting transfers between devices: 17.9 us -> 5.8 us  [body(): moved = lax.ppermute(result, ('section', 'core'), route)]
    ppermute x2, starting transfers between devices: 7.86 us -> 17.6 us  [swapped(): return lax.ppermute(block, 'core', [(0, 1), (1, 0)])]
    all_to_all x1, blocking collectives: 22.5 us -> 17.4 us  [body(): mine = lax.all_to_all(pieces, 'y', 0, 0, tiled=True).reshape(count, -1)]
where the time goes in v7:
time: 132 us
  blocking collectives  59.5 us (45%)
  starting transfers between devices  40 us (30%)
  waiting for transfers between devices  19 us (14%)
  other arithmetic  5.37 us (4%)
  Pallas kernels  4.15 us (3%)
  matrix products  3.23 us (2%)
    all_to_all x1, blocking collectives, body(): lax.all_to_all(chip_sum.reshape(ny, piece, -1), 'y', 0, 0, tiled=True)  24.8 us
    ppermute x2, starting transfers between devices, swapped(): return lax.ppermute(block, 'core', [(0, 1), (1, 0)])  17.6 us
    all_to_all x1, blocking collectives, body(): mine = lax.all_to_all(pieces, 'y', 0, 0, tiled=True).reshape(count, -1)  17.4 us
    all_to_all x1, blocking collectives, body(): parts = lax.all_to_all(partials, 'col', 0, 0, tiled=True)  17.3 us
    all_to_all x1, starting transfers between devices, body(): gathered = lax.all_to_all(copies, ('core', 'col'), 0, 0, tiled=True)  16.6 us
    all_to_all x1, waiting for transfers between devices, body(): gathered = lax.all_to_all(copies, ('core', 'col'), 0, 0, tiled=True)  12.7 us
    ppermute x1, starting transfers between devices, body(): moved = lax.ppermute(result, ('section', 'core'), route)  5.8 us
    ppermute x2, waiting for transfers between devices, swapped(): return lax.ppermute(block, 'core', [(0, 1), (1, 0)])  3.95 us
  transfers between devices with their start and end apart: 4, of which 4 were waited for; matrix products, arithmetic and copies ran while one was open for 3% of the time, Pallas kernels for 0%

profile of v7, /device:TPU:1, one launch (start us, length us, event | category | flops | bytes accessed | tf_op | source)
XLA Modules:
  0.0 132.0 jit_solution(16160690768834269076)
XLA Ops:
  0.6 0.0 copy-start.1
  0.6 0.0 copy-start.2
  0.7 2.5 %convolution_convert_fusion = bf16[512,768]{1,0:T(8,128)(2,1)S(1)} fusion(bf16[1,768,768]{2,1,0:T(8,128)(2,1)} %param.7, bf16[1,512,768]{2,1,0:T(8,128)(2,1)} %param.8), kind=kOutput, calls=%fused_computation.2 | convolution fusion | flops 604372992 | bytes 2752512 | tf_op jit(solution)/shard_map/dot_general | solution.py:24
  3.1 0.8 convolution_convert_fusion.1
  3.9 0.1 pad_maximum_fusion
  4.1 0.0 copy-start
  4.1 17.3 %all_to_all.20.parts_ref = bf16[4,2,128,768]{3,2,1,0:T(8,128)(2,1)S(1)} all-to-all(bf16[4,2,128,768]{3,2,1,0:T(8,128)(2,1)S(1)} %pad_maximum_fusion), channel_id=1, replica_groups=mesh['section'=16,'y'=8,'core'=2,'col'=4] {'col'}, dimensions={0} | all-to-all | bytes 3145728 | tf_op jit(solution)/shard_map/all_to_all | solution.py:113
  21.4 1.5 %shard_map.68 = bf16[2,4,128,768]{3,2,1,0:T(8,128)(2,1)} custom-call(bf16[4,2,128,768]{3,2,1,0:T(8,128)(2,1)S(1)} %all_to_all.20.parts_ref, bf16[128,768]{1,0:T(8,128)(2,1)S(1)} %bitcast.34), custom_call_target="tpu_custom_call" | custom-call | tf_op jit(solution)/shard_map/pallas_call | solution.py:48
  22.9 16.6 %all-to-all-start.1 = ((bf16[8,128,768]{2,1,0:T(8,128)(2,1)}), bf16[8,128,768]{2,1,0:T(8,128)(2,1)S(1)}, u32[]{:S(2)}, u32[]{:S(2)}) async-start(bf16[8,128,768]{2,1,0:T(8,128)(2,1)} %bitcast.8), calls=%async_computation.1 | async-start | bytes 3145728 | tf_op jit(solution)/shard_map/all_to_all | solution.py:118
  39.5 2.8 %bitcast_select_fusion = (bf16[768,768]{1,0:T(8,128)(2,1)}, bf16[768,768]{1,0:T(8,128)(2,1)S(1)}) fusion(bf16[1,768,768]{2,1,0:T(8,128)(2,1)} %param.7, bf16[1,768,768]{2,1,0:T(8,128)(2,1)} %param.6, pred[]{:T(512)S(6)} %eq.3), kind=kLoop, calls=%fused_computation.4 | loop fusion | flops 1179648 | bytes 4718593 | tf_op jit(solution)/shard_map/jit(_where)/select_n | solution.py:115
  42.3 2.0 %collective-permute-start = (bf16[768,768]{1,0:T(8,128)(2,1)}, bf16[768,768]{1,0:T(8,128)(2,1)}, u32[]{:S(2)}, u32[]{:S(2)}) collective-permute-start(bf16[768,768]{1,0:T(8,128)(2,1)} %get-tuple-element.14), channel_id=1, source_target_pairs={{0,4},{4,0},{1,5},{5,1},{2,6},{6,2},{3,7},{7,3},{8,12},{12,8},{9,1... | collective-permute-start | bytes 3538952 | tf_op jit(solution)/shard_map/ppermute | solution.py:30
  44.3 1.0 select_bitcast_fusion.2
  45.3 2.1 %collective-permute-done.arrived_ref = bf16[768,768]{1,0:T(8,128)(2,1)} collective-permute-done((bf16[768,768]{1,0:T(8,128)(2,1)}, bf16[768,768]{1,0:T(8,128)(2,1)}, u32[]{:S(2)}, u32[]{:S(2)}) %collective-permute-start) | collective-permute-done | bytes 1179680 | tf_op jit(solution)/shard_map/ppermute | solution.py:30
  47.4 12.7 %all-to-all-done.1 = bf16[8,128,768]{2,1,0:T(8,128)(2,1)S(1)} async-done(((bf16[8,128,768]{2,1,0:T(8,128)(2,1)}), bf16[8,128,768]{2,1,0:T(8,128)(2,1)S(1)}, u32[]{:S(2)}, u32[]{:S(2)}) %all-to-all-start.1) | async-done | bytes 1572896 | tf_op jit(solution)/shard_map/all_to_all | solution.py:118
  60.1 2.7 %shard_map.69 = bf16[512,768]{1,0:T(8,128)(2,1)S(1)} custom-call(s32[1]{0:T(128)} %bitcast.6.core_ref, bf16[2,512,768]{2,1,0:T(8,128)(2,1)S(1)} %bitcast.32, bf16[768,768]{1,0:T(8,128)(2,1)S(1)} %get-tuple-element.15.own_ref, bf16[768,768]{1,0:T(8,128)(2,1)} %collective-permute-done.arrived_ref), custom_call_target="tpu_custom_call" | custom-call | tf_op jit(solution)/shard_map/pallas_call | solution.py:80
  62.8 24.8 %all_to_all.21 = bf16[8,64,768]{2,1,0:T(8,128)(2,1)S(1)} all-to-all(bf16[8,64,768]{2,1,0:T(8,128)(2,1)S(1)} %bitcast.33), channel_id=1, replica_groups=mesh['section'=16,'y'=8,'core'=2,'col'=4] {'y'}, dimensions={0} | all-to-all | bytes 1572864 | tf_op jit(solution)/shard_map/all_to_all | solution.py:126
  87.6 0.1 convert_reduce_fusion
  87.7 5.8 %collective-permute-start.1 = (bf16[64,768]{1,0:T(8,128)(2,1)S(1)}, bf16[64,768]{1,0:T(8,128)(2,1)S(1)}, u32[]{:S(2)}, u32[]{:S(2)}) collective-permute-start(bf16[64,768]{1,0:T(8,128)(2,1)S(1)} %add_convert_fusion), channel_id=1, source_target_pairs={{4,64},{68,128},{132,192},{196,256},{260,320},{324,384},{388,448},... | collective-permute-start | bytes 294920 | tf_op jit(solution)/shard_map/ppermute | solution.py:131
  93.5 2.3 %collective-permute-done.1 = bf16[64,768]{1,0:T(8,128)(2,1)S(1)} collective-permute-done((bf16[64,768]{1,0:T(8,128)(2,1)S(1)}, bf16[64,768]{1,0:T(8,128)(2,1)S(1)}, u32[]{:S(2)}, u32[]{:S(2)}) %collective-permute-start.1) | collective-permute-done | bytes 98336 | tf_op jit(solution)/shard_map/ppermute | solution.py:131
  95.8 0.1 broadcast_in_dim.12
  95.9 17.4 %all_to_all.22 = bf16[8,64,768]{2,1,0:T(8,128)(2,1)S(1)} all-to-all(bf16[8,64,768]{2,1,0:T(8,128)(2,1)S(1)} %broadcast_in_dim.12), channel_id=1, replica_groups=mesh['section'=16,'y'=8,'core'=2,'col'=4] {'y'}, dimensions={0} | all-to-all | bytes 1572864 | tf_op jit(solution)/shard_map/all_to_all | solution.py:133
  113.2 15.6 %collective-permute-start.2 = (bf16[512,768]{1,0:T(8,128)(2,1)S(1)}, bf16[512,768]{1,0:T(8,128)(2,1)S(1)}, u32[]{:S(2)}, u32[]{:S(2)}) collective-permute-start(bf16[512,768]{1,0:T(8,128)(2,1)S(1)} %bitcast.35), channel_id=1, source_target_pairs={{0,4},{4,0},{1,5},{5,1},{2,6},{6,2},{3,7},{7,3},{8,12},{12,8},{9,1... | collective-permute-start | bytes 2359304 | tf_op jit(solution)/shard_map/ppermute | solution.py:30
  128.8 1.9 %collective-permute-done.2 = bf16[512,768]{1,0:T(8,128)(2,1)S(1)} collective-permute-done((bf16[512,768]{1,0:T(8,128)(2,1)S(1)}, bf16[512,768]{1,0:T(8,128)(2,1)S(1)}, u32[]{:S(2)}, u32[]{:S(2)}) %collective-permute-start.2) | collective-permute-done | bytes 786464 | tf_op jit(solution)/shard_map/ppermute | solution.py:30
  130.7 1.3 select_bitcast_fusion
  (4 shorter events, 0.0 us)
Async XLA Ops:
  0.6 2.5 %copy-start.1 = (bf16[1,768,768]{2,1,0:T(8,128)(2,1)S(1)}, bf16[1,768,768]{2,1,0:T(8,128)(2,1)}, u32[]{:S(2)}) copy-start(bf16[1,768,768]{2,1,0:T(8,128)(2,1)} %param.6) | copy-start | bytes 3538948
  0.6 2.5 %copy-start.2 = (bf16[1,512,768]{2,1,0:T(8,128)(2,1)S(1)}, bf16[1,512,768]{2,1,0:T(8,128)(2,1)}, u32[]{:S(2)}) copy-start(bf16[1,512,768]{2,1,0:T(8,128)(2,1)} %param.5) | copy-start | bytes 2359300
  4.1 17.3 %copy-start = (bf16[1,128,768]{2,1,0:T(8,128)(2,1)S(1)}, bf16[1,128,768]{2,1,0:T(8,128)(2,1)}, u32[]{:S(2)}) copy-start(bf16[1,128,768]{2,1,0:T(8,128)(2,1)} %param.9) | copy-start | bytes 589828
  22.9 37.2 %all-to-all-start.1 = ((bf16[8,128,768]{2,1,0:T(8,128)(2,1)}), bf16[8,128,768]{2,1,0:T(8,128)(2,1)S(1)}, u32[]{:S(2)}, u32[]{:S(2)}) async-start(bf16[8,128,768]{2,1,0:T(8,128)(2,1)} %bitcast.8), calls=%async_computation.1 | async-start | bytes 3145728 | tf_op jit(solution)/shard_map/all_to_all | solution.py:118
  42.3 5.1 %collective-permute-start = (bf16[768,768]{1,0:T(8,128)(2,1)}, bf16[768,768]{1,0:T(8,128)(2,1)}, u32[]{:S(2)}, u32[]{:S(2)}) collective-permute-start(bf16[768,768]{1,0:T(8,128)(2,1)} %get-tuple-element.14), channel_id=1, source_target_pairs={{0,4},{4,0},{1,5},{5,1},{2,6},{6,2},{3,7},{7,3},{8,12},{12,8},{9,1... | collective-permute-start | bytes 3538952 | tf_op jit(solution)/shard_map/ppermute | solution.py:30
  87.7 8.1 %collective-permute-start.1 = (bf16[64,768]{1,0:T(8,128)(2,1)S(1)}, bf16[64,768]{1,0:T(8,128)(2,1)S(1)}, u32[]{:S(2)}, u32[]{:S(2)}) collective-permute-start(bf16[64,768]{1,0:T(8,128)(2,1)S(1)} %add_convert_fusion), channel_id=1, source_target_pairs={{4,64},{68,128},{132,192},{196,256},{260,320},{324,384},{388,448},... | collective-permute-start | bytes 294920 | tf_op jit(solution)/shard_map/ppermute | solution.py:131
  113.2 17.5 %collective-permute-start.2 = (bf16[512,768]{1,0:T(8,128)(2,1)S(1)}, bf16[512,768]{1,0:T(8,128)(2,1)S(1)}, u32[]{:S(2)}, u32[]{:S(2)}) collective-permute-start(bf16[512,768]{1,0:T(8,128)(2,1)S(1)} %bitcast.35), channel_id=1, source_target_pairs={{0,4},{4,0},{1,5},{5,1},{2,6},{6,2},{3,7},{7,3},{8,12},{12,8},{9,1... | collective-permute-start | bytes 2359304 | tf_op jit(solution)/shard_map/ppermute | solution.py:30

commit v8 on v7

--- a/solution.py
+++ b/solution.py
@@ -30,32 +30,28 @@
     return lax.ppermute(block, "core", [(0, 1), (1, 0)])
 
 
-def hidden_kernel(parts_ref, stored_ref, copies_ref):
-    ncol = parts_ref.shape[0]
-    sums = parts_ref[0].astype(jnp.float32)
-    for i in range(1, ncol):
-        sums += parts_ref[i].astype(jnp.float32)
+def hidden_kernel(*refs):
+    *part_refs, stored_ref, copies_ref = refs
+    sums = sum(part_ref[...].astype(jnp.float32) for part_ref in part_refs)
     active = gelu_value(sums[0]).astype(jnp.bfloat16)
     hidden_grad = (sums[1] * gelu_slope(stored_ref[...].astype(jnp.float32))).astype(jnp.bfloat16)
-    for i in range(ncol):
+    for i in range(copies_ref.shape[1]):
         copies_ref[0, i] = hidden_grad
         copies_ref[1, i] = active
 
 
 def hidden_copies(parts, stored, steps=2):
-    ncol, _, rows, width = parts.shape
+    _, rows, width = parts[0].shape
     tile = rows // steps
     return pl.pallas_call(
         hidden_kernel,
         grid=(steps,),
-        in_specs=[
-            pl.BlockSpec((ncol, 2, tile, width), lambda i: (0, 0, i, 0)),
-            pl.BlockSpec((tile, width), lambda i: (i, 0)),
-        ],
-        out_specs=pl.BlockSpec((2, ncol, tile, width), lambda i: (0, 0, i, 0)),
-        out_shape=jax.ShapeDtypeStruct((2, ncol, rows, width), jnp.bfloat16),
+        in_specs=[pl.BlockSpec((2, tile, width), lambda i: (0, i, 0))] * len(parts)
+        + [pl.BlockSpec((tile, width), lambda i: (i, 0))],
+        out_specs=pl.BlockSpec((2, len(parts), tile, width), lambda i: (0, 0, i, 0)),
+        out_shape=jax.ShapeDtypeStruct((2, len(parts), rows, width), jnp.bfloat16),
         compiler_params=pltpu.CompilerParams(vmem_limit_bytes=32 << 20),
-    )(parts, stored)
+    )(*parts, stored)
 
 
 def feature_kernel(core_ref, hidden_ref, own_ref, arrived_ref, out_ref):
@@ -101,19 +97,26 @@
     forward = core == 1
     count = inputs.shape[0]
 
-    def by_col(partial):
-        return partial.astype(jnp.bfloat16).reshape(ncol, count // ncol, -1)
-
-    partials = jnp.stack(
-        [by_col(product(inputs, w_up, 0)), by_col(product(upstream, w_down, 1))], axis=1
-    )
     piece = count // ny
     start = lax.axis_index("y") * piece
-    partials, core, forward, start = lax.optimization_barrier((partials, core, forward, start))
-    parts = lax.all_to_all(partials, "col", 0, 0, tiled=True)
+    partials = [
+        product(inputs, w_up, 0).astype(jnp.bfloat16),
+        product(upstream, w_down, 1).astype(jnp.bfloat16),
+    ]
+    col, rows = lax.axis_index("col"), count // ncol
+
+    def chunk_for(distance):
+        first = ((col + distance) % ncol) * rows
+        return jnp.stack([lax.dynamic_slice_in_dim(p, first, rows, 0) for p in partials])
+
+    parts = [chunk_for(0)]
+    for distance in sorted(range(1, ncol), key=lambda d: -min(d, ncol - d)):
+        route = [(i, (i + distance) % ncol) for i in range(ncol)]
+        parts.append(lax.ppermute(chunk_for(distance), "col", route))
+    copies = hidden_copies(parts, saved_hidden[0])
+    copies, w_up, w_down = lax.optimization_barrier((copies, w_up, w_down))
     own = jnp.where(forward, w_down, w_up)
     arrived = swapped(jnp.where(forward, w_up, w_down))
-    copies = hidden_copies(parts, saved_hidden[0])
     copies = copies.reshape((2 * ncol,) + copies.shape[2:])
     gathered = lax.all_to_all(copies, ("core", "col"), 0, 0, tiled=True)
     chip_sum = feature_terms(core, gathered.reshape(2, count, -1), own, arrived)

time: 132 us -> 131 us (level)
  blocking collectives: 59.5 us -> 43.3 us
  waiting for transfers between devices: 19 us -> 26.3 us
  starting transfers between devices: 40 us -> 47.2 us
    all_to_all x1 -> x0, blocking collectives: 17.3 us -> none  [body(): parts = lax.all_to_all(partials, 'col', 0, 0, tiled=True)]
    ppermute x0 -> x3, starting transfers between devices: none -> 12.1 us  [body(): parts.append(lax.ppermute(chunk_for(distance), 'col', route))]
    ppermute x0 -> x3, waiting for transfers between devices: none -> 7.07 us  [body(): parts.append(lax.ppermute(chunk_for(distance), 'col', route))]
    ppermute x1, starting transfers between devices: 5.8 us -> 3.46 us  [body(): moved = lax.ppermute(result, ('section', 'core'), route)]
    all_to_all x1, starting transfers between devices: 16.6 us -> 14.3 us  [body(): gathered = lax.all_to_all(copies, ('core', 'col'), 0, 0, tiled=True)]
  transfers between devices with their start and end apart: 4 -> 7, of which waited for: 4 -> 6; matrix products, arithmetic and copies ran while one was open for 3% -> 3% of each run, Pallas kernels for 0% -> 0%
where the time goes in v8:
time: 131 us
  starting transfers between devices  47.2 us (36%)
  blocking collectives  43.3 us (33%)
  waiting for transfers between devices  26.3 us (20%)
  other arithmetic  5.34 us (4%)
  Pallas kernels  4.16 us (3%)
  matrix products  3.23 us (2%)
    all_to_all x1, blocking collectives, body(): lax.all_to_all(chip_sum.reshape(ny, piece, -1), 'y', 0, 0, tiled=True)  26 us
    all_to_all x1, blocking collectives, body(): mine = lax.all_to_all(pieces, 'y', 0, 0, tiled=True).reshape(count, -1)  17.4 us
    ppermute x2, starting transfers between devices, swapped(): return lax.ppermute(block, 'core', [(0, 1), (1, 0)])  17.3 us
    all_to_all x1, starting transfers between devices, body(): gathered = lax.all_to_all(copies, ('core', 'col'), 0, 0, tiled=True)  14.3 us
    all_to_all x1, waiting for transfers between devices, body(): gathered = lax.all_to_all(copies, ('core', 'col'), 0, 0, tiled=True)  12.7 us
    ppermute x3, starting transfers between devices, body(): parts.append(lax.ppermute(chunk_for(distance), 'col', route))  12.1 us
    ppermute x3, waiting for transfers between devices, body(): parts.append(lax.ppermute(chunk_for(distance), 'col', route))  7.07 us
    ppermute x2, waiting for transfers between devices, swapped(): return lax.ppermute(block, 'core', [(0, 1), (1, 0)])  4.07 us
  transfers between devices with their start and end apart: 7, of which 6 were waited for; matrix products, arithmetic and copies ran while one was open for 3% of the time, Pallas kernels for 0%

profile of v8, /device:TPU:1, one launch (start us, length us, event | category | flops | bytes accessed | tf_op | source)
XLA Modules:
  0.0 130.7 jit_solution(7030667817582477322)
XLA Ops:
  0.7 2.5 %convolution_convert_fusion = bf16[512,768]{1,0:T(8,128)(2,1)S(1)} fusion(bf16[1,512,768]{2,1,0:T(8,128)(2,1)} %param.8, bf16[1,768,768]{2,1,0:T(8,128)(2,1)} %param.7), kind=kOutput, calls=%fused_computation.1 | convolution fusion | flops 604372992 | bytes 2752512 | tf_op jit(solution)/shard_map/dot_general | solution.py:24
  3.2 0.8 convolution_convert_fusion.1
  4.0 0.2 dynamic-slice_bitcast_fusion
  4.2 5.5 %collective-permute-start = (bf16[2,128,768]{2,1,0:T(8,128)(2,1)S(1)}, bf16[2,128,768]{2,1,0:T(8,128)(2,1)S(1)}, u32[]{:S(2)}, u32[]{:S(2)}) collective-permute-start(bf16[2,128,768]{2,1,0:T(8,128)(2,1)S(1)} %pad_maximum_fusion.1), channel_id=1, source_target_pairs={{0,2},{1,3},{2,0},{3,1},{4,6},{5,7},{6,4},{7,5},{8,10},{9,11},{10,... | collective-permute-start | bytes 1179656 | tf_op jit(solution)/shard_map/ppermute | solution.py:115
  9.8 2.4 %collective-permute-start.1 = (bf16[2,128,768]{2,1,0:T(8,128)(2,1)S(1)}, bf16[2,128,768]{2,1,0:T(8,128)(2,1)S(1)}, u32[]{:S(2)}, u32[]{:S(2)}) collective-permute-start(bf16[2,128,768]{2,1,0:T(8,128)(2,1)S(1)} %pad_maximum_fusion.2), channel_id=1, source_target_pairs={{0,1},{1,2},{2,3},{3,0},{4,5},{5,6},{6,7},{7,4},{8,9},{9,10},{10,1... | collective-permute-start | bytes 1179656 | tf_op jit(solution)/shard_map/ppermute | solution.py:115
  12.2 4.3 %collective-permute-start.2 = (bf16[2,128,768]{2,1,0:T(8,128)(2,1)S(1)}, bf16[2,128,768]{2,1,0:T(8,128)(2,1)S(1)}, u32[]{:S(2)}, u32[]{:S(2)}) collective-permute-start(bf16[2,128,768]{2,1,0:T(8,128)(2,1)S(1)} %pad_maximum_fusion.3), channel_id=1, source_target_pairs={{0,3},{1,0},{2,1},{3,2},{4,7},{5,4},{6,5},{7,6},{8,11},{9,8},{10,9... | collective-permute-start | bytes 1179656 | tf_op jit(solution)/shard_map/ppermute | solution.py:115
  16.5 3.1 %collective-permute-done.1.refs_2_ = bf16[2,128,768]{2,1,0:T(8,128)(2,1)S(1)} collective-permute-done((bf16[2,128,768]{2,1,0:T(8,128)(2,1)S(1)}, bf16[2,128,768]{2,1,0:T(8,128)(2,1)S(1)}, u32[]{:S(2)}, u32[]{:S(2)}) %collective-permute-start.1) | collective-permute-done | bytes 393248 | tf_op jit(solution)/shard_map/ppermute | solution.py:115
  19.6 4.0 %collective-permute-done.2.refs_3_ = bf16[2,128,768]{2,1,0:T(8,128)(2,1)S(1)} collective-permute-done((bf16[2,128,768]{2,1,0:T(8,128)(2,1)S(1)}, bf16[2,128,768]{2,1,0:T(8,128)(2,1)S(1)}, u32[]{:S(2)}, u32[]{:S(2)}) %collective-permute-start.2) | collective-permute-done | bytes 393248 | tf_op jit(solution)/shard_map/ppermute | solution.py:115
  23.6 1.5 %shard_map.68 = bf16[2,4,128,768]{3,2,1,0:T(8,128)(2,1)} custom-call(bf16[2,128,768]{2,1,0:T(8,128)(2,1)S(1)} %pad_maximum_fusion.refs_0_, bf16[2,128,768]{2,1,0:T(8,128)(2,1)S(1)} %collective-permute-done.refs_1_, bf16[2,128,768]{2,1,0:T(8,128)(2,1)S(1)} %collective-permute-done.1.refs_2_, bf16[2,128,768]{2,1,0:T(8,128)(2,1)S(1)} %collective-permute-done.2.refs_3_, ...), custom_call_target="tpu_custom_call" | custom-call | tf_op jit(solution)/shard_map/pallas_call | solution.py:46
  25.1 14.3 %all-to-all-start = ((bf16[8,128,768]{2,1,0:T(8,128)(2,1)}), bf16[8,128,768]{2,1,0:T(8,128)(2,1)S(1)}, u32[]{:S(2)}, u32[]{:S(2)}) async-start(bf16[8,128,768]{2,1,0:T(8,128)(2,1)} %bitcast.14), calls=%async_computation | async-start | bytes 3145728 | tf_op jit(solution)/shard_map/all_to_all | solution.py:121
  39.4 2.8 %broadcast_select_fusion = (bf16[768,768]{1,0:T(8,128)(2,1)}, bf16[768,768]{1,0:T(8,128)(2,1)S(1)}) fusion(bf16[768,768]{1,0:T(8,128)(2,1)} %bitcast.47, bf16[768,768]{1,0:T(8,128)(2,1)} %bitcast.46, pred[]{:T(512)S(6)} %eq.8), kind=kLoop, calls=%fused_computation.3 | loop fusion | flops 1179648 | bytes 4718593 | tf_op jit(solution)/shard_map/jit(_where)/select_n | solution.py:119
  42.2 1.9 %collective-permute-start.3 = (bf16[768,768]{1,0:T(8,128)(2,1)}, bf16[768,768]{1,0:T(8,128)(2,1)}, u32[]{:S(2)}, u32[]{:S(2)}) collective-permute-start(bf16[768,768]{1,0:T(8,128)(2,1)} %get-tuple-element.12), channel_id=1, source_target_pairs={{0,4},{4,0},{1,5},{5,1},{2,6},{6,2},{3,7},{7,3},{8,12},{12,8},{9,1... | collective-permute-start | bytes 3538952 | tf_op jit(solution)/shard_map/ppermute | solution.py:30
  44.1 1.0 select_bitcast_fusion.2
  45.0 2.2 %collective-permute-done.3.arrived_ref = bf16[768,768]{1,0:T(8,128)(2,1)} collective-permute-done((bf16[768,768]{1,0:T(8,128)(2,1)}, bf16[768,768]{1,0:T(8,128)(2,1)}, u32[]{:S(2)}, u32[]{:S(2)}) %collective-permute-start.3) | collective-permute-done | bytes 1179680 | tf_op jit(solution)/shard_map/ppermute | solution.py:30
  47.2 12.7 %all-to-all-done = bf16[8,128,768]{2,1,0:T(8,128)(2,1)S(1)} async-done(((bf16[8,128,768]{2,1,0:T(8,128)(2,1)}), bf16[8,128,768]{2,1,0:T(8,128)(2,1)S(1)}, u32[]{:S(2)}, u32[]{:S(2)}) %all-to-all-start) | async-done | bytes 1572896 | tf_op jit(solution)/shard_map/all_to_all | solution.py:121
  60.0 2.7 %shard_map.69 = bf16[512,768]{1,0:T(8,128)(2,1)S(1)} custom-call(s32[1]{0:T(128)} %bitcast.core_ref, bf16[2,512,768]{2,1,0:T(8,128)(2,1)S(1)} %bitcast.42, bf16[768,768]{1,0:T(8,128)(2,1)S(1)} %get-tuple-element.13.own_ref, bf16[768,768]{1,0:T(8,128)(2,1)} %collective-permute-done.3.arrived_ref), custom_call_target="tpu_custom_call" | custom-call | tf_op jit(solution)/shard_map/pallas_call | solution.py:76
  62.6 26.0 %all_to_all.15 = bf16[8,64,768]{2,1,0:T(8,128)(2,1)S(1)} all-to-all(bf16[8,64,768]{2,1,0:T(8,128)(2,1)S(1)} %bitcast.43), channel_id=1, replica_groups=mesh['section'=16,'y'=8,'core'=2,'col'=4] {'y'}, dimensions={0} | all-to-all | bytes 1572864 | tf_op jit(solution)/shard_map/all_to_all | solution.py:129
  88.6 0.1 convert_reduce_fusion
  88.7 3.5 %collective-permute-start.4 = (bf16[64,768]{1,0:T(8,128)(2,1)S(1)}, bf16[64,768]{1,0:T(8,128)(2,1)S(1)}, u32[]{:S(2)}, u32[]{:S(2)}) collective-permute-start(bf16[64,768]{1,0:T(8,128)(2,1)S(1)} %add_convert_fusion), channel_id=1, source_target_pairs={{4,64},{68,128},{132,192},{196,256},{260,320},{324,384},{388,448},... | collective-permute-start | bytes 294920 | tf_op jit(solution)/shard_map/ppermute | solution.py:134
  92.2 2.5 %collective-permute-done.4 = bf16[64,768]{1,0:T(8,128)(2,1)S(1)} collective-permute-done((bf16[64,768]{1,0:T(8,128)(2,1)S(1)}, bf16[64,768]{1,0:T(8,128)(2,1)S(1)}, u32[]{:S(2)}, u32[]{:S(2)}) %collective-permute-start.4) | collective-permute-done | bytes 98336 | tf_op jit(solution)/shard_map/ppermute | solution.py:134
  94.7 17.4 %all_to_all.16 = bf16[8,64,768]{2,1,0:T(8,128)(2,1)S(1)} all-to-all(bf16[8,64,768]{2,1,0:T(8,128)(2,1)S(1)} %broadcast_in_dim.12), channel_id=1, replica_groups=mesh['section'=16,'y'=8,'core'=2,'col'=4] {'y'}, dimensions={0} | all-to-all | bytes 1572864 | tf_op jit(solution)/shard_map/all_to_all | solution.py:136
  112.1 15.4 %collective-permute-start.5 = (bf16[512,768]{1,0:T(8,128)(2,1)S(1)}, bf16[512,768]{1,0:T(8,128)(2,1)S(1)}, u32[]{:S(2)}, u32[]{:S(2)}) collective-permute-start(bf16[512,768]{1,0:T(8,128)(2,1)S(1)} %bitcast.45), channel_id=1, source_target_pairs={{0,4},{4,0},{1,5},{5,1},{2,6},{6,2},{3,7},{7,3},{8,12},{12,8},{9,1... | collective-permute-start | bytes 2359304 | tf_op jit(solution)/shard_map/ppermute | solution.py:30
  127.5 1.9 %collective-permute-done.5 = bf16[512,768]{1,0:T(8,128)(2,1)S(1)} collective-permute-done((bf16[512,768]{1,0:T(8,128)(2,1)S(1)}, bf16[512,768]{1,0:T(8,128)(2,1)S(1)}, u32[]{:S(2)}, u32[]{:S(2)}) %collective-permute-start.5) | collective-permute-done | bytes 786464 | tf_op jit(solution)/shard_map/ppermute | solution.py:30
  129.4 1.3 select_bitcast_fusion
  (13 shorter events, 0.3 us)
Async XLA Ops:
  0.7 2.5 %copy-start.1 = (bf16[1,768,768]{2,1,0:T(8,128)(2,1)S(1)}, bf16[1,768,768]{2,1,0:T(8,128)(2,1)}, u32[]{:S(2)}) copy-start(bf16[1,768,768]{2,1,0:T(8,128)(2,1)} %param.6) | copy-start | bytes 3538948
  0.7 2.5 %copy-start.2 = (bf16[1,512,768]{2,1,0:T(8,128)(2,1)S(1)}, bf16[1,512,768]{2,1,0:T(8,128)(2,1)}, u32[]{:S(2)}) copy-start(bf16[1,512,768]{2,1,0:T(8,128)(2,1)} %param.5) | copy-start | bytes 2359300
  4.2 12.3 %collective-permute-start = (bf16[2,128,768]{2,1,0:T(8,128)(2,1)S(1)}, bf16[2,128,768]{2,1,0:T(8,128)(2,1)S(1)}, u32[]{:S(2)}, u32[]{:S(2)}) collective-permute-start(bf16[2,128,768]{2,1,0:T(8,128)(2,1)S(1)} %pad_maximum_fusion.1), channel_id=1, source_target_pairs={{0,2},{1,3},{2,0},{3,1},{4,6},{5,7},{6,4},{7,5},{8,10},{9,11},{10,... | collective-permute-start | bytes 1179656 | tf_op jit(solution)/shard_map/ppermute | solution.py:115
  9.7 13.9 %copy-start = (bf16[1,128,768]{2,1,0:T(8,128)(2,1)S(1)}, bf16[1,128,768]{2,1,0:T(8,128)(2,1)}, u32[]{:S(2)}) copy-start(bf16[1,128,768]{2,1,0:T(8,128)(2,1)} %param.9) | copy-start | bytes 589828
  9.8 9.9 %collective-permute-start.1 = (bf16[2,128,768]{2,1,0:T(8,128)(2,1)S(1)}, bf16[2,128,768]{2,1,0:T(8,128)(2,1)S(1)}, u32[]{:S(2)}, u32[]{:S(2)}) collective-permute-start(bf16[2,128,768]{2,1,0:T(8,128)(2,1)S(1)} %pad_maximum_fusion.2), channel_id=1, source_target_pairs={{0,1},{1,2},{2,3},{3,0},{4,5},{5,6},{6,7},{7,4},{8,9},{9,10},{10,1... | collective-permute-start | bytes 1179656 | tf_op jit(solution)/shard_map/ppermute | solution.py:115
  12.2 11.4 %collective-permute-start.2 = (bf16[2,128,768]{2,1,0:T(8,128)(2,1)S(1)}, bf16[2,128,768]{2,1,0:T(8,128)(2,1)S(1)}, u32[]{:S(2)}, u32[]{:S(2)}) collective-permute-start(bf16[2,128,768]{2,1,0:T(8,128)(2,1)S(1)} %pad_maximum_fusion.3), channel_id=1, source_target_pairs={{0,3},{1,0},{2,1},{3,2},{4,7},{5,4},{6,5},{7,6},{8,11},{9,8},{10,9... | collective-permute-start | bytes 1179656 | tf_op jit(solution)/shard_map/ppermute | solution.py:115
  25.1 34.9 %all-to-all-start = ((bf16[8,128,768]{2,1,0:T(8,128)(2,1)}), bf16[8,128,768]{2,1,0:T(8,128)(2,1)S(1)}, u32[]{:S(2)}, u32[]{:S(2)}) async-start(bf16[8,128,768]{2,1,0:T(8,128)(2,1)} %bitcast.14), calls=%async_computation | async-start | bytes 3145728 | tf_op jit(solution)/shard_map/all_to_all | solution.py:121
  42.2 5.1 %collective-permute-start.3 = (bf16[768,768]{1,0:T(8,128)(2,1)}, bf16[768,768]{1,0:T(8,128)(2,1)}, u32[]{:S(2)}, u32[]{:S(2)}) collective-permute-start(bf16[768,768]{1,0:T(8,128)(2,1)} %get-tuple-element.12), channel_id=1, source_target_pairs={{0,4},{4,0},{1,5},{5,1},{2,6},{6,2},{3,7},{7,3},{8,12},{12,8},{9,1... | collective-permute-start | bytes 3538952 | tf_op jit(solution)/shard_map/ppermute | solution.py:30
  88.7 5.9 %collective-permute-start.4 = (bf16[64,768]{1,0:T(8,128)(2,1)S(1)}, bf16[64,768]{1,0:T(8,128)(2,1)S(1)}, u32[]{:S(2)}, u32[]{:S(2)}) collective-permute-start(bf16[64,768]{1,0:T(8,128)(2,1)S(1)} %add_convert_fusion), channel_id=1, source_target_pairs={{4,64},{68,128},{132,192},{196,256},{260,320},{324,384},{388,448},... | collective-permute-start | bytes 294920 | tf_op jit(solution)/shard_map/ppermute | solution.py:134
  112.1 17.3 %collective-permute-start.5 = (bf16[512,768]{1,0:T(8,128)(2,1)S(1)}, bf16[512,768]{1,0:T(8,128)(2,1)S(1)}, u32[]{:S(2)}, u32[]{:S(2)}) collective-permute-start(bf16[512,768]{1,0:T(8,128)(2,1)S(1)} %bitcast.45), channel_id=1, source_target_pairs={{0,4},{4,0},{1,5},{5,1},{2,6},{6,2},{3,7},{7,3},{8,12},{12,8},{9,1... | collective-permute-start | bytes 2359304 | tf_op jit(solution)/shard_map/ppermute | solution.py:30

commit v9 on v8

--- a/solution.py
+++ b/solution.py
@@ -110,7 +110,7 @@
         return jnp.stack([lax.dynamic_slice_in_dim(p, first, rows, 0) for p in partials])
 
     parts = [chunk_for(0)]
-    for distance in sorted(range(1, ncol), key=lambda d: -min(d, ncol - d)):
+    for distance in sorted(range(1, ncol), key=lambda d: min(d, ncol - d)):
         route = [(i, (i + distance) % ncol) for i in range(ncol)]
         parts.append(lax.ppermute(chunk_for(distance), "col", route))
     copies = hidden_copies(parts, saved_hidden[0])

time: 131 us -> 133 us (1.015)
  waiting for transfers between devices: 26.3 us -> 28.8 us
    all_to_all x1, starting transfers between devices: 14.3 us -> 16.2 us  [body(): gathered = lax.all_to_all(copies, ('core', 'col'), 0, 0, tiled=True)]
    ppermute x3, waiting for transfers between devices: 7.07 us -> 8.89 us  [body(): parts.append(lax.ppermute(chunk_for(distance), 'col', route))]
where the time goes in v9:
time: 133 us; the launch traced here: 132 us
  starting transfers between devices  46.4 us (35%)
  blocking collectives  43.3 us (33%)
  waiting for transfers between devices  28.8 us (22%)
  other arithmetic  5.34 us (4%)
  Pallas kernels  4.16 us (3%)
  matrix products  3.23 us (2%)
    all_to_all x1, blocking collectives, body(): lax.all_to_all(chip_sum.reshape(ny, piece, -1), 'y', 0, 0, tiled=True)  26 us
    all_to_all x1, blocking collectives, body(): mine = lax.all_to_all(pieces, 'y', 0, 0, tiled=True).reshape(count, -1)  17.4 us
    ppermute x2, starting transfers between devices, swapped(): return lax.ppermute(block, 'core', [(0, 1), (1, 0)])  16.7 us
    all_to_all x1, starting transfers between devices, body(): gathered = lax.all_to_all(copies, ('core', 'col'), 0, 0, tiled=True)  16.2 us
    all_to_all x1, waiting for transfers between devices, body(): gathered = lax.all_to_all(copies, ('core', 'col'), 0, 0, tiled=True)  12.7 us
    ppermute x3, starting transfers between devices, body(): parts.append(lax.ppermute(chunk_for(distance), 'col', route))  10.9 us
    ppermute x3, waiting for transfers between devices, body(): parts.append(lax.ppermute(chunk_for(distance), 'col', route))  8.89 us
    ppermute x2, waiting for transfers between devices, swapped(): return lax.ppermute(block, 'core', [(0, 1), (1, 0)])  3.99 us
  transfers between devices with their start and end apart: 7, of which 6 were waited for; matrix products, arithmetic and copies ran while one was open for 3% of the time, Pallas kernels for 0%

profile of v9, /device:TPU:1, one launch (start us, length us, event | category | flops | bytes accessed | tf_op | source)
XLA Modules:
  0.0 132.5 jit_solution(4032569037937649882)
XLA Ops:
  0.7 2.5 %convolution_convert_fusion = bf16[512,768]{1,0:T(8,128)(2,1)S(1)} fusion(bf16[1,512,768]{2,1,0:T(8,128)(2,1)} %param.8, bf16[1,768,768]{2,1,0:T(8,128)(2,1)} %param.7), kind=kOutput, calls=%fused_computation.1 | convolution fusion | flops 604372992 | bytes 2752512 | tf_op jit(solution)/shard_map/dot_general | solution.py:24
  3.2 0.8 convolution_convert_fusion.1
  4.0 0.2 dynamic-slice_bitcast_fusion
  4.2 4.0 %collective-permute-start = (bf16[2,128,768]{2,1,0:T(8,128)(2,1)S(1)}, bf16[2,128,768]{2,1,0:T(8,128)(2,1)S(1)}, u32[]{:S(2)}, u32[]{:S(2)}) collective-permute-start(bf16[2,128,768]{2,1,0:T(8,128)(2,1)S(1)} %pad_maximum_fusion.1), channel_id=1, source_target_pairs={{0,1},{1,2},{2,3},{3,0},{4,5},{5,6},{6,7},{7,4},{8,9},{9,10},{10,1... | collective-permute-start | bytes 1179656 | tf_op jit(solution)/shard_map/ppermute | solution.py:115
  8.2 3.3 %collective-permute-start.1 = (bf16[2,128,768]{2,1,0:T(8,128)(2,1)S(1)}, bf16[2,128,768]{2,1,0:T(8,128)(2,1)S(1)}, u32[]{:S(2)}, u32[]{:S(2)}) collective-permute-start(bf16[2,128,768]{2,1,0:T(8,128)(2,1)S(1)} %pad_maximum_fusion.2), channel_id=1, source_target_pairs={{0,3},{1,0},{2,1},{3,2},{4,7},{5,4},{6,5},{7,6},{8,11},{9,8},{10,9... | collective-permute-start | bytes 1179656 | tf_op jit(solution)/shard_map/ppermute | solution.py:115
  11.6 3.6 %collective-permute-start.2 = (bf16[2,128,768]{2,1,0:T(8,128)(2,1)S(1)}, bf16[2,128,768]{2,1,0:T(8,128)(2,1)S(1)}, u32[]{:S(2)}, u32[]{:S(2)}) collective-permute-start(bf16[2,128,768]{2,1,0:T(8,128)(2,1)S(1)} %pad_maximum_fusion.3), channel_id=1, source_target_pairs={{0,2},{1,3},{2,0},{3,1},{4,6},{5,7},{6,4},{7,5},{8,10},{9,11},{10,... | collective-permute-start | bytes 1179656 | tf_op jit(solution)/shard_map/ppermute | solution.py:115
  15.3 1.6 %collective-permute-done.1.refs_2_ = bf16[2,128,768]{2,1,0:T(8,128)(2,1)S(1)} collective-permute-done((bf16[2,128,768]{2,1,0:T(8,128)(2,1)S(1)}, bf16[2,128,768]{2,1,0:T(8,128)(2,1)S(1)}, u32[]{:S(2)}, u32[]{:S(2)}) %collective-permute-start.1) | collective-permute-done | bytes 393248 | tf_op jit(solution)/shard_map/ppermute | solution.py:115
  16.9 7.3 %collective-permute-done.2.refs_3_ = bf16[2,128,768]{2,1,0:T(8,128)(2,1)S(1)} collective-permute-done((bf16[2,128,768]{2,1,0:T(8,128)(2,1)S(1)}, bf16[2,128,768]{2,1,0:T(8,128)(2,1)S(1)}, u32[]{:S(2)}, u32[]{:S(2)}) %collective-permute-start.2) | collective-permute-done | bytes 393248 | tf_op jit(solution)/shard_map/ppermute | solution.py:115
  24.2 1.5 %shard_map.68 = bf16[2,4,128,768]{3,2,1,0:T(8,128)(2,1)} custom-call(bf16[2,128,768]{2,1,0:T(8,128)(2,1)S(1)} %pad_maximum_fusion.refs_0_, bf16[2,128,768]{2,1,0:T(8,128)(2,1)S(1)} %collective-permute-done.refs_1_, bf16[2,128,768]{2,1,0:T(8,128)(2,1)S(1)} %collective-permute-done.1.refs_2_, bf16[2,128,768]{2,1,0:T(8,128)(2,1)S(1)} %collective-permute-done.2.refs_3_, ...), custom_call_target="tpu_custom_call" | custom-call | tf_op jit(solution)/shard_map/pallas_call | solution.py:46
  25.7 16.2 %all-to-all-start = ((bf16[8,128,768]{2,1,0:T(8,128)(2,1)}), bf16[8,128,768]{2,1,0:T(8,128)(2,1)S(1)}, u32[]{:S(2)}, u32[]{:S(2)}) async-start(bf16[8,128,768]{2,1,0:T(8,128)(2,1)} %bitcast.14), calls=%async_computation | async-start | bytes 3145728 | tf_op jit(solution)/shard_map/all_to_all | solution.py:121
  41.9 2.8 %broadcast_select_fusion = (bf16[768,768]{1,0:T(8,128)(2,1)}, bf16[768,768]{1,0:T(8,128)(2,1)S(1)}) fusion(bf16[768,768]{1,0:T(8,128)(2,1)} %bitcast.47, bf16[768,768]{1,0:T(8,128)(2,1)} %bitcast.46, pred[]{:T(512)S(6)} %eq.8), kind=kLoop, calls=%fused_computation.3 | loop fusion | flops 1179648 | bytes 4718593 | tf_op jit(solution)/shard_map/jit(_where)/select_n | solution.py:119
  44.7 2.0 %collective-permute-start.3 = (bf16[768,768]{1,0:T(8,128)(2,1)}, bf16[768,768]{1,0:T(8,128)(2,1)}, u32[]{:S(2)}, u32[]{:S(2)}) collective-permute-start(bf16[768,768]{1,0:T(8,128)(2,1)} %get-tuple-element.12), channel_id=1, source_target_pairs={{0,4},{4,0},{1,5},{5,1},{2,6},{6,2},{3,7},{7,3},{8,12},{12,8},{9,1... | collective-permute-start | bytes 3538952 | tf_op jit(solution)/shard_map/ppermute | solution.py:30
  46.7 1.0 select_bitcast_fusion.2
  47.6 2.1 %collective-permute-done.3.arrived_ref = bf16[768,768]{1,0:T(8,128)(2,1)} collective-permute-done((bf16[768,768]{1,0:T(8,128)(2,1)}, bf16[768,768]{1,0:T(8,128)(2,1)}, u32[]{:S(2)}, u32[]{:S(2)}) %collective-permute-start.3) | collective-permute-done | bytes 1179680 | tf_op jit(solution)/shard_map/ppermute | solution.py:30
  49.7 12.7 %all-to-all-done = bf16[8,128,768]{2,1,0:T(8,128)(2,1)S(1)} async-done(((bf16[8,128,768]{2,1,0:T(8,128)(2,1)}), bf16[8,128,768]{2,1,0:T(8,128)(2,1)S(1)}, u32[]{:S(2)}, u32[]{:S(2)}) %all-to-all-start) | async-done | bytes 1572896 | tf_op jit(solution)/shard_map/all_to_all | solution.py:121
  62.5 2.7 %shard_map.69 = bf16[512,768]{1,0:T(8,128)(2,1)S(1)} custom-call(s32[1]{0:T(128)} %bitcast.core_ref, bf16[2,512,768]{2,1,0:T(8,128)(2,1)S(1)} %bitcast.42, bf16[768,768]{1,0:T(8,128)(2,1)S(1)} %get-tuple-element.13.own_ref, bf16[768,768]{1,0:T(8,128)(2,1)} %collective-permute-done.3.arrived_ref), custom_call_target="tpu_custom_call" | custom-call | tf_op jit(solution)/shard_map/pallas_call | solution.py:76
  65.1 26.0 %all_to_all.15 = bf16[8,64,768]{2,1,0:T(8,128)(2,1)S(1)} all-to-all(bf16[8,64,768]{2,1,0:T(8,128)(2,1)S(1)} %bitcast.43), channel_id=1, replica_groups=mesh['section'=16,'y'=8,'core'=2,'col'=4] {'y'}, dimensions={0} | all-to-all | bytes 1572864 | tf_op jit(solution)/shard_map/all_to_all | solution.py:129
  91.1 0.1 convert_reduce_fusion
  91.2 2.7 %collective-permute-start.4 = (bf16[64,768]{1,0:T(8,128)(2,1)S(1)}, bf16[64,768]{1,0:T(8,128)(2,1)S(1)}, u32[]{:S(2)}, u32[]{:S(2)}) collective-permute-start(bf16[64,768]{1,0:T(8,128)(2,1)S(1)} %add_convert_fusion), channel_id=1, source_target_pairs={{4,64},{68,128},{132,192},{196,256},{260,320},{324,384},{388,448},... | collective-permute-start | bytes 294920 | tf_op jit(solution)/shard_map/ppermute | solution.py:134
  93.9 3.2 %collective-permute-done.4 = bf16[64,768]{1,0:T(8,128)(2,1)S(1)} collective-permute-done((bf16[64,768]{1,0:T(8,128)(2,1)S(1)}, bf16[64,768]{1,0:T(8,128)(2,1)S(1)}, u32[]{:S(2)}, u32[]{:S(2)}) %collective-permute-start.4) | collective-permute-done | bytes 98336 | tf_op jit(solution)/shard_map/ppermute | solution.py:134
  97.2 17.4 %all_to_all.16 = bf16[8,64,768]{2,1,0:T(8,128)(2,1)S(1)} all-to-all(bf16[8,64,768]{2,1,0:T(8,128)(2,1)S(1)} %broadcast_in_dim.12), channel_id=1, replica_groups=mesh['section'=16,'y'=8,'core'=2,'col'=4] {'y'}, dimensions={0} | all-to-all | bytes 1572864 | tf_op jit(solution)/shard_map/all_to_all | solution.py:136
  114.6 14.7 %collective-permute-start.5 = (bf16[512,768]{1,0:T(8,128)(2,1)S(1)}, bf16[512,768]{1,0:T(8,128)(2,1)S(1)}, u32[]{:S(2)}, u32[]{:S(2)}) collective-permute-start(bf16[512,768]{1,0:T(8,128)(2,1)S(1)} %bitcast.45), channel_id=1, source_target_pairs={{0,4},{4,0},{1,5},{5,1},{2,6},{6,2},{3,7},{7,3},{8,12},{12,8},{9,1... | collective-permute-start | bytes 2359304 | tf_op jit(solution)/shard_map/ppermute | solution.py:30
  129.3 1.9 %collective-permute-done.5 = bf16[512,768]{1,0:T(8,128)(2,1)S(1)} collective-permute-done((bf16[512,768]{1,0:T(8,128)(2,1)S(1)}, bf16[512,768]{1,0:T(8,128)(2,1)S(1)}, u32[]{:S(2)}, u32[]{:S(2)}) %collective-permute-start.5) | collective-permute-done | bytes 786464 | tf_op jit(solution)/shard_map/ppermute | solution.py:30
  131.2 1.3 select_bitcast_fusion
  (13 shorter events, 0.3 us)
Async XLA Ops:
  0.7 2.5 %copy-start.1 = (bf16[1,768,768]{2,1,0:T(8,128)(2,1)S(1)}, bf16[1,768,768]{2,1,0:T(8,128)(2,1)}, u32[]{:S(2)}) copy-start(bf16[1,768,768]{2,1,0:T(8,128)(2,1)} %param.6) | copy-start | bytes 3538948
  0.7 2.5 %copy-start.2 = (bf16[1,512,768]{2,1,0:T(8,128)(2,1)S(1)}, bf16[1,512,768]{2,1,0:T(8,128)(2,1)}, u32[]{:S(2)}) copy-start(bf16[1,512,768]{2,1,0:T(8,128)(2,1)} %param.5) | copy-start | bytes 2359300
  4.2 11.1 %collective-permute-start = (bf16[2,128,768]{2,1,0:T(8,128)(2,1)S(1)}, bf16[2,128,768]{2,1,0:T(8,128)(2,1)S(1)}, u32[]{:S(2)}, u32[]{:S(2)}) collective-permute-start(bf16[2,128,768]{2,1,0:T(8,128)(2,1)S(1)} %pad_maximum_fusion.1), channel_id=1, source_target_pairs={{0,1},{1,2},{2,3},{3,0},{4,5},{5,6},{6,7},{7,4},{8,9},{9,10},{10,1... | collective-permute-start | bytes 1179656 | tf_op jit(solution)/shard_map/ppermute | solution.py:115
  8.2 16.0 %copy-start = (bf16[1,128,768]{2,1,0:T(8,128)(2,1)S(1)}, bf16[1,128,768]{2,1,0:T(8,128)(2,1)}, u32[]{:S(2)}) copy-start(bf16[1,128,768]{2,1,0:T(8,128)(2,1)} %param.9) | copy-start | bytes 589828
  8.2 8.7 %collective-permute-start.1 = (bf16[2,128,768]{2,1,0:T(8,128)(2,1)S(1)}, bf16[2,128,768]{2,1,0:T(8,128)(2,1)S(1)}, u32[]{:S(2)}, u32[]{:S(2)}) collective-permute-start(bf16[2,128,768]{2,1,0:T(8,128)(2,1)S(1)} %pad_maximum_fusion.2), channel_id=1, source_target_pairs={{0,3},{1,0},{2,1},{3,2},{4,7},{5,4},{6,5},{7,6},{8,11},{9,8},{10,9... | collective-permute-start | bytes 1179656 | tf_op jit(solution)/shard_map/ppermute | solution.py:115
  11.6 12.6 %collective-permute-start.2 = (bf16[2,128,768]{2,1,0:T(8,128)(2,1)S(1)}, bf16[2,128,768]{2,1,0:T(8,128)(2,1)S(1)}, u32[]{:S(2)}, u32[]{:S(2)}) collective-permute-start(bf16[2,128,768]{2,1,0:T(8,128)(2,1)S(1)} %pad_maximum_fusion.3), channel_id=1, source_target_pairs={{0,2},{1,3},{2,0},{3,1},{4,6},{5,7},{6,4},{7,5},{8,10},{9,11},{10,... | collective-permute-start | bytes 1179656 | tf_op jit(solution)/shard_map/ppermute | solution.py:115
  25.7 36.8 %all-to-all-start = ((bf16[8,128,768]{2,1,0:T(8,128)(2,1)}), bf16[8,128,768]{2,1,0:T(8,128)(2,1)S(1)}, u32[]{:S(2)}, u32[]{:S(2)}) async-start(bf16[8,128,768]{2,1,0:T(8,128)(2,1)} %bitcast.14), calls=%async_computation | async-start | bytes 3145728 | tf_op jit(solution)/shard_map/all_to_all | solution.py:121
  44.7 5.1 %collective-permute-start.3 = (bf16[768,768]{1,0:T(8,128)(2,1)}, bf16[768,768]{1,0:T(8,128)(2,1)}, u32[]{:S(2)}, u32[]{:S(2)}) collective-permute-start(bf16[768,768]{1,0:T(8,128)(2,1)} %get-tuple-element.12), channel_id=1, source_target_pairs={{0,4},{4,0},{1,5},{5,1},{2,6},{6,2},{3,7},{7,3},{8,12},{12,8},{9,1... | collective-permute-start | bytes 3538952 | tf_op jit(solution)/shard_map/ppermute | solution.py:30
  91.2 5.9 %collective-permute-start.4 = (bf16[64,768]{1,0:T(8,128)(2,1)S(1)}, bf16[64,768]{1,0:T(8,128)(2,1)S(1)}, u32[]{:S(2)}, u32[]{:S(2)}) collective-permute-start(bf16[64,768]{1,0:T(8,128)(2,1)S(1)} %add_convert_fusion), channel_id=1, source_target_pairs={{4,64},{68,128},{132,192},{196,256},{260,320},{324,384},{388,448},... | collective-permute-start | bytes 294920 | tf_op jit(solution)/shard_map/ppermute | solution.py:134
  114.6 16.6 %collective-permute-start.5 = (bf16[512,768]{1,0:T(8,128)(2,1)S(1)}, bf16[512,768]{1,0:T(8,128)(2,1)S(1)}, u32[]{:S(2)}, u32[]{:S(2)}) collective-permute-start(bf16[512,768]{1,0:T(8,128)(2,1)S(1)} %bitcast.45), channel_id=1, source_target_pairs={{0,4},{4,0},{1,5},{5,1},{2,6},{6,2},{3,7},{7,3},{8,12},{12,8},{9,1... | collective-permute-start | bytes 2359304 | tf_op jit(solution)/shard_map/ppermute | solution.py:30
